TPU v7x, 512 devices: a whole 4x8x8 slice. The times are simulated.
512 devices in a mesh: tm: 64 (over y_hi, z, x), space: 8 (over y_lo, core).
Axes of the slice: x: 4, y: 8 (y_hi: 2, y_lo: 4; y = y_hi * 4 + y_lo), z: 8, core: 2. Of those that a mesh axis runs over, the one named last changes fastest.
Arguments:
- guess: float32 [256, 12, 48, 512], P('tm', None, 'space'), may hold values from -6 to 6
- forcing: float32 [12, 48, 512], P(None, 'space'), may hold values from -6 to 6
- coarse_gain: float32 [12, 48, 512], P(None, 'space'), may hold values from 0.9 to 1
- kernel_levels: float32 [8], replicated, may hold values from 0.002 to 0.03
- kernel_code: int32 [12, 12], replicated, may hold values from 0 to 7
- settle_levels: float32 [4], replicated, may hold values from 0.02 to 0.15
- settle_class: int32 [12], replicated, may hold values from 0 to 3
Outputs:
- updated: float32 [256, 12, 48, 512], P('tm', None, 'space')
- correction: float32 [64, 12, 48, 512], P('tm', None, 'space')
All inputs are finite; a program needn't handle non-finite values.
Results may differ from a plain program's by a relative error of at most 0.0001.
Values sent between devices are 32-bit elements; how exact they have to be, the bound alone decides.
No kernel may reach another device: no remote copies, remote signals or barrier semaphores. Data moves between devices by JAX's collectives and lax.ppermute only.
A program may use at most 64 MiB of HBM per device.

v0:
```python
import jax
import jax.numpy as jnp
from jax import lax
from jax.sharding import PartitionSpec as P

NY = 16
NZ = 32


def with_halo(value, sides, width):
    for axis, dim in sides:
        devices, length = (lax.axis_size(axis), value.shape[dim])
        up = [(i, (i + 1) % devices) for i in range(devices - 1)]
        down = [(j, i) for i, j in up]
        last = lax.slice_in_dim(value, length - width, length, axis=dim)
        first = lax.slice_in_dim(value, 0, width, axis=dim)
        before = lax.ppermute(last, axis, up)
        after = lax.ppermute(first, axis, down)
        value = jnp.concatenate([before, value, after], axis=dim)
    return value


def shifted(value, axis, by):
    devices = lax.axis_size(axis)
    pairs = [(i, i + by) for i in range(devices) if 0 <= i + by < devices]
    return lax.ppermute(value, axis, pairs)


def entering(value, axis, join, neutral):
    count, mine = (lax.axis_size(axis), lax.axis_index(axis))
    pieces = jax.tree.map(lambda part: lax.all_gather(part, axis), value)
    running = jax.tree.map(
        lambda part, zero: jnp.full_like(part, 0) + jnp.asarray(zero, part.dtype), value, neutral
    )

    def hop(position, running):
        longer = join(running, jax.tree.map(lambda part: part[position], pieces))
        return jax.tree.map(lambda new, old: jnp.where(position < mine, new, old), longer, running)

    return lax.fori_loop(0, count - 1, hop, running)


def operators(kernel_levels, kernel_code, settle_levels, settle_class):
    level_ids = jnp.arange(kernel_levels.shape[0], dtype=jnp.int32)
    kernel = jnp.sum(jnp.where(kernel_code[:, :, None] == level_ids, kernel_levels, 0.0), axis=-1)
    kmat = kernel - jnp.diag(jnp.sum(kernel, axis=0))
    speed_ids = jnp.arange(settle_levels.shape[0], dtype=jnp.int32)
    speed = jnp.sum(jnp.where(settle_class[:, None] == speed_ids, settle_levels, 0.0), axis=-1)
    return (kmat, speed)


def step_core(padded, forcing, kmat, speed):
    state = padded[:, 1:-1, :]
    width = state.shape[-1]
    place = jnp.arange(width, dtype=jnp.int32)
    zpos = place % NZ
    ypos = place // NZ
    xsum = padded[:, 2:, :] + padded[:, :-2, :]
    upper = jnp.where(zpos < NZ - 1, jnp.roll(state, -1, axis=-1), 0.0)
    lower = jnp.where(zpos > 0, jnp.roll(state, 1, axis=-1), 0.0)
    ahead = jnp.where(ypos < NY - 1, jnp.roll(state, -NZ, axis=-1), 0.0)
    behind = jnp.where(ypos > 0, jnp.roll(state, NZ, axis=-1), 0.0)
    laplace = xsum + upper + lower + ahead + behind - 6.0 * state
    classes = state.shape[0]
    mixing = jnp.dot(kmat, state.reshape(classes, -1), precision=lax.Precision.HIGHEST).reshape(
        state.shape
    )
    return state + 0.08 * laplace + speed[:, None, None] * (upper - state) + mixing + 0.1 * forcing


def fine_step(state, forcing, kmat, speed):
    padded = with_halo(state, (("space", 1),), 1)
    return step_core(padded, forcing, kmat, speed)


def shards(guess, forcing, coarse_gain, kernel_levels, kernel_code, settle_levels, settle_class):
    kmat, speed = operators(kernel_levels, kernel_code, settle_levels, settle_class)
    slices = guess.shape[0]
    states = [guess[j] for j in range(slices)]
    group = lax.axis_index("tm")

    def relax(states):
        for j in range(1, slices):
            states[j] = fine_step(states[j - 1], forcing, kmat, speed)
        return states

    states = relax(states)
    incoming = shifted(states[slices - 1], "tm", 1)
    states[0] = jnp.where(group > 0, fine_step(incoming, forcing, kmat, speed), states[0])
    states = relax(states)
    advanced = fine_step(states[slices - 1], forcing, kmat, speed)
    element = jnp.where(group > 0, advanced - coarse_gain * states[0], advanced)

    def compose(earlier, later):
        return (earlier[0] + later[0], jnp.power(coarse_gain, later[0]) * earlier[1] + later[1])

    ident = (jnp.zeros((), jnp.float32), jnp.zeros_like(element))
    count, before = entering((jnp.ones((), jnp.float32), element), "tm", compose, ident)
    correction = jnp.where(group > 0, before - states[0], 0.0)
    states[0] = states[0] + correction
    states = relax(states)
    return (jnp.stack(states, axis=0), correction[None])


def solution(mesh):
    in_specs = (
        P("tm", None, "space", None),
        P(None, "space", None),
        P(None, "space", None),
        P(),
        P(),
        P(),
        P(),
    )
    out_specs = (P("tm", None, "space", None), P("tm", None, "space", None))
    return jax.shard_map(shards, mesh=mesh, in_specs=in_specs, out_specs=out_specs, check_vma=False)
```

profile of v0, /device:TPU:56, one launch (start us, length us, event | category | flops | bytes accessed | tf_op | source)
XLA Modules:
  0.0 524.8 jit_solution(11309118523702390447)
XLA Ops:
  8.8 2.7 collective-permute-start
  11.5 1.9 collective-permute-start.1
  18.5 2.6 collective-permute-start.2
  21.1 1.9 collective-permute-start.3
  23.4 2.9 collective-permute-done.3
  28.1 1.9 collective-permute-start.4
  30.0 2.4 collective-permute-start.5
  32.8 2.4 collective-permute-done.5
  35.7 3.4 collective-permute-start.6
  39.2 14.8 %collective-permute-done.6 = f32[12,6,512]{2,0,1:T(8,128)S(1)} collective-permute-done((f32[12,6,512]{2,0,1:T(8,128)S(1)}, f32[12,6,512]{2,0,1:T(8,128)S(1)}, u32[]{:S(2)}, u32[]{:S(2)}) %collective-permute-start.6) | collective-permute-done | bytes 147488 | tf_op jit(solution)/shard_map/ppermute | solution.py:26
  54.0 5.0 collective-permute-start.7
  59.0 1.9 collective-permute-start.8
  61.6 2.5 collective-permute-done.8
  65.1 1.9 collective-permute-start.10
  67.0 3.6 collective-permute-start.9
  73.1 3.6 collective-permute-start.11
  76.7 1.9 collective-permute-start.12
  79.1 2.9 collective-permute-done.12
  82.8 1.9 collective-permute-start.13
  84.7 2.4 collective-permute-start.14
  87.6 2.4 collective-permute-done.14
  90.8 1.9 collective-permute-start.15
  92.7 2.4 collective-permute-start.16
  95.6 2.4 collective-permute-done.16
  101.3 228.8 %all-reduce = f32[64]{0:T(128)S(1)} all-reduce(f32[64]{0:T(128)S(1)} %dynamic-update-slice), channel_id=1, replica_groups=mesh['tm'=64,'space'=8] {'tm'}, use_global_device_ids=true, to_apply=%add | all-reduce | flops 64 | bytes 512
  330.1 152.3 %while.14 = (s32[]{:T(128)}, f32[12,6,512]{2,1,0:T(8,128)S(1)}, s32[]{:T(128)}, f32[64]{0:T(128)S(1)}, f32[12,6,512]{2,1,0:T(8,128)S(1)}, /*index=5*/f32[64,12,6,512]{3,2,1,0:T(8,128)}, s32[]{:T(128)}, s32[]{:T(128)}) while((s32[]{:T(128)}, f32[12,6,512]{2,1,0:T(8,128)S(1)}, s32[]{:T(128)}, f32[64]{0:T(128)S(1)}, ...), condition=%wide.region_4.5_spmd.clone, body=%wide.region_3.4_spmd.clone.sunk | while | flops 147460 | bytes 589949 | solution.py:40
  330.7 1.8 fusion.209
  333.2 1.8 fusion.209
  335.6 1.8 fusion.209
  338.0 1.8 fusion.209
  340.4 1.8 fusion.209
  342.8 1.8 fusion.209
  345.2 1.8 fusion.209
  347.7 1.8 fusion.209
  350.1 1.8 fusion.209
  354.9 1.8 fusion.209
  357.3 1.8 fusion.209
  359.8 1.8 fusion.209
  362.2 1.8 fusion.209
  364.6 1.8 fusion.209
  482.9 1.9 collective-permute-start.17
  484.8 2.6 collective-permute-start.18
  490.9 1.9 collective-permute-start.19
  492.8 2.4 collective-permute-start.20
  495.6 2.4 collective-permute-done.20
  498.9 1.9 collective-permute-start.21
  500.8 2.4 collective-permute-start.22
  503.7 12.5 %collective-permute-done.22 = f32[12,1,512]{2,0,1:T(8,128)S(1)} collective-permute-done((f32[12,1,512]{2,0,1:T(8,128)S(1)}, f32[12,1,512]{2,0,1:T(8,128)S(1)}, u32[]{:S(2)}, u32[]{:S(2)}) %collective-permute-start.22) | collective-permute-done | bytes 24608 | tf_op jit(solution)/shard_map/ppermute | solution.py:17
  (257 shorter events, 152.6 us)
Async XLA Ops:
  7.2 28.1 %copy-start.1 = (f32[12,6,512]{2,1,0:T(8,128)S(1)}, f32[12,6,512]{2,1,0:T(8,128)}, u32[]{:S(2)}) copy-start(f32[12,6,512]{2,1,0:T(8,128)} %param.10) | copy-start | bytes 442372
  7.2 323.0 %all-gather.3.cloned.1.call-start = ((), (), s32[]{:S(2)}) async-start(), calls=%async_computation | async-start | bytes 12779520 | tf_op jit(solution)/shard_map/all_gather | solution.py:31
  8.8 6.9 %collective-permute-start = (f32[12,1,512]{2,0,1:T(8,128)S(1)}, f32[12,1,512]{2,0,1:T(8,128)S(1)}, u32[]{:S(2)}, u32[]{:S(2)}) collective-permute-start(f32[12,1,512]{2,0,1:T(8,128)S(1)} %get-tuple-element.291), channel_id=1, source_target_pairs={{1,0},{2,1},{3,2},{4,3},{5,4},{6,5},{7,6},{9,8},{10,9},{11,10},{12... | collective-permute-start | bytes 73736 | tf_op jit(solution)/shard_map/ppermute | solution.py:18
  11.5 5.2 collective-permute-start.1
  18.5 5.0 collective-permute-start.2
  21.1 5.2 collective-permute-start.3
  28.1 4.8 collective-permute-start.4
  30.0 5.2 collective-permute-start.5
  35.7 18.3 %collective-permute-start.6 = (f32[12,6,512]{2,0,1:T(8,128)S(1)}, f32[12,6,512]{2,0,1:T(8,128)S(1)}, u32[]{:S(2)}, u32[]{:S(2)}) collective-permute-start(f32[12,6,512]{2,0,1:T(8,128)S(1)} %fusion.9), channel_id=1, source_target_pairs={{0,8},{8,16},{16,24},{24,32},{32,40},{40,48},{48,56},{56,64},{64,7... | collective-permute-start | bytes 442376 | tf_op jit(solution)/shard_map/ppermute | solution.py:26
  54.0 7.6 %collective-permute-start.7 = (f32[12,1,512]{2,0,1:T(8,128)S(1)}, f32[12,1,512]{2,0,1:T(8,128)S(1)}, u32[]{:S(2)}, u32[]{:S(2)}) collective-permute-start(f32[12,1,512]{2,0,1:T(8,128)S(1)} %get-tuple-element.261), channel_id=1, source_target_pairs={{1,0},{2,1},{3,2},{4,3},{5,4},{6,5},{7,6},{9,8},{10,9},{11,10},{12... | collective-permute-start | bytes 73736 | tf_op jit(solution)/shard_map/ppermute | solution.py:18
  59.0 5.2 collective-permute-start.8
  61.3 36.7 %copy-start = (f32[12,6,512]{2,1,0:T(8,128)S(1)}, f32[12,6,512]{2,1,0:T(8,128)}, u32[]{:S(2)}) copy-start(f32[12,6,512]{2,1,0:T(8,128)} %param.11) | copy-start | bytes 442372
  65.1 6.0 %collective-permute-start.10 = (f32[12,1,512]{2,0,1:T(8,128)S(1)}, f32[12,1,512]{2,0,1:T(8,128)S(1)}, u32[]{:S(2)}, u32[]{:S(2)}) collective-permute-start(f32[12,1,512]{2,0,1:T(8,128)S(1)} %get-tuple-element.252), channel_id=1, source_target_pairs={{0,1},{1,2},{2,3},{3,4},{4,5},{5,6},{6,7},{8,9},{9,10},{10,11},{11... | collective-permute-start | bytes 73736 | tf_op jit(solution)/shard_map/ppermute | solution.py:17
  67.0 5.2 collective-permute-start.9
  73.1 6.0 %collective-permute-start.11 = (f32[12,1,512]{2,0,1:T(8,128)S(1)}, f32[12,1,512]{2,0,1:T(8,128)S(1)}, u32[]{:S(2)}, u32[]{:S(2)}) collective-permute-start(f32[12,1,512]{2,0,1:T(8,128)S(1)} %get-tuple-element.241), channel_id=1, source_target_pairs={{1,0},{2,1},{3,2},{4,3},{5,4},{6,5},{7,6},{9,8},{10,9},{11,10},{12... | collective-permute-start | bytes 73736 | tf_op jit(solution)/shard_map/ppermute | solution.py:18
  76.7 5.2 collective-permute-start.12
  82.8 4.8 collective-permute-start.13
  84.7 5.2 collective-permute-start.14
  90.8 4.8 collective-permute-start.15
  92.7 5.2 collective-permute-start.16
  482.9 5.7 %collective-permute-start.17 = (f32[12,1,512]{2,0,1:T(8,128)S(1)}, f32[12,1,512]{2,0,1:T(8,128)S(1)}, u32[]{:S(2)}, u32[]{:S(2)}) collective-permute-start(f32[12,1,512]{2,0,1:T(8,128)S(1)} %get-tuple-element.211), channel_id=1, source_target_pairs={{1,0},{2,1},{3,2},{4,3},{5,4},{6,5},{7,6},{9,8},{10,9},{11,10},{12... | collective-permute-start | bytes 73736 | tf_op jit(solution)/shard_map/ppermute | solution.py:18
  484.8 5.2 collective-permute-start.18
  490.9 4.8 collective-permute-start.19
  492.8 5.2 collective-permute-start.20
  498.9 4.8 collective-permute-start.21
  500.8 15.4 %collective-permute-start.22 = (f32[12,1,512]{2,0,1:T(8,128)S(1)}, f32[12,1,512]{2,0,1:T(8,128)S(1)}, u32[]{:S(2)}, u32[]{:S(2)}) collective-permute-start(f32[12,1,512]{2,0,1:T(8,128)S(1)} %get-tuple-element.192), channel_id=1, source_target_pairs={{0,1},{1,2},{2,3},{3,4},{4,5},{5,6},{6,7},{8,9},{9,10},{10,11},{11... | collective-permute-start | bytes 73736 | tf_op jit(solution)/shard_map/ppermute | solution.py:17
Sparse Core Ops, SparseCore 0:
  99.5 214.2 all-gather.2
where the time goes:
time: 528 us; the launch traced here: 525 us
  blocking collectives  229 us (43%)
  other arithmetic  116 us (22%)
  starting transfers between devices  56.6 us (11%)
  local copies, waits for them, and re-layouts  50.9 us (10%)
  waiting for transfers between devices  48.9 us (9%)
  between operations  15 us (3%)
  matrix products  7.47 us (1%)
    unnamed x1, blocking collectives  229 us
    select_n x63, other arithmetic, hop(): jnp.where(position < mine, new, old)  114 us
    dynamic_slice x63, local copies, waits for them, and re-layouts, hop(): longer = join(running, jax.tree.map(lambda part: part[position], pieces))  36.9 us
    ppermute x11, waiting for transfers between devices, with_halo(): before = lax.ppermute(last, axis, up)  32.9 us
    ppermute x11, starting transfers between devices, with_halo(): after = lax.ppermute(first, axis, down)  29 us
    ppermute x11, starting transfers between devices, with_halo(): before = lax.ppermute(last, axis, up)  24.2 us
    ppermute x1, waiting for transfers between devices, shifted(): return lax.ppermute(value, axis, pairs)  14.8 us
  transfers between devices with their start and end apart: 24, of which 12 were waited for; matrix products, arithmetic and copies ran while one was open for 2% of the time, Pallas kernels for 0%

commit v1 on v0

v1 whole, which is shorter than its diff:
```python
import functools

import jax
import jax.numpy as jnp
from jax import lax
from jax.experimental import pallas as pl
from jax.experimental.pallas import tpu as pltpu
from jax.sharding import PartitionSpec as P

F32 = jnp.float32
C = 12
NY = 16
NZ = 32
PLANES = 6
NX = 48
SLICES = 4
ROWS = 4
OWN = PLANES * ROWS
HALO = 4 * ROWS
WIN = 64
BASE = 5 * ROWS
PIECE = 5
VMEM = pl.BlockSpec(memory_space=pltpu.VMEM)
SMEM = pl.BlockSpec(memory_space=pltpu.SMEM)
PARAMS = pltpu.CompilerParams(vmem_limit_bytes=32 * 1024 * 1024)


def arr(*shape):
    return jax.ShapeDtypeStruct(shape, F32)


def even_place():
    return lax.axis_index("space") % 2 == 0


def put_sends(first, last, near, far):
    even = even_place()

    @pl.when(even)
    def _():
        near[...] = last()
        far[...] = first()

    @pl.when(jnp.logical_not(even))
    def _():
        near[...] = first()
        far[...] = last()


def put_halo(buf, near, far):
    even = even_place()

    @pl.when(even)
    def _():
        buf[:, 4:BASE, :] = far()
        buf[:, BASE + OWN : 60, :] = near()

    @pl.when(jnp.logical_not(even))
    def _():
        buf[:, 4:BASE, :] = near()
        buf[:, BASE + OWN : 60, :] = far()


def prep_kernel(guess, forcing, gain, levels, code, settle, klass, own, near, far, gain_out, kmat, speed):
    for j in range(C):
        total = None
        col = []
        for i in range(C):
            v = levels[code[i, j]]
            col.append(v)
            total = v if total is None else total + v
        for i in range(C):
            if i == j:
                w = settle[klass[i]]
                speed[i] = w
                kmat[i, j] = (col[i] - total) + (1.0 - 0.48) - w
            else:
                kmat[i, j] = col[i]
    for c in range(C):
        own[c] = guess[pl.ds(c * OWN * SLICES, OWN, stride=SLICES), :]
        for r in range(ROWS):
            lanes = pl.ds(128 * r, 128)
            own[C + c, pl.ds(r, PLANES, stride=ROWS), :] = forcing[c, :, lanes] * 0.1
            gain_out[pl.ds(c * OWN + r, PLANES, stride=ROWS), :] = gain[c, :, lanes]
    gain_out[C * OWN :, :] = jnp.zeros((64 * PIECE - C * OWN, 128), F32)
    put_sends(lambda: own[:, :HALO, :], lambda: own[:, OWN - HALO :, :], near, far)


def coefficients(kmat, speed, kv, wup, wfix, mask):
    lane = lax.broadcasted_iota(jnp.int32, (8, 128), 1)
    row = lax.broadcasted_iota(jnp.int32, (8, 128), 0)
    z = lane % NZ
    edge_row = row % ROWS
    for i in range(C):
        for j in range(C):
            kv[i * C + j] = jnp.full((8, 128), kmat[i, j], F32)
        wup[i] = jnp.where(z < NZ - 1, 0.08 + speed[i], 0.0)
    wfix[0] = jnp.where(z > 0, F32(0.08), F32(0.0))
    wfix[1] = jnp.where(jnp.logical_and(lane >= 96, edge_row == ROWS - 1), F32(0.0), F32(0.08))
    wfix[2] = jnp.where(jnp.logical_and(lane < 32, edge_row == 0), F32(0.0), F32(0.08))
    start = lax.axis_index("space") * PLANES - 5
    for t in range(WIN // 8):
        plane = start + 2 * t + row // ROWS
        inside = jnp.logical_and(plane >= 0, plane < NX)
        mask[t] = jnp.where(inside, F32(1.0), F32(0.0))


def clear_edges(buf):
    z = jnp.zeros((C, 8, 128), F32)
    buf[:, 0:8, :] = z
    buf[:, WIN - 8 : WIN, :] = z


def block_step(src, dst, fwin, t, kv, wup, wfix, mask):
    lane = lax.broadcasted_iota(jnp.int32, (8, 128), 1)
    row = lax.broadcasted_iota(jnp.int32, (8, 128), 0)
    low = row < ROWS
    right = lane >= 96
    left = lane < 32
    wdn, wah, wbe = wfix[0], wfix[1], wfix[2]

    def rows(k):
        return pl.ds(pl.multiple_of((t + k) * 8, 8), 8)

    acc = []
    for i in range(C):
        p = [src[i, rows(k), :] for k in (-1, 0, 1, 2)]
        q = [pltpu.roll(v, 4, 0) for v in p]
        pair = []
        for k in (0, 1):
            c = p[k + 1]
            xs = q[k + 1] + jnp.where(low, q[k], q[k + 2])
            up = pltpu.roll(c, 127, 1)
            dn = pltpu.roll(c, 1, 1)
            ra = pltpu.roll(c, 96, 1)
            rb = pltpu.roll(c, 32, 1)
            ah = jnp.where(right, pltpu.roll(ra, 7, 0), ra)
            be = jnp.where(left, pltpu.roll(rb, 1, 0), rb)
            new = fwin[i, rows(k), :] + 0.08 * xs
            new = new + wup[i] * up
            new = new + wdn * dn
            new = new + wah * ah
            new = new + wbe * be
            pair.append(new)
        acc.append(pair)
    for j in range(C):
        c = [src[j, rows(k), :] for k in (0, 1)]
        for i in range(C):
            w = kv[i * C + j]
            acc[i] = [acc[i][k] + w * c[k] for k in (0, 1)]
    for k in (0, 1):
        m = mask[t + k]
        for i in range(C):
            dst[i, rows(k), :] = acc[i][k] * m


def steps(bufs, fwin, plan, coefs):
    for s, (first, count) in enumerate(plan):
        src, dst = bufs[s % 2], bufs[(s + 1) % 2]

        @pl.loop(0, count)
        def _(b):
            block_step(src, dst, fwin, first + 2 * b, *coefs)


FOUR = ((1, 3), (1, 3), (2, 2), (2, 2))


def first_kernel(own, near, far, kmat, speed, state, send_near, send_far, fwin, a, b, kv, wup, wfix, mask):
    coefs = (kv, wup, wfix, mask)
    coefficients(kmat, speed, *coefs)
    clear_edges(a)
    clear_edges(b)
    clear_edges(fwin)
    a[:, BASE : BASE + OWN, :] = own[:C]
    fwin[:, BASE : BASE + OWN, :] = own[C:]
    put_halo(a, lambda: near[:C], lambda: far[:C])
    put_halo(fwin, lambda: near[C:], lambda: far[C:])
    steps((a, b), fwin, FOUR, coefs)
    state[...] = a[:, BASE : BASE + OWN, :]
    put_sends(lambda: state[:, :HALO, :], lambda: state[:, OWN - HALO :, :], send_near, send_far)


def second_kernel(state, near, far, fwin, gain, kmat, speed, out, a, b, kv, wup, wfix, mask):
    coefs = (kv, wup, wfix, mask)
    coefficients(kmat, speed, *coefs)
    clear_edges(a)
    clear_edges(b)
    a[:, BASE : BASE + OWN, :] = state[...]
    put_halo(a, lambda: near[...], lambda: far[...])
    steps((a, b), fwin, FOUR, coefs)
    use = jnp.where(lax.axis_index("tm") > 0, F32(1.0), F32(0.0))
    for c in range(C):
        here = pl.ds(c * OWN, OWN)
        out[here, :] = a[c, BASE : BASE + OWN, :] - use * (gain[here, :] * state[c])
    out[C * OWN :, :] = jnp.zeros((64 * PIECE - C * OWN, 128), F32)


def scan_kernel(pieces, gain, out):
    count = pieces.shape[0] // PIECE
    mine = gain[0]
    running = pieces[0:PIECE, :]
    out[0 : 2 * PIECE, :] = jnp.zeros((2 * PIECE, 128), F32)
    for k in range(2, count):
        out[k * PIECE : (k + 1) * PIECE, :] = running
        if k + 1 < count:
            m = k - 1
            running = mine * running + pieces[m * PIECE : (m + 1) * PIECE, :]


def gather_kernel(pieces, shifted, own, state, near, far, corr):
    k = lax.axis_index("tm")

    @pl.when(k == 0)
    def _():
        state[...] = own[:C]

    @pl.when(k == 1)
    def _():
        state[...] = shifted[...]

    @pl.when(k >= 2)
    def _():
        for c in range(C):
            state[c] = pieces[c * OWN : (c + 1) * OWN, :]

    put_sends(lambda: state[:, :HALO, :], lambda: state[:, OWN - HALO :, :], near, far)

    @pl.when(k < 2)
    def _():
        corr[...] = jnp.zeros_like(corr)

    @pl.when(k >= 2)
    def _():
        for c in range(C):
            corr[c * OWN : (c + 1) * OWN, :] = state[c] - shifted[c]


def last_kernel(state, near, far, fwin, kmat, speed, out, a, b, kv, wup, wfix, mask):
    coefs = (kv, wup, wfix, mask)
    coefficients(kmat, speed, *coefs)
    clear_edges(a)
    clear_edges(b)
    a[:, BASE : BASE + OWN, :] = state[...]
    put_halo(a, lambda: near[...], lambda: far[...])

    def emit(buf, j):
        for c in range(C):
            out[pl.ds(c * OWN * SLICES + j, OWN, stride=SLICES), :] = buf[c, BASE : BASE + OWN, :]

    emit(a, 0)
    bufs = (a, b)
    for j, one in enumerate(((1, 3), (2, 2), (2, 2))):
        src, dst = bufs[j % 2], bufs[(j + 1) % 2]
        steps((src, dst), fwin, (one,), coefs)
        emit(dst, j + 1)


WORK = [
    pltpu.VMEM((C, WIN, 128), F32),
    pltpu.VMEM((C, WIN, 128), F32),
    pltpu.VMEM((C * C, 8, 128), F32),
    pltpu.VMEM((C, 8, 128), F32),
    pltpu.VMEM((3, 8, 128), F32),
    pltpu.VMEM((WIN // 8, 8, 128), F32),
]


def call(kernel, ins, outs, out_specs=None, scratch=()):
    specs = out_specs or [VMEM] * len(outs)
    in_specs = [spec for _, spec in ins]
    return pl.pallas_call(
        kernel,
        out_shape=outs,
        in_specs=in_specs,
        out_specs=specs,
        scratch_shapes=list(scratch),
        compiler_params=PARAMS,
        name=kernel.__name__,
    )(*[value for value, _ in ins])


def exchange(near, far):
    places = lax.axis_size("space")
    inner = [(i, i ^ 1) for i in range(places)]
    outer = [(i, j) for i in range(places) for j in [i - 1 if i % 2 == 0 else i + 1] if 0 <= j < places]
    return lax.ppermute(near, "space", inner), lax.ppermute(far, "space", outer)


def shards(guess, forcing, coarse_gain, kernel_levels, kernel_code, settle_levels, settle_class):
    intervals = lax.axis_size("tm")
    rows = guess.reshape(SLICES, C, PLANES, ROWS, 128).transpose(1, 2, 3, 0, 4).reshape(C * OWN * SLICES, 128)
    own, near, far, gain, kmat, speed = call(
        prep_kernel,
        [(rows, VMEM), (forcing, VMEM), (coarse_gain, VMEM)]
        + [(x, SMEM) for x in (kernel_levels, kernel_code, settle_levels, settle_class)],
        [arr(2 * C, OWN, 128), arr(2 * C, HALO, 128), arr(2 * C, HALO, 128), arr(intervals * PIECE, 128), arr(C, C), arr(C)],
        [VMEM] * 4 + [SMEM] * 2,
    )
    ops = [(kmat, SMEM), (speed, SMEM)]
    near, far = exchange(near, far)
    state, near, far, fwin = call(
        first_kernel,
        [(own, VMEM), (near, VMEM), (far, VMEM)] + ops,
        [arr(C, OWN, 128), arr(C, HALO, 128), arr(C, HALO, 128), arr(C, WIN, 128)],
        scratch=WORK,
    )
    near, far = exchange(near, far)
    shifted = lax.ppermute(state, "tm", [(i, i + 1) for i in range(intervals - 1)])
    (element,) = call(
        second_kernel,
        [(state, VMEM), (near, VMEM), (far, VMEM), (fwin, VMEM), (gain, VMEM)] + ops,
        [arr(intervals * PIECE, 128)],
        scratch=WORK,
    )
    pieces = lax.all_to_all(element.reshape(intervals, PIECE * 128), "tm", 0, 0, tiled=True)
    mine = lax.dynamic_slice_in_dim(gain.reshape(intervals, PIECE, 128), lax.axis_index("tm"), 1, axis=0)
    (sums,) = call(
        scan_kernel,
        [(pieces.reshape(intervals * PIECE, 128), VMEM), (mine, VMEM)],
        [arr(intervals * PIECE, 128)],
    )
    back = lax.all_to_all(sums.reshape(intervals, PIECE * 128), "tm", 0, 0, tiled=True)
    state, near, far, corr = call(
        gather_kernel,
        [(back.reshape(intervals * PIECE, 128), VMEM), (shifted, VMEM), (own, VMEM)],
        [arr(C, OWN, 128), arr(C, HALO, 128), arr(C, HALO, 128), arr(C * OWN, 128)],
    )
    near, far = exchange(near, far)
    (updated,) = call(
        last_kernel,
        [(state, VMEM), (near, VMEM), (far, VMEM), (fwin, VMEM)] + ops,
        [arr(C * OWN * SLICES, 128)],
        scratch=WORK,
    )
    updated = updated.reshape(C, PLANES, ROWS, SLICES, 128).transpose(3, 0, 1, 2, 4)
    return (
        updated.reshape(SLICES, C, PLANES, ROWS * 128),
        corr.reshape(1, C, PLANES, ROWS * 128),
    )


def solution(mesh):
    in_specs = (
        P("tm", None, "space", None),
        P(None, "space", None),
        P(None, "space", None),
        P(),
        P(),
        P(),
        P(),
    )
    out_specs = (P("tm", None, "space", None), P("tm", None, "space", None))
    return jax.shard_map(shards, mesh=mesh, in_specs=in_specs, out_specs=out_specs, check_vma=False)
```

time: 528 us -> 100 us (0.19)
  blocking collectives: 229 us -> 0 us
  other arithmetic: 116 us -> 0 us
  local copies, waits for them, and re-layouts: 50.9 us -> 4.31 us
  waiting for transfers between devices: 48.9 us -> 30.4 us
  between operations: 15 us -> 0.8 us
  Pallas kernels: 0 us -> 13 us
  matrix products: 7.47 us -> 0 us
  starting transfers between devices: 56.6 us -> 50.1 us
    unnamed x1 -> x0, blocking collectives: 229 us -> none
    select_n x63 -> x0, other arithmetic: 114 us -> none  [hop(): jnp.where(position < mine, new, old)]
    dynamic_slice x63 -> x1, local copies, waits for them, and re-layouts: 36.9 us -> 0.01 us  [shards(): lax.dynamic_slice_in_dim(gain.reshape(intervals, PIECE, 128), lax.axis_in...]
    ppermute x23 -> x7, starting transfers between devices: 56.6 us -> 21.8 us  [the longest x3 12.7 us: exchange(): lax.ppermute(far, 'space', outer)]
    ppermute x23 -> x7, waiting for transfers between devices: 48.9 us -> 20.3 us  [the longest x1 11.9 us: shards(): lax.ppermute(state, 'tm', [(i, i + 1) for i in range(intervals - 1)])]
    all_to_all x0 -> x2, starting transfers between devices: none -> 28.3 us  [the longest x1 18.8 us: shards(): lax.all_to_all(element.reshape(intervals, PIECE * 128), 'tm', 0, 0, tiled...]
    pallas_call x0 -> x6, Pallas kernels: none -> 13 us  [call(): pl.pallas_call(kernel, out_shape=outs, in_specs=in_specs, out_specs=specs...]
    all_to_all x0 -> x2, waiting for transfers between devices: none -> 10.1 us  [the longest x1 10.1 us: shards(): lax.all_to_all(element.reshape(intervals, PIECE * 128), 'tm', 0, 0, tiled...]
  transfers between devices with their start and end apart: 24 -> 9, of which waited for: 12 -> 5; matrix products, arithmetic and copies ran while one was open for 2% -> 0% of each run, Pallas kernels for 0% -> 0%
where the time goes in v1:
time: 100 us; the launch traced here: 98.6 us
  starting transfers between devices  50.1 us (50%)
  waiting for transfers between devices  30.4 us (30%)
  Pallas kernels  13 us (13%)
  local copies, waits for them, and re-layouts  4.31 us (4%)
    all_to_all x1, starting transfers between devices, shards(): lax.all_to_all(element.reshape(intervals, PIECE * 128), 'tm', 0, 0, tiled...  18.8 us
    pallas_call x6, Pallas kernels, call(): pl.pallas_call(kernel, out_shape=outs, in_specs=in_specs, out_specs=specs...  13 us
    ppermute x3, starting transfers between devices, exchange(): lax.ppermute(far, 'space', outer)  12.7 us
    ppermute x1, waiting for transfers between devices, shards(): lax.ppermute(state, 'tm', [(i, i + 1) for i in range(intervals - 1)])  11.9 us
    all_to_all x1, waiting for transfers between devices, shards(): lax.all_to_all(element.reshape(intervals, PIECE * 128), 'tm', 0, 0, tiled...  10.1 us
    all_to_all x1, starting transfers between devices, shards(): lax.all_to_all(sums.reshape(intervals, PIECE * 128), 'tm', 0, 0, tiled=True)  9.47 us
    ppermute x3, waiting for transfers between devices, exchange(): lax.ppermute(far, 'space', outer)  8.44 us
    ppermute x3, starting transfers between devices, exchange(): lax.ppermute(near, 'space', inner)  5.75 us
  transfers between devices with their start and end apart: 9, of which 5 were waited for; matrix products, arithmetic and copies ran while one was open for 0% of the time, Pallas kernels for 0%

profile of v1, /device:TPU:56, one launch (start us, length us, event | category | flops | bytes accessed | tf_op | source)
XLA Modules:
  0.0 98.6 jit_solution(16951341632075020566)
XLA Ops:
  0.6 0.0 copy-start.4
  0.6 0.0 copy-start.5
  0.7 0.0 copy-start.6
  0.7 0.6 copy-done.4
  1.3 0.0 copy-done.5
  1.3 0.0 copy-done.6
  1.3 0.0 copy-start
  1.3 1.1 %copy-done = f32[4,12,6,512]{3,0,2,1:T(4,128)S(1)} copy-done((f32[4,12,6,512]{3,0,2,1:T(4,128)S(1)}, f32[4,12,6,512]{3,0,2,1:T(4,128)}, u32[]{:S(2)}) %copy-start) | copy-done | bytes 589848
  2.4 0.0 copy-start.1
  2.4 0.9 copy-done.1
  3.3 0.0 copy-start.2
  3.3 0.9 copy-done.2
  4.2 0.0 copy-start.3
  4.2 0.7 copy-done.3
  4.9 1.6 %prep_kernel.1 = (f32[24,24,128]{2,1,0:T(8,128)S(1)}, f32[24,16,128]{2,1,0:T(8,128)S(1)}, f32[24,16,128]{2,1,0:T(8,128)S(1)}, f32[320,128]{1,0:T(8,128)S(1)}, f32[12,12]{1,0:T(8,128)S(1)}, /*index=5*/f32[12]{0:T(128)S(1)}) custom-call(f32[1152,128]{1,0:T(8,128)S(1)} %bitcast.17, f32[12,6,512]{2,1,0:T(8,128)S(1)} %copy-done.1, f32[12,6,512]{2,1,0:T(8,128)S(1)} %copy-done.2, ...), custom_call_target="tpu_custom_call" | custom-call | tf_op jit(solution)/shard_map/prep_kernel/pallas_call | solution.py:272
  6.6 1.9 %collective-permute-start = (f32[24,16,128]{2,1,0:T(8,128)S(1)}, f32[24,16,128]{2,1,0:T(8,128)S(1)}, u32[]{:S(2)}, u32[]{:S(2)}) collective-permute-start(f32[24,16,128]{2,1,0:T(8,128)S(1)} %get-tuple-element.17), channel_id=1, source_target_pairs={{0,1},{1,0},{2,3},{3,2},{4,5},{5,4},{6,7},{7,6},{8,9},{9,8},{10,11... | collective-permute-start | bytes 589832 | tf_op jit(solution)/shard_map/ppermute | solution.py:287
  8.5 3.4 %collective-permute-start.1 = (f32[24,16,128]{2,1,0:T(8,128)S(1)}, f32[24,16,128]{2,1,0:T(8,128)S(1)}, u32[]{:S(2)}, u32[]{:S(2)}) collective-permute-start(f32[24,16,128]{2,1,0:T(8,128)S(1)} %get-tuple-element.18), channel_id=1, source_target_pairs={{1,2},{2,1},{3,4},{4,3},{5,6},{6,5},{9,10},{10,9},{11,12},{12,11},... | collective-permute-start | bytes 589832 | tf_op jit(solution)/shard_map/ppermute | solution.py:287
  11.9 0.0 collective-permute-done.near
  11.9 3.6 %collective-permute-done.1.far = f32[24,16,128]{2,1,0:T(8,128)S(1)} collective-permute-done((f32[24,16,128]{2,1,0:T(8,128)S(1)}, f32[24,16,128]{2,1,0:T(8,128)S(1)}, u32[]{:S(2)}, u32[]{:S(2)}) %collective-permute-start.1) | collective-permute-done | bytes 196640 | tf_op jit(solution)/shard_map/ppermute | solution.py:287
  15.5 3.0 %first_kernel.1 = (f32[12,24,128]{2,1,0:T(8,128)S(1)}, f32[12,16,128]{2,1,0:T(8,128)S(1)}, f32[12,16,128]{2,1,0:T(8,128)S(1)}, f32[12,64,128]{2,1,0:T(8,128)S(1)}) custom-call(f32[24,24,128]{2,1,0:T(8,128)S(1)} %get-tuple-element.16.own, f32[24,16,128]{2,1,0:T(8,128)S(1)} %collective-permute-done.near, f32[24,16,128]{2,1,0:T(8,128)S(1)} %collective-permute-done.1.far, ...), custom_call_target="tpu_custom_call" | custom-call | tf_op jit(solution)/shard_map/first_kernel/pallas_call | solution.py:272
  18.5 1.9 %collective-permute-start.2 = (f32[12,16,128]{2,1,0:T(8,128)S(1)}, f32[12,16,128]{2,1,0:T(8,128)S(1)}, u32[]{:S(2)}, u32[]{:S(2)}) collective-permute-start(f32[12,16,128]{2,1,0:T(8,128)S(1)} %get-tuple-element.22), channel_id=1, source_target_pairs={{0,1},{1,0},{2,3},{3,2},{4,5},{5,4},{6,7},{7,6},{8,9},{9,8},{10,11... | collective-permute-start | bytes 294920 | tf_op jit(solution)/shard_map/ppermute | solution.py:287
  20.5 3.4 %collective-permute-start.3 = (f32[12,16,128]{2,1,0:T(8,128)S(1)}, f32[12,16,128]{2,1,0:T(8,128)S(1)}, u32[]{:S(2)}, u32[]{:S(2)}) collective-permute-start(f32[12,16,128]{2,1,0:T(8,128)S(1)} %get-tuple-element.23), channel_id=1, source_target_pairs={{1,2},{2,1},{3,4},{4,3},{5,6},{6,5},{9,10},{10,9},{11,12},{12,11},... | collective-permute-start | bytes 294920 | tf_op jit(solution)/shard_map/ppermute | solution.py:287
  23.8 0.0 collective-permute-done.2.near
  23.8 2.6 %collective-permute-done.3.far = f32[12,16,128]{2,1,0:T(8,128)S(1)} collective-permute-done((f32[12,16,128]{2,1,0:T(8,128)S(1)}, f32[12,16,128]{2,1,0:T(8,128)S(1)}, u32[]{:S(2)}, u32[]{:S(2)}) %collective-permute-start.3) | collective-permute-done | bytes 98336 | tf_op jit(solution)/shard_map/ppermute | solution.py:287
  26.4 3.7 %second_kernel.1 = f32[320,128]{1,0:T(8,128)} custom-call(f32[12,24,128]{2,1,0:T(8,128)S(1)} %get-tuple-element.21.state, f32[12,16,128]{2,1,0:T(8,128)S(1)} %collective-permute-done.2.near, f32[12,16,128]{2,1,0:T(8,128)S(1)} %collective-permute-done.3.far, f32[12,64,128]{2,1,0:T(8,128)S(1)} %get-tuple-element.24.fwin, ...), custom_call_target="tpu_custom_call" | custom-call | tf_op jit(solution)/shard_map/second_kernel/pallas_call | solution.py:272
  30.0 18.8 %all-to-all-start = ((f32[64,1,640]{2,1,0:T(1,128)}), f32[64,1,640]{2,1,0:T(1,128)S(1)}, u32[]{:S(2)}, u32[]{:S(2)}) async-start(f32[64,1,640]{2,1,0:T(1,128)} %bitcast.3), calls=%async_computation | async-start | bytes 327680 | tf_op jit(solution)/shard_map/all_to_all | solution.py:316
  48.9 10.1 %all-to-all-done = f32[64,1,640]{2,1,0:T(1,128)S(1)} async-done(((f32[64,1,640]{2,1,0:T(1,128)}), f32[64,1,640]{2,1,0:T(1,128)S(1)}, u32[]{:S(2)}, u32[]{:S(2)}) %all-to-all-start) | async-done | bytes 163872 | tf_op jit(solution)/shard_map/all_to_all | solution.py:316
  59.0 0.8 scan_kernel.1
  59.8 9.5 %all-to-all-start.1 = ((f32[64,1,640]{2,1,0:T(1,128)}), f32[64,1,640]{2,1,0:T(1,128)S(1)}, u32[]{:S(2)}, u32[]{:S(2)}) async-start(f32[64,1,640]{2,1,0:T(1,128)} %bitcast.5), calls=%async_computation.1 | async-start | bytes 327680 | tf_op jit(solution)/shard_map/all_to_all | solution.py:323
  69.2 3.4 %collective-permute-start.4 = (f32[12,24,128]{2,1,0:T(8,128)S(1)}, f32[12,24,128]{2,1,0:T(8,128)S(1)}, u32[]{:S(2)}, u32[]{:S(2)}) collective-permute-start(f32[12,24,128]{2,1,0:T(8,128)S(1)} %get-tuple-element.21.state), channel_id=1, source_target_pairs={{0,8},{8,16},{16,24},{24,32},{32,40},{40,48},{48,56},{56,64},{64,7... | collective-permute-start | bytes 442376 | tf_op jit(solution)/shard_map/ppermute | solution.py:309
  72.6 11.9 %collective-permute-done.4.shifted = f32[12,24,128]{2,1,0:T(8,128)S(1)} collective-permute-done((f32[12,24,128]{2,1,0:T(8,128)S(1)}, f32[12,24,128]{2,1,0:T(8,128)S(1)}, u32[]{:S(2)}, u32[]{:S(2)}) %collective-permute-start.4) | collective-permute-done | bytes 147488 | tf_op jit(solution)/shard_map/ppermute | solution.py:309
  84.5 0.0 all-to-all-done.1
  84.5 0.7 gather_kernel.1
  85.2 1.9 %collective-permute-start.5 = (f32[12,16,128]{2,1,0:T(8,128)S(1)}, f32[12,16,128]{2,1,0:T(8,128)S(1)}, u32[]{:S(2)}, u32[]{:S(2)}) collective-permute-start(f32[12,16,128]{2,1,0:T(8,128)S(1)} %get-tuple-element.27), channel_id=1, source_target_pairs={{0,1},{1,0},{2,3},{3,2},{4,5},{5,4},{6,7},{7,6},{8,9},{9,8},{10,11... | collective-permute-start | bytes 294920 | tf_op jit(solution)/shard_map/ppermute | solution.py:287
  87.1 6.0 %collective-permute-start.6 = (f32[12,16,128]{2,1,0:T(8,128)S(1)}, f32[12,16,128]{2,1,0:T(8,128)S(1)}, u32[]{:S(2)}, u32[]{:S(2)}) collective-permute-start(f32[12,16,128]{2,1,0:T(8,128)S(1)} %get-tuple-element.28), channel_id=1, source_target_pairs={{1,2},{2,1},{3,4},{4,3},{5,6},{6,5},{9,10},{10,9},{11,12},{12,11},... | collective-permute-start | bytes 294920 | tf_op jit(solution)/shard_map/ppermute | solution.py:287
  93.1 0.0 collective-permute-done.5.near
  93.1 2.3 %collective-permute-done.6.far = f32[12,16,128]{2,1,0:T(8,128)S(1)} collective-permute-done((f32[12,16,128]{2,1,0:T(8,128)S(1)}, f32[12,16,128]{2,1,0:T(8,128)S(1)}, u32[]{:S(2)}, u32[]{:S(2)}) %collective-permute-start.6) | collective-permute-done | bytes 98336 | tf_op jit(solution)/shard_map/ppermute | solution.py:287
  95.4 3.2 %last_kernel.1 = f32[1152,128]{1,0:T(8,128)} custom-call(f32[12,24,128]{2,1,0:T(8,128)S(1)} %get-tuple-element.26.state, f32[12,16,128]{2,1,0:T(8,128)S(1)} %collective-permute-done.5.near, f32[12,16,128]{2,1,0:T(8,128)S(1)} %collective-permute-done.6.far, f32[12,64,128]{2,1,0:T(8,128)S(1)} %get-tuple-element.24.fwin, f32[12,12]{1,0:T(8,128)S(1)} %get-tuple-element.19.kmat, ...), custom_call_target="tpu_custom_call" | custom-call | tf_op jit(solution)/shard_map/last_kernel/pallas_call | solution.py:272
  (2 shorter events, 0.0 us)
Async XLA Ops:
  0.6 0.7 copy-start.4
  0.6 0.7 copy-start.5
  0.7 0.7 copy-start.6
  1.3 1.1 %copy-start = (f32[4,12,6,512]{3,0,2,1:T(4,128)S(1)}, f32[4,12,6,512]{3,0,2,1:T(4,128)}, u32[]{:S(2)}) copy-start(f32[4,12,6,512]{3,0,2,1:T(4,128)} %param.7) | copy-start | bytes 1769476
  2.4 0.9 copy-start.1
  3.3 0.9 copy-start.2
  4.2 0.7 copy-start.3
  6.6 5.3 %collective-permute-start = (f32[24,16,128]{2,1,0:T(8,128)S(1)}, f32[24,16,128]{2,1,0:T(8,128)S(1)}, u32[]{:S(2)}, u32[]{:S(2)}) collective-permute-start(f32[24,16,128]{2,1,0:T(8,128)S(1)} %get-tuple-element.17), channel_id=1, source_target_pairs={{0,1},{1,0},{2,3},{3,2},{4,5},{5,4},{6,7},{7,6},{8,9},{9,8},{10,11... | collective-permute-start | bytes 589832 | tf_op jit(solution)/shard_map/ppermute | solution.py:287
  8.5 7.0 %collective-permute-start.1 = (f32[24,16,128]{2,1,0:T(8,128)S(1)}, f32[24,16,128]{2,1,0:T(8,128)S(1)}, u32[]{:S(2)}, u32[]{:S(2)}) collective-permute-start(f32[24,16,128]{2,1,0:T(8,128)S(1)} %get-tuple-element.18), channel_id=1, source_target_pairs={{1,2},{2,1},{3,4},{4,3},{5,6},{6,5},{9,10},{10,9},{11,12},{12,11},... | collective-permute-start | bytes 589832 | tf_op jit(solution)/shard_map/ppermute | solution.py:287
  18.5 5.3 %collective-permute-start.2 = (f32[12,16,128]{2,1,0:T(8,128)S(1)}, f32[12,16,128]{2,1,0:T(8,128)S(1)}, u32[]{:S(2)}, u32[]{:S(2)}) collective-permute-start(f32[12,16,128]{2,1,0:T(8,128)S(1)} %get-tuple-element.22), channel_id=1, source_target_pairs={{0,1},{1,0},{2,3},{3,2},{4,5},{5,4},{6,7},{7,6},{8,9},{9,8},{10,11... | collective-permute-start | bytes 294920 | tf_op jit(solution)/shard_map/ppermute | solution.py:287
  20.5 5.9 %collective-permute-start.3 = (f32[12,16,128]{2,1,0:T(8,128)S(1)}, f32[12,16,128]{2,1,0:T(8,128)S(1)}, u32[]{:S(2)}, u32[]{:S(2)}) collective-permute-start(f32[12,16,128]{2,1,0:T(8,128)S(1)} %get-tuple-element.23), channel_id=1, source_target_pairs={{1,2},{2,1},{3,4},{4,3},{5,6},{6,5},{9,10},{10,9},{11,12},{12,11},... | collective-permute-start | bytes 294920 | tf_op jit(solution)/shard_map/ppermute | solution.py:287
  30.0 28.9 %all-to-all-start = ((f32[64,1,640]{2,1,0:T(1,128)}), f32[64,1,640]{2,1,0:T(1,128)S(1)}, u32[]{:S(2)}, u32[]{:S(2)}) async-start(f32[64,1,640]{2,1,0:T(1,128)} %bitcast.3), calls=%async_computation | async-start | bytes 327680 | tf_op jit(solution)/shard_map/all_to_all | solution.py:316
  59.8 24.7 %all-to-all-start.1 = ((f32[64,1,640]{2,1,0:T(1,128)}), f32[64,1,640]{2,1,0:T(1,128)S(1)}, u32[]{:S(2)}, u32[]{:S(2)}) async-start(f32[64,1,640]{2,1,0:T(1,128)} %bitcast.5), calls=%async_computation.1 | async-start | bytes 327680 | tf_op jit(solution)/shard_map/all_to_all | solution.py:323
  69.2 15.3 %collective-permute-start.4 = (f32[12,24,128]{2,1,0:T(8,128)S(1)}, f32[12,24,128]{2,1,0:T(8,128)S(1)}, u32[]{:S(2)}, u32[]{:S(2)}) collective-permute-start(f32[12,24,128]{2,1,0:T(8,128)S(1)} %get-tuple-element.21.state), channel_id=1, source_target_pairs={{0,8},{8,16},{16,24},{24,32},{32,40},{40,48},{48,56},{56,64},{64,7... | collective-permute-start | bytes 442376 | tf_op jit(solution)/shard_map/ppermute | solution.py:309
  85.2 7.9 %collective-permute-start.5 = (f32[12,16,128]{2,1,0:T(8,128)S(1)}, f32[12,16,128]{2,1,0:T(8,128)S(1)}, u32[]{:S(2)}, u32[]{:S(2)}) collective-permute-start(f32[12,16,128]{2,1,0:T(8,128)S(1)} %get-tuple-element.27), channel_id=1, source_target_pairs={{0,1},{1,0},{2,3},{3,2},{4,5},{5,4},{6,7},{7,6},{8,9},{9,8},{10,11... | collective-permute-start | bytes 294920 | tf_op jit(solution)/shard_map/ppermute | solution.py:287
  87.1 8.3 %collective-permute-start.6 = (f32[12,16,128]{2,1,0:T(8,128)S(1)}, f32[12,16,128]{2,1,0:T(8,128)S(1)}, u32[]{:S(2)}, u32[]{:S(2)}) collective-permute-start(f32[12,16,128]{2,1,0:T(8,128)S(1)} %get-tuple-element.28), channel_id=1, source_target_pairs={{1,2},{2,1},{3,4},{4,3},{5,6},{6,5},{9,10},{10,9},{11,12},{12,11},... | collective-permute-start | bytes 294920 | tf_op jit(solution)/shard_map/ppermute | solution.py:287

commit v2 on v1

v2 whole, which is shorter than its diff:
```python
import functools

import jax
import jax.numpy as jnp
from jax import lax
from jax.experimental import pallas as pl
from jax.experimental.pallas import tpu as pltpu
from jax.sharding import PartitionSpec as P

F32 = jnp.float32
C = 12
NY = 16
NZ = 32
PLANES = 6
NX = 48
SLICES = 4
ROWS = 4
OWN = PLANES * ROWS
HALO = 4 * ROWS
THREE = 3 * ROWS
WIN = 64
BASE = 5 * ROWS
PIECE = 5
VMEM = pl.BlockSpec(memory_space=pltpu.VMEM)
SMEM = pl.BlockSpec(memory_space=pltpu.SMEM)
HBM = pl.BlockSpec(memory_space=pl.ANY)


def arr(*shape):
    return jax.ShapeDtypeStruct(shape, F32)


def even_place():
    return lax.axis_index("space") % 2 == 0


def put_sends(first, last, near, far):
    even = even_place()

    @pl.when(even)
    def _():
        last(near)
        first(far)

    @pl.when(jnp.logical_not(even))
    def _():
        first(near)
        last(far)


def put_halo(buf, near, far, count, start):
    even = even_place()

    def put(src, row):
        for c in range(C):
            buf[c, row : row + count, :] = src[start + c * count : start + (c + 1) * count, :]

    @pl.when(even)
    def _():
        put(far, BASE - count)
        put(near, BASE + OWN)

    @pl.when(jnp.logical_not(even))
    def _():
        put(near, BASE - count)
        put(far, BASE + OWN)


def pack(src, row, count, start):
    def into(dst):
        for c in range(C):
            dst[start + c * count : start + (c + 1) * count, :] = src[c, row : row + count, :]

    return into


def prep_kernel(guess, forcing, own, force, near, far, raw, fraw, sems):
    one = pltpu.make_async_copy(forcing, fraw, sems.at[0])
    two = pltpu.make_async_copy(guess, raw, sems.at[1])
    one.start()
    two.start()
    one.wait()
    for c in range(C):
        for r in range(ROWS):
            force[c, pl.ds(r, PLANES, stride=ROWS), :] = fraw[c, :, 128 * r : 128 * r + 128] * 0.1
    two.wait()
    for c in range(C):
        own[c] = raw[pl.ds(c * OWN * SLICES, OWN, stride=SLICES), :]

    def first(dst):
        pack(own, 0, HALO, 0)(dst)
        pack(force, 0, THREE, C * HALO)(dst)

    def last(dst):
        pack(own, OWN - HALO, HALO, 0)(dst)
        pack(force, OWN - THREE, THREE, C * HALO)(dst)

    put_sends(first, last, near, far)


def setup_kernel(raw, lv, cd, st, kl, gain_out, kv, wup, wfix, mask):
    for c in range(C):
        for r in range(ROWS):
            gain_out[pl.ds(c * OWN + r, PLANES, stride=ROWS), :] = raw[c, :, 128 * r : 128 * r + 128]
    gain_out[C * OWN :, :] = jnp.zeros((gain_out.shape[0] - C * OWN, 128), F32)
    lane = lax.broadcasted_iota(jnp.int32, (8, 128), 1)
    row = lax.broadcasted_iota(jnp.int32, (8, 128), 0)
    z = lane % NZ
    edge_row = row % ROWS
    for j in range(C):
        col = [lv[cd[i, j]] for i in range(C)]
        total = functools.reduce(lambda x, y: x + y, col)
        speed = st[kl[j]]
        for i in range(C):
            v = (col[i] - total) + (1.0 - 0.48) - speed if i == j else col[i]
            kv[i * C + j] = jnp.full((8, 128), v, F32)
        wup[j] = jnp.where(z < NZ - 1, 0.08 + speed, 0.0)
    wfix[0] = jnp.where(z > 0, F32(0.08), F32(0.0))
    wfix[1] = jnp.where(jnp.logical_and(lane >= 96, edge_row == ROWS - 1), F32(0.0), F32(0.08))
    wfix[2] = jnp.where(jnp.logical_and(lane < 32, edge_row == 0), F32(0.0), F32(0.08))
    start = lax.axis_index("space") * PLANES - 5
    for t in range(WIN // 8):
        plane = start + 2 * t + row // ROWS
        inside = jnp.logical_and(plane >= 0, plane < NX)
        mask[t] = jnp.where(inside, F32(1.0), F32(0.0))


def clear_edges(buf):
    z = jnp.zeros((C, 8, 128), F32)
    buf[:, 0:8, :] = z
    buf[:, WIN - 8 : WIN, :] = z


def block_step(src, dst, fwin, t, kv, wup, wfix, mask):
    lane = lax.broadcasted_iota(jnp.int32, (8, 128), 1)
    row = lax.broadcasted_iota(jnp.int32, (8, 128), 0)
    low = row < ROWS
    right = lane >= 96
    left = lane < 32
    wdn, wah, wbe = wfix[0], wfix[1], wfix[2]

    def rows(k):
        return pl.ds((t + k) * 8, 8)

    acc = []
    for i in range(C):
        p = [src[i, rows(k), :] for k in (-1, 0, 1, 2)]
        q = [pltpu.roll(v, 4, 0) for v in p]
        pair = []
        for k in (0, 1):
            c = p[k + 1]
            xs = q[k + 1] + jnp.where(low, q[k], q[k + 2])
            up = pltpu.roll(c, 127, 1)
            dn = pltpu.roll(c, 1, 1)
            ra = pltpu.roll(c, 96, 1)
            rb = pltpu.roll(c, 32, 1)
            ah = jnp.where(right, pltpu.roll(ra, 7, 0), ra)
            be = jnp.where(left, pltpu.roll(rb, 1, 0), rb)
            new = fwin[i, rows(k), :] + 0.08 * xs
            new = new + wup[i] * up
            new = new + wdn * dn
            new = new + wah * ah
            new = new + wbe * be
            pair.append(new)
        acc.append(pair)
    for j in range(C):
        c = [src[j, rows(k), :] for k in (0, 1)]
        for i in range(C):
            w = kv[i * C + j]
            acc[i] = [acc[i][k] + w * c[k] for k in (0, 1)]
    for k in (0, 1):
        m = mask[t + k]
        for i in range(C):
            dst[i, rows(k), :] = acc[i][k] * m


def steps(bufs, fwin, plan, coefs):
    for s, (first, count) in enumerate(plan):
        src, dst = bufs[s % 2], bufs[(s + 1) % 2]
        for b in range(count):
            block_step(src, dst, fwin, first + 2 * b, *coefs)


FOUR = ((1, 3), (1, 3), (2, 2), (2, 2))


def first_kernel(own, force, far, near, kv, wup, wfix, mask, state, send_near, send_far, fwin, a, b):
    clear_edges(a)
    clear_edges(b)
    clear_edges(fwin)
    a[:, BASE : BASE + OWN, :] = own[...]
    fwin[:, BASE : BASE + OWN, :] = force[...]
    put_halo(a, near, far, HALO, 0)
    put_halo(fwin, near, far, THREE, C * HALO)
    steps((a, b), fwin, FOUR, (kv, wup, wfix, mask))
    state[...] = a[:, BASE : BASE + OWN, :]
    put_sends(pack(state, 0, HALO, 0), pack(state, OWN - HALO, HALO, 0), send_near, send_far)


def second_kernel(state, far, near, fwin, gain, kv, wup, wfix, mask, out, a, b):
    clear_edges(a)
    clear_edges(b)
    a[:, BASE : BASE + OWN, :] = state[...]
    put_halo(a, near, far, HALO, 0)
    steps((a, b), fwin, FOUR, (kv, wup, wfix, mask))
    use = jnp.where(lax.axis_index("tm") > 0, F32(1.0), F32(0.0))
    for c in range(C):
        here = pl.ds(c * OWN, OWN)
        out[here, :] = a[c, BASE : BASE + OWN, :] - use * (gain[here, :] * state[c])
    out[C * OWN :, :] = jnp.zeros((out.shape[0] - C * OWN, 128), F32)


def scan_kernel(pieces, gain, out):
    count = pieces.shape[0] // PIECE
    mine = gain[0]
    running = pieces[0:PIECE, :]
    out[0 : 2 * PIECE, :] = jnp.zeros((2 * PIECE, 128), F32)
    for k in range(2, count):
        out[k * PIECE : (k + 1) * PIECE, :] = running
        if k + 1 < count:
            m = k - 1
            running = mine * running + pieces[m * PIECE : (m + 1) * PIECE, :]


def gather_kernel(pieces, one, own, state, near, far):
    k = lax.axis_index("tm")

    @pl.when(k == 0)
    def _():
        state[...] = own[...]

    @pl.when(k == 1)
    def _():
        state[...] = one[...]

    @pl.when(k >= 2)
    def _():
        for c in range(C):
            state[c] = pieces[c * OWN : (c + 1) * OWN, :]

    put_sends(pack(state, 0, THREE, 0), pack(state, OWN - THREE, THREE, 0), near, far)


def last_kernel(state, far, near, fwin, shifted, kv, wup, wfix, mask, out, corr, a, b):
    clear_edges(a)
    clear_edges(b)
    a[:, BASE : BASE + OWN, :] = state[...]
    put_halo(a, near, far, THREE, 0)

    def emit(buf, j):
        for c in range(C):
            out[pl.ds(c * OWN * SLICES + j, OWN, stride=SLICES), :] = buf[c, BASE : BASE + OWN, :]

    emit(a, 0)
    bufs = (a, b)
    for j, one in enumerate(((1, 3), (2, 2), (2, 2))):
        src, dst = bufs[j % 2], bufs[(j + 1) % 2]
        steps((src, dst), fwin, (one,), (kv, wup, wfix, mask))
        emit(dst, j + 1)
    late = lax.axis_index("tm") >= 2
    for c in range(C):
        corr[c * OWN : (c + 1) * OWN, :] = jnp.where(late, state[c] - shifted[c], 0.0)


WORK = [pltpu.VMEM((C, WIN, 128), F32), pltpu.VMEM((C, WIN, 128), F32)]


def call(kernel, ins, outs, scratch=(), place=None, grant=32):
    return pl.pallas_call(
        kernel,
        out_shape=outs,
        in_specs=place or [VMEM] * len(ins),
        out_specs=[VMEM] * len(outs),
        scratch_shapes=list(scratch),
        compiler_params=pltpu.CompilerParams(vmem_limit_bytes=grant * 1024 * 1024),
        name=kernel.__name__,
    )(*ins)


def exchange(near, far):
    places = lax.axis_size("space")
    inner = [(i, i ^ 1) for i in range(places)]
    outer = [(i, j) for i in range(places) for j in [i - 1 if i % 2 == 0 else i + 1] if 0 <= j < places]
    far = lax.ppermute(far, "space", outer)
    near = lax.ppermute(near, "space", inner)
    return near, far


def shards(guess, forcing, coarse_gain, kernel_levels, kernel_code, settle_levels, settle_class):
    intervals = lax.axis_size("tm")
    rows = guess.reshape(SLICES, C, PLANES, ROWS, 128).transpose(1, 2, 3, 0, 4).reshape(C * OWN * SLICES, 128)
    slab = arr(C, OWN, 128)
    wide, four, three = (arr(C * n, 128) for n in (HALO + THREE, HALO, THREE))
    pieces = arr(intervals * PIECE, 128)
    own, force, near, far = call(
        prep_kernel,
        [rows, forcing],
        [slab, slab, wide, wide],
        [pltpu.VMEM(rows.shape, F32), pltpu.VMEM(forcing.shape, F32), pltpu.SemaphoreType.DMA((2,))],
        [HBM] * 2,
        60,
    )
    near, far = exchange(near, far)
    small = (kernel_levels, kernel_code, settle_levels, settle_class)
    gain, *coefs = call(
        setup_kernel,
        [coarse_gain, *small],
        [pieces, arr(C * C, 8, 128), arr(C, 8, 128), arr(3, 8, 128), arr(WIN // 8, 8, 128)],
        place=[VMEM] + [SMEM] * len(small),
    )
    mine = lax.dynamic_slice_in_dim(gain.reshape(intervals, PIECE, 128), lax.axis_index("tm"), 1, axis=0)
    state, near, far, fwin = call(
        first_kernel, [own, force, far, near, *coefs], [slab, four, four, arr(C, WIN, 128)], WORK
    )
    near, far = exchange(near, far)
    one = lax.ppermute(state, "tm", [(0, 1)])
    shifted = lax.ppermute(state, "tm", [(i, i + 1) for i in range(1, intervals - 1)])
    (element,) = call(second_kernel, [state, far, near, fwin, gain, *coefs], [pieces], WORK)
    spread = lax.all_to_all(element.reshape(intervals, PIECE * 128), "tm", 0, 0, tiled=True)
    (sums,) = call(scan_kernel, [spread.reshape(intervals * PIECE, 128), mine], [pieces])
    back = lax.all_to_all(sums.reshape(intervals, PIECE * 128), "tm", 0, 0, tiled=True)
    state, near, far = call(
        gather_kernel, [back.reshape(intervals * PIECE, 128), one, own], [slab, three, three]
    )
    near, far = exchange(near, far)
    updated, corr = call(
        last_kernel,
        [state, far, near, fwin, shifted, *coefs],
        [arr(C * OWN * SLICES, 128), arr(C * OWN, 128)],
        WORK,
    )
    updated = updated.reshape(C, PLANES, ROWS, SLICES, 128).transpose(3, 0, 1, 2, 4)
    return (
        updated.reshape(SLICES, C, PLANES, ROWS * 128),
        corr.reshape(1, C, PLANES, ROWS * 128),
    )


def solution(mesh):
    in_specs = (
        P("tm", None, "space", None),
        P(None, "space", None),
        P(None, "space", None),
        P(),
        P(),
        P(),
        P(),
    )
    out_specs = (P("tm", None, "space", None), P("tm", None, "space", None))
    return jax.shard_map(shards, mesh=mesh, in_specs=in_specs, out_specs=out_specs, check_vma=False)
```

time: 100 us -> 86.2 us (0.86)
  the two profiles are of different devices: /device:TPU:56 before, /device:TPU:1 now
where the time goes in v2:
time: 86.2 us; the launch traced here: 85.7 us
  starting transfers between devices  46.6 us (54%)
  waiting for transfers between devices  27.3 us (32%)
  Pallas kernels  9.98 us (12%)
  local copies, waits for them, and re-layouts  0.97 us (1%)
  between operations  0.88 us (1%)
    all_to_all x1, starting transfers between devices, shards(): lax.all_to_all(element.reshape(intervals, PIECE * 128), 'tm', 0, 0, tiled...  16 us
    all_to_all x1, waiting for transfers between devices, shards(): lax.all_to_all(element.reshape(intervals, PIECE * 128), 'tm', 0, 0, tiled...  13.7 us
    ppermute x3, starting transfers between devices, exchange(): far = lax.ppermute(far, 'space', outer)  12.3 us
    pallas_call x7, Pallas kernels, call(): pl.pallas_call(kernel, out_shape=outs, in_specs=place or [VMEM] * len(ins...  9.98 us
    ppermute x3, starting transfers between devices, exchange(): near = lax.ppermute(near, 'space', inner)  8.7 us
    all_to_all x1, waiting for transfers between devices, shards(): lax.all_to_all(sums.reshape(intervals, PIECE * 128), 'tm', 0, 0, tiled=True)  8.31 us
    all_to_all x1, starting transfers between devices, shards(): lax.all_to_all(sums.reshape(intervals, PIECE * 128), 'tm', 0, 0, tiled=True)  6.05 us
    ppermute x1, starting transfers between devices, shards(): one = lax.ppermute(state, 'tm', [(0, 1)])  2.92 us
  transfers between devices with their start and end apart: 10, of which 7 were waited for; matrix products, arithmetic and copies ran while one was open for 0% of the time, Pallas kernels for 1%

profile of v2, /device:TPU:1, one launch (start us, length us, event | category | flops | bytes accessed | tf_op | source)
XLA Modules:
  0.0 85.7 jit_solution(11608577589115835264)
XLA Ops:
  0.6 0.0 copy-start.1
  0.6 0.0 copy-start.3
  0.7 0.0 copy-start.4
  0.7 0.0 copy-start.5
  0.7 0.0 copy-start.6
  0.7 2.1 %prep_kernel.1 = (f32[12,24,128]{2,1,0:T(8,128)}, f32[12,24,128]{2,1,0:T(8,128)}, f32[336,128]{1,0:T(8,128)}, f32[336,128]{1,0:T(8,128)}) custom-call(f32[1152,128]{1,0:T(8,128)} %bitcast.17, f32[12,6,512]{2,1,0:T(8,128)} %forcing.1), custom_call_target="tpu_custom_call" | custom-call | tf_op jit(solution)/shard_map/prep_kernel/pallas_call | solution.py:269
  2.8 0.0 copy-start
  2.8 4.7 %collective-permute-start = (f32[336,128]{1,0:T(8,128)}, f32[336,128]{1,0:T(8,128)S(1)}, u32[]{:S(2)}, u32[]{:S(2)}) collective-permute-start(f32[336,128]{1,0:T(8,128)} %get-tuple-element.22), channel_id=1, source_target_pairs={{1,2},{2,1},{3,4},{4,3},{5,6},{6,5},{9,10},{10,9},{11,12},{12,11},... | collective-permute-start | bytes 516104 | tf_op jit(solution)/shard_map/ppermute | solution.py:284
  7.6 4.9 %collective-permute-start.1 = (f32[336,128]{1,0:T(8,128)}, f32[336,128]{1,0:T(8,128)S(1)}, u32[]{:S(2)}, u32[]{:S(2)}) collective-permute-start(f32[336,128]{1,0:T(8,128)} %get-tuple-element.23), channel_id=1, source_target_pairs={{0,1},{1,0},{2,3},{3,2},{4,5},{5,4},{6,7},{7,6},{8,9},{9,8},{10,11... | collective-permute-start | bytes 516104 | tf_op jit(solution)/shard_map/ppermute | solution.py:285
  12.5 0.0 copy-done.1
  12.5 0.0 copy-done.3
  12.5 0.0 copy-done.4
  12.5 0.0 copy-done.5
  12.5 0.0 copy-done.6
  12.5 0.9 %setup_kernel.1 = (f32[320,128]{1,0:T(8,128)S(1)}, f32[144,8,128]{2,1,0:T(8,128)S(1)}, f32[12,8,128]{2,1,0:T(8,128)S(1)}, f32[3,8,128]{2,1,0:T(8,128)S(1)}, f32[8,8,128]{2,1,0:T(8,128)S(1)}) custom-call(f32[12,6,512]{2,1,0:T(8,128)S(1)} %copy-done.1, f32[8]{0:T(128)S(1)} %copy-done.4, s32[12,12]{1,0:T(8,128)S(1)} %copy-done.3, f32[4]{0:T(128)S(1)} %copy-done.5, ...), custom_call_target="tpu_custom_call" | custom-call | tf_op jit(solution)/shard_map/setup_kernel/pallas_call | solution.py:269
  13.4 0.0 collective-permute-done.far
  13.4 0.3 collective-permute-done.1.near
  13.7 0.0 copy-done
  13.7 0.0 copy-start.2
  13.7 0.9 %copy-done.2 = f32[12,24,128]{2,1,0:T(8,128)S(1)} copy-done((f32[12,24,128]{2,1,0:T(8,128)S(1)}, f32[12,24,128]{2,1,0:T(8,128)}, u32[]{:S(2)}) %copy-start.2) | copy-done | bytes 147480
  14.6 1.6 %first_kernel.1 = (f32[12,24,128]{2,1,0:T(8,128)S(1)}, f32[192,128]{1,0:T(8,128)S(1)}, f32[192,128]{1,0:T(8,128)S(1)}, f32[12,64,128]{2,1,0:T(8,128)S(1)}) custom-call(f32[12,24,128]{2,1,0:T(8,128)S(1)} %copy-done, f32[12,24,128]{2,1,0:T(8,128)S(1)} %copy-done.2, f32[336,128]{1,0:T(8,128)S(1)} %collective-permute-done.far, ...), custom_call_target="tpu_custom_call" | custom-call | tf_op jit(solution)/shard_map/first_kernel/pallas_call | solution.py:269
  16.2 1.9 %collective-permute-start.2 = (f32[192,128]{1,0:T(8,128)S(1)}, f32[192,128]{1,0:T(8,128)S(1)}, u32[]{:S(2)}, u32[]{:S(2)}) collective-permute-start(f32[192,128]{1,0:T(8,128)S(1)} %get-tuple-element.29), channel_id=1, source_target_pairs={{1,2},{2,1},{3,4},{4,3},{5,6},{6,5},{9,10},{10,9},{11,12},{12,11},... | collective-permute-start | bytes 294920 | tf_op jit(solution)/shard_map/ppermute | solution.py:284
  18.2 1.9 %collective-permute-start.3 = (f32[192,128]{1,0:T(8,128)S(1)}, f32[192,128]{1,0:T(8,128)S(1)}, u32[]{:S(2)}, u32[]{:S(2)}) collective-permute-start(f32[192,128]{1,0:T(8,128)S(1)} %get-tuple-element.30), channel_id=1, source_target_pairs={{0,1},{1,0},{2,3},{3,2},{4,5},{5,4},{6,7},{7,6},{8,9},{9,8},{10,11... | collective-permute-start | bytes 294920 | tf_op jit(solution)/shard_map/ppermute | solution.py:285
  20.1 2.1 %collective-permute-done.2.far = f32[192,128]{1,0:T(8,128)S(1)} collective-permute-done((f32[192,128]{1,0:T(8,128)S(1)}, f32[192,128]{1,0:T(8,128)S(1)}, u32[]{:S(2)}, u32[]{:S(2)}) %collective-permute-start.2) | collective-permute-done | bytes 98336 | tf_op jit(solution)/shard_map/ppermute | solution.py:284
  22.2 0.0 collective-permute-done.3.near
  22.2 2.3 %second_kernel.1 = f32[320,128]{1,0:T(8,128)} custom-call(f32[12,24,128]{2,1,0:T(8,128)S(1)} %get-tuple-element.28.state, f32[192,128]{1,0:T(8,128)S(1)} %collective-permute-done.2.far, f32[192,128]{1,0:T(8,128)S(1)} %collective-permute-done.3.near, f32[12,64,128]{2,1,0:T(8,128)S(1)} %get-tuple-element.31.fwin, f32[320,128]{1,0:T(8,128)S(1)} %get-tuple-element.32.gain, ...), custom_call_target="tpu_custom_call" | custom-call | tf_op jit(solution)/shard_map/second_kernel/pallas_call | solution.py:269
  24.4 16.0 %all-to-all-start = ((f32[64,1,640]{2,1,0:T(1,128)}), f32[64,1,640]{2,1,0:T(1,128)S(1)}, u32[]{:S(2)}, u32[]{:S(2)}) async-start(f32[64,1,640]{2,1,0:T(1,128)} %bitcast.3), calls=%async_computation | async-start | bytes 327680 | tf_op jit(solution)/shard_map/all_to_all | solution.py:319
  40.4 13.7 %all-to-all-done = f32[64,1,640]{2,1,0:T(1,128)S(1)} async-done(((f32[64,1,640]{2,1,0:T(1,128)}), f32[64,1,640]{2,1,0:T(1,128)S(1)}, u32[]{:S(2)}, u32[]{:S(2)}) %all-to-all-start) | async-done | bytes 163872 | tf_op jit(solution)/shard_map/all_to_all | solution.py:319
  54.1 0.8 scan_kernel.1
  54.9 6.1 %all-to-all-start.1 = ((f32[64,1,640]{2,1,0:T(1,128)}), f32[64,1,640]{2,1,0:T(1,128)S(1)}, u32[]{:S(2)}, u32[]{:S(2)}) async-start(f32[64,1,640]{2,1,0:T(1,128)} %bitcast.5), calls=%async_computation.1 | async-start | bytes 327680 | tf_op jit(solution)/shard_map/all_to_all | solution.py:321
  61.0 2.9 %collective-permute-start.4 = (f32[12,24,128]{2,1,0:T(8,128)S(1)}, f32[12,24,128]{2,1,0:T(8,128)S(1)}, u32[]{:S(2)}, u32[]{:S(2)}) collective-permute-start(f32[12,24,128]{2,1,0:T(8,128)S(1)} %get-tuple-element.28.state), channel_id=1, source_target_pairs={{0,8},{1,9},{2,10},{3,11},{4,12},{5,13},{6,14},{7,15}} | collective-permute-start | bytes 442376 | tf_op jit(solution)/shard_map/ppermute | solution.py:316
  63.9 0.7 collective-permute-start.7
  64.6 1.7 %collective-permute-done.4.one = f32[12,24,128]{2,1,0:T(8,128)S(1)} collective-permute-done((f32[12,24,128]{2,1,0:T(8,128)S(1)}, f32[12,24,128]{2,1,0:T(8,128)S(1)}, u32[]{:S(2)}, u32[]{:S(2)}) %collective-permute-start.4) | collective-permute-done | bytes 147488 | tf_op jit(solution)/shard_map/ppermute | solution.py:316
  66.3 8.3 %all-to-all-done.1 = f32[64,1,640]{2,1,0:T(1,128)S(1)} async-done(((f32[64,1,640]{2,1,0:T(1,128)}), f32[64,1,640]{2,1,0:T(1,128)S(1)}, u32[]{:S(2)}, u32[]{:S(2)}) %all-to-all-start.1) | async-done | bytes 163872 | tf_op jit(solution)/shard_map/all_to_all | solution.py:321
  74.6 5.7 %collective-permute-start.5 = (f32[144,128]{1,0:T(8,128)S(1)}, f32[144,128]{1,0:T(8,128)S(1)}, u32[]{:S(2)}, u32[]{:S(2)}) collective-permute-start(f32[144,128]{1,0:T(8,128)S(1)} %get-tuple-element.34), channel_id=1, source_target_pairs={{1,2},{2,1},{3,4},{4,3},{5,6},{6,5},{9,10},{10,9},{11,12},{12,11},... | collective-permute-start | bytes 221192 | tf_op jit(solution)/shard_map/ppermute | solution.py:284
  80.3 1.9 %collective-permute-start.6 = (f32[144,128]{1,0:T(8,128)S(1)}, f32[144,128]{1,0:T(8,128)S(1)}, u32[]{:S(2)}, u32[]{:S(2)}) collective-permute-start(f32[144,128]{1,0:T(8,128)S(1)} %get-tuple-element.35), channel_id=1, source_target_pairs={{0,1},{1,0},{2,3},{3,2},{4,5},{5,4},{6,7},{7,6},{8,9},{9,8},{10,11... | collective-permute-start | bytes 221192 | tf_op jit(solution)/shard_map/ppermute | solution.py:285
  82.2 0.0 collective-permute-done.7.shifted
  82.2 0.1 collective-permute-done.5.far
  82.3 1.1 %collective-permute-done.6.near = f32[144,128]{1,0:T(8,128)S(1)} collective-permute-done((f32[144,128]{1,0:T(8,128)S(1)}, f32[144,128]{1,0:T(8,128)S(1)}, u32[]{:S(2)}, u32[]{:S(2)}) %collective-permute-start.6) | collective-permute-done | bytes 73760 | tf_op jit(solution)/shard_map/ppermute | solution.py:285
  83.5 2.2 %last_kernel.1 = (f32[1152,128]{1,0:T(8,128)}, f32[288,128]{1,0:T(8,128)}) custom-call(f32[12,24,128]{2,1,0:T(8,128)S(1)} %get-tuple-element.33.state, f32[144,128]{1,0:T(8,128)S(1)} %collective-permute-done.5.far, f32[144,128]{1,0:T(8,128)S(1)} %collective-permute-done.6.near, f32[12,64,128]{2,1,0:T(8,128)S(1)} %get-tuple-element.31.fwin, ...), custom_call_target="tpu_custom_call" | custom-call | tf_op jit(solution)/shard_map/last_kernel/pallas_call | solution.py:269
  (3 shorter events, 0.1 us)
Async XLA Ops:
  0.6 11.8 %copy-start.1 = (f32[12,6,512]{2,1,0:T(8,128)S(1)}, f32[12,6,512]{2,1,0:T(8,128)}, u32[]{:S(2)}) copy-start(f32[12,6,512]{2,1,0:T(8,128)} %raw.1) | copy-start | bytes 442372
  0.6 11.8 %copy-start.3 = (s32[12,12]{1,0:T(8,128)S(1)}, s32[12,12]{1,0:T(8,128)}, u32[]{:S(2)}) copy-start(s32[12,12]{1,0:T(8,128)} %cd.1) | copy-start | bytes 1732
  0.7 11.8 %copy-start.4 = (f32[8]{0:T(128)S(1)}, f32[8]{0:T(128)}, u32[]{:S(2)}) copy-start(f32[8]{0:T(128)} %lv.1) | copy-start | bytes 100
  0.7 11.8 %copy-start.5 = (f32[4]{0:T(128)S(1)}, f32[4]{0:T(128)}, u32[]{:S(2)}) copy-start(f32[4]{0:T(128)} %st.1) | copy-start | bytes 52
  0.7 11.8 %copy-start.6 = (s32[12]{0:T(128)S(1)}, s32[12]{0:T(128)}, u32[]{:S(2)}) copy-start(s32[12]{0:T(128)} %kl.1) | copy-start | bytes 148
  2.8 10.8 %copy-start = (f32[12,24,128]{2,1,0:T(8,128)S(1)}, f32[12,24,128]{2,1,0:T(8,128)}, u32[]{:S(2)}) copy-start(f32[12,24,128]{2,1,0:T(8,128)} %get-tuple-element.20.own) | copy-start | bytes 442372
  2.8 10.5 %collective-permute-start = (f32[336,128]{1,0:T(8,128)}, f32[336,128]{1,0:T(8,128)S(1)}, u32[]{:S(2)}, u32[]{:S(2)}) collective-permute-start(f32[336,128]{1,0:T(8,128)} %get-tuple-element.22), channel_id=1, source_target_pairs={{1,2},{2,1},{3,4},{4,3},{5,6},{6,5},{9,10},{10,9},{11,12},{12,11},... | collective-permute-start | bytes 516104 | tf_op jit(solution)/shard_map/ppermute | solution.py:284
  7.6 6.1 %collective-permute-start.1 = (f32[336,128]{1,0:T(8,128)}, f32[336,128]{1,0:T(8,128)S(1)}, u32[]{:S(2)}, u32[]{:S(2)}) collective-permute-start(f32[336,128]{1,0:T(8,128)} %get-tuple-element.23), channel_id=1, source_target_pairs={{0,1},{1,0},{2,3},{3,2},{4,5},{5,4},{6,7},{7,6},{8,9},{9,8},{10,11... | collective-permute-start | bytes 516104 | tf_op jit(solution)/shard_map/ppermute | solution.py:285
  13.7 0.9 %copy-start.2 = (f32[12,24,128]{2,1,0:T(8,128)S(1)}, f32[12,24,128]{2,1,0:T(8,128)}, u32[]{:S(2)}) copy-start(f32[12,24,128]{2,1,0:T(8,128)} %get-tuple-element.21.force) | copy-start | bytes 442372
  16.2 5.9 %collective-permute-start.2 = (f32[192,128]{1,0:T(8,128)S(1)}, f32[192,128]{1,0:T(8,128)S(1)}, u32[]{:S(2)}, u32[]{:S(2)}) collective-permute-start(f32[192,128]{1,0:T(8,128)S(1)} %get-tuple-element.29), channel_id=1, source_target_pairs={{1,2},{2,1},{3,4},{4,3},{5,6},{6,5},{9,10},{10,9},{11,12},{12,11},... | collective-permute-start | bytes 294920 | tf_op jit(solution)/shard_map/ppermute | solution.py:284
  18.2 4.0 %collective-permute-start.3 = (f32[192,128]{1,0:T(8,128)S(1)}, f32[192,128]{1,0:T(8,128)S(1)}, u32[]{:S(2)}, u32[]{:S(2)}) collective-permute-start(f32[192,128]{1,0:T(8,128)S(1)} %get-tuple-element.30), channel_id=1, source_target_pairs={{0,1},{1,0},{2,3},{3,2},{4,5},{5,4},{6,7},{7,6},{8,9},{9,8},{10,11... | collective-permute-start | bytes 294920 | tf_op jit(solution)/shard_map/ppermute | solution.py:285
  24.4 29.7 %all-to-all-start = ((f32[64,1,640]{2,1,0:T(1,128)}), f32[64,1,640]{2,1,0:T(1,128)S(1)}, u32[]{:S(2)}, u32[]{:S(2)}) async-start(f32[64,1,640]{2,1,0:T(1,128)} %bitcast.3), calls=%async_computation | async-start | bytes 327680 | tf_op jit(solution)/shard_map/all_to_all | solution.py:319
  54.9 19.7 %all-to-all-start.1 = ((f32[64,1,640]{2,1,0:T(1,128)}), f32[64,1,640]{2,1,0:T(1,128)S(1)}, u32[]{:S(2)}, u32[]{:S(2)}) async-start(f32[64,1,640]{2,1,0:T(1,128)} %bitcast.5), calls=%async_computation.1 | async-start | bytes 327680 | tf_op jit(solution)/shard_map/all_to_all | solution.py:321
  61.0 5.3 %collective-permute-start.4 = (f32[12,24,128]{2,1,0:T(8,128)S(1)}, f32[12,24,128]{2,1,0:T(8,128)S(1)}, u32[]{:S(2)}, u32[]{:S(2)}) collective-permute-start(f32[12,24,128]{2,1,0:T(8,128)S(1)} %get-tuple-element.28.state), channel_id=1, source_target_pairs={{0,8},{1,9},{2,10},{3,11},{4,12},{5,13},{6,14},{7,15}} | collective-permute-start | bytes 442376 | tf_op jit(solution)/shard_map/ppermute | solution.py:316
  63.9 18.3 %collective-permute-start.7 = (f32[12,24,128]{2,1,0:T(8,128)S(1)}, f32[12,24,128]{2,1,0:T(8,128)S(1)}, u32[]{:S(2)}, u32[]{:S(2)}) collective-permute-start(f32[12,24,128]{2,1,0:T(8,128)S(1)} %get-tuple-element.28.state), channel_id=1, source_target_pairs={{8,16},{16,24},{24,32},{32,40},{40,48},{48,56},{56,64},{64,72},{72... | collective-permute-start | bytes 442376 | tf_op jit(solution)/shard_map/ppermute | solution.py:317
  74.6 7.7 %collective-permute-start.5 = (f32[144,128]{1,0:T(8,128)S(1)}, f32[144,128]{1,0:T(8,128)S(1)}, u32[]{:S(2)}, u32[]{:S(2)}) collective-permute-start(f32[144,128]{1,0:T(8,128)S(1)} %get-tuple-element.34), channel_id=1, source_target_pairs={{1,2},{2,1},{3,4},{4,3},{5,6},{6,5},{9,10},{10,9},{11,12},{12,11},... | collective-permute-start | bytes 221192 | tf_op jit(solution)/shard_map/ppermute | solution.py:284
  80.3 3.2 %collective-permute-start.6 = (f32[144,128]{1,0:T(8,128)S(1)}, f32[144,128]{1,0:T(8,128)S(1)}, u32[]{:S(2)}, u32[]{:S(2)}) collective-permute-start(f32[144,128]{1,0:T(8,128)S(1)} %get-tuple-element.35), channel_id=1, source_target_pairs={{0,1},{1,0},{2,3},{3,2},{4,5},{5,4},{6,7},{7,6},{8,9},{9,8},{10,11... | collective-permute-start | bytes 221192 | tf_op jit(solution)/shard_map/ppermute | solution.py:285

commit v3 on v2

--- a/solution.py
+++ b/solution.py
@@ -20,7 +20,8 @@
 THREE = 3 * ROWS
 WIN = 64
 BASE = 5 * ROWS
-PIECE = 5
+GROUP = 8
+PIECE = 40
 VMEM = pl.BlockSpec(memory_space=pltpu.VMEM)
 SMEM = pl.BlockSpec(memory_space=pltpu.SMEM)
 HBM = pl.BlockSpec(memory_space=pl.ANY)
@@ -66,39 +67,49 @@
         put(far, BASE + OWN)
 
 
-def pack(src, row, count, start):
+def pack(src, row, count, start, base=0):
     def into(dst):
         for c in range(C):
-            dst[start + c * count : start + (c + 1) * count, :] = src[c, row : row + count, :]
+            dst[start + c * count : start + (c + 1) * count, :] = src[base + c, row : row + count, :]
 
     return into
 
 
-def prep_kernel(guess, forcing, own, force, near, far, raw, fraw, sems):
+def take_guess(raw, both):
+    for c in range(C):
+        both[c] = raw[pl.ds(c * OWN * SLICES, OWN, stride=SLICES), :]
+
+
+def take_forcing(raw, both):
+    for c in range(C):
+        for r in range(ROWS):
+            both[C + c, pl.ds(r, PLANES, stride=ROWS), :] = raw[c, :, 128 * r : 128 * r + 128] * 0.1
+
+
+def prep_kernel(guess, forcing, near, far, both, raw, fraw, sems):
     one = pltpu.make_async_copy(forcing, fraw, sems.at[0])
     two = pltpu.make_async_copy(guess, raw, sems.at[1])
     one.start()
     two.start()
     one.wait()
-    for c in range(C):
-        for r in range(ROWS):
-            force[c, pl.ds(r, PLANES, stride=ROWS), :] = fraw[c, :, 128 * r : 128 * r + 128] * 0.1
+    take_forcing(fraw, both)
     two.wait()
-    for c in range(C):
-        own[c] = raw[pl.ds(c * OWN * SLICES, OWN, stride=SLICES), :]
+    take_guess(raw, both)
 
     def first(dst):
-        pack(own, 0, HALO, 0)(dst)
-        pack(force, 0, THREE, C * HALO)(dst)
+        pack(both, 0, HALO, 0)(dst)
+        pack(both, 0, THREE, C * HALO, C)(dst)
 
     def last(dst):
-        pack(own, OWN - HALO, HALO, 0)(dst)
-        pack(force, OWN - THREE, THREE, C * HALO)(dst)
+        pack(both, OWN - HALO, HALO, 0)(dst)
+        pack(both, OWN - THREE, THREE, C * HALO, C)(dst)
 
     put_sends(first, last, near, far)
 
 
-def setup_kernel(raw, lv, cd, st, kl, gain_out, kv, wup, wfix, mask):
+def setup_kernel(guess, forcing, raw, lv, cd, st, kl, both, gain_out, kv, wup, wfix, mask):
+    take_guess(guess, both)
+    take_forcing(forcing, both)
     for c in range(C):
         for r in range(ROWS):
             gain_out[pl.ds(c * OWN + r, PLANES, stride=ROWS), :] = raw[c, :, 128 * r : 128 * r + 128]
@@ -184,12 +195,12 @@
 FOUR = ((1, 3), (1, 3), (2, 2), (2, 2))
 
 
-def first_kernel(own, force, far, near, kv, wup, wfix, mask, state, send_near, send_far, fwin, a, b):
+def first_kernel(both, far, near, kv, wup, wfix, mask, state, send_near, send_far, fwin, a, b):
     clear_edges(a)
     clear_edges(b)
     clear_edges(fwin)
-    a[:, BASE : BASE + OWN, :] = own[...]
-    fwin[:, BASE : BASE + OWN, :] = force[...]
+    a[:, BASE : BASE + OWN, :] = both[:C]
+    fwin[:, BASE : BASE + OWN, :] = both[C:]
     put_halo(a, near, far, HALO, 0)
     put_halo(fwin, near, far, THREE, C * HALO)
     steps((a, b), fwin, FOUR, (kv, wup, wfix, mask))
@@ -210,24 +221,53 @@
     out[C * OWN :, :] = jnp.zeros((out.shape[0] - C * OWN, 128), F32)
 
 
-def scan_kernel(pieces, gain, out):
-    count = pieces.shape[0] // PIECE
-    mine = gain[0]
-    running = pieces[0:PIECE, :]
-    out[0 : 2 * PIECE, :] = jnp.zeros((2 * PIECE, 128), F32)
-    for k in range(2, count):
-        out[k * PIECE : (k + 1) * PIECE, :] = running
-        if k + 1 < count:
-            m = k - 1
-            running = mine * running + pieces[m * PIECE : (m + 1) * PIECE, :]
-
-
-def gather_kernel(pieces, one, own, state, near, far):
+def my_gain(gain):
+    place = lax.axis_index("tm") % GROUP
+    return gain[pl.ds(pl.multiple_of(place * PIECE, 8), PIECE), :]
+
+
+def slot(i):
+    return slice(i * PIECE, (i + 1) * PIECE)
+
+
+def local_kernel(pieces, gain, sums, total, short):
+    mine = my_gain(gain)
+    running = pieces[slot(0), :]
+    sums[slot(0), :] = running
+    for i in range(1, GROUP):
+        running = mine * running + pieces[slot(i), :]
+        sums[slot(i), :] = running
+        if i == GROUP - 2:
+            short[...] = running
+    for i in range(GROUP):
+        total[slot(i), :] = running
+
+
+def prefix_kernel(totals, short, sums, gain, out):
+    group = lax.axis_index("tm") // GROUP
+    g1 = my_gain(gain)
+    g2 = g1 * g1
+    g4 = g2 * g2
+    g8 = g4 * g4
+    before = jnp.zeros((PIECE, 128), F32)
+    ahead = before
+    for g in range(GROUP - 1):
+        take = g < group
+        ahead = jnp.where(take, before, ahead)
+        before = jnp.where(take, g8 * before + totals[slot(g), :], before)
+    out[slot(0), :] = short[...] + (g4 * g2 * g1) * ahead
+    out[slot(1), :] = before
+    for i in range(2, GROUP):
+        before = g1 * before
+        out[slot(i), :] = sums[slot(i - 2), :] + before
+
+
+def gather_kernel(pieces, one, both, state, near, far):
     k = lax.axis_index("tm")
 
     @pl.when(k == 0)
     def _():
-        state[...] = own[...]
+        state[...] = both[:C]
 
     @pl.when(k == 1)
     def _():
@@ -286,41 +326,51 @@
     return near, far
 
 
+def swap(value, stride):
+    count = lax.axis_size("tm")
+    firsts = [i for i in range(count) if (i // stride) % GROUP == 0]
+    groups = [[i + stride * j for j in range(GROUP)] for i in firsts]
+    slots = value.reshape(GROUP, PIECE, 128)
+    return lax.all_to_all(slots, "tm", 0, 0, tiled=True, axis_index_groups=groups).reshape(value.shape)
+
+
 def shards(guess, forcing, coarse_gain, kernel_levels, kernel_code, settle_levels, settle_class):
     intervals = lax.axis_size("tm")
     rows = guess.reshape(SLICES, C, PLANES, ROWS, 128).transpose(1, 2, 3, 0, 4).reshape(C * OWN * SLICES, 128)
     slab = arr(C, OWN, 128)
     wide, four, three = (arr(C * n, 128) for n in (HALO + THREE, HALO, THREE))
-    pieces = arr(intervals * PIECE, 128)
-    own, force, near, far = call(
+    pieces = arr(GROUP * PIECE, 128)
+    near, far = call(
         prep_kernel,
         [rows, forcing],
-        [slab, slab, wide, wide],
-        [pltpu.VMEM(rows.shape, F32), pltpu.VMEM(forcing.shape, F32), pltpu.SemaphoreType.DMA((2,))],
+        [wide, wide],
+        [pltpu.VMEM((2 * C, OWN, 128), F32), pltpu.VMEM(rows.shape, F32), pltpu.VMEM(forcing.shape, F32), pltpu.SemaphoreType.DMA((2,))],
         [HBM] * 2,
         60,
     )
     near, far = exchange(near, far)
     small = (kernel_levels, kernel_code, settle_levels, settle_class)
-    gain, *coefs = call(
+    both, gain, *coefs = call(
         setup_kernel,
-        [coarse_gain, *small],
-        [pieces, arr(C * C, 8, 128), arr(C, 8, 128), arr(3, 8, 128), arr(WIN // 8, 8, 128)],
-        place=[VMEM] + [SMEM] * len(small),
-    )
-    mine = lax.dynamic_slice_in_dim(gain.reshape(intervals, PIECE, 128), lax.axis_index("tm"), 1, axis=0)
+        [rows, forcing, coarse_gain, *small],
+        [arr(2 * C, OWN, 128), pieces, arr(C * C, 8, 128), arr(C, 8, 128), arr(3, 8, 128), arr(WIN // 8, 8, 128)],
+        place=[VMEM] * 3 + [SMEM] * len(small),
+    )
     state, near, far, fwin = call(
-        first_kernel, [own, force, far, near, *coefs], [slab, four, four, arr(C, WIN, 128)], WORK
+        first_kernel, [both, far, near, *coefs], [slab, four, four, arr(C, WIN, 128)], WORK
     )
     near, far = exchange(near, far)
     one = lax.ppermute(state, "tm", [(0, 1)])
     shifted = lax.ppermute(state, "tm", [(i, i + 1) for i in range(1, intervals - 1)])
     (element,) = call(second_kernel, [state, far, near, fwin, gain, *coefs], [pieces], WORK)
-    spread = lax.all_to_all(element.reshape(intervals, PIECE * 128), "tm", 0, 0, tiled=True)
-    (sums,) = call(scan_kernel, [spread.reshape(intervals * PIECE, 128), mine], [pieces])
-    back = lax.all_to_all(sums.reshape(intervals, PIECE * 128), "tm", 0, 0, tiled=True)
+    spread = swap(element, 1)
+    sums, totals, short = call(local_kernel, [spread, gain], [pieces, pieces, arr(PIECE, 128)])
+    totals = swap(totals, GROUP)
+    short = lax.ppermute(short, "tm", [(i, i + GROUP) for i in range(intervals - GROUP)])
+    (back,) = call(prefix_kernel, [totals, short, sums, gain], [pieces])
+    back = swap(back, 1)
     state, near, far = call(
-        gather_kernel, [back.reshape(intervals * PIECE, 128), one, own], [slab, three, three]
+        gather_kernel, [back, one, both], [slab, three, three]
     )
     near, far = exchange(near, far)
     updated, corr = call(

time: 86.2 us -> 85.8 us (level)
  the two profiles are of different devices: /device:TPU:1 before, /device:TPU:48 now
where the time goes in v3:
time: 85.8 us; the launch traced here: 85.2 us
  starting transfers between devices  41.5 us (48%)
  waiting for transfers between devices  18.6 us (22%)
  blocking collectives  12.7 us (15%)
  Pallas kernels  9.82 us (11%)
  local copies, waits for them, and re-layouts  1.65 us (2%)
  between operations  0.86 us (1%)
    all_to_all x2, starting transfers between devices, swap(): lax.all_to_all(slots, 'tm', 0, 0, tiled=True, axis_index_groups=groups)  18.2 us
    all_to_all x1, blocking collectives, swap(): lax.all_to_all(slots, 'tm', 0, 0, tiled=True, axis_index_groups=groups)  12.7 us
    pallas_call x8, Pallas kernels, call(): pl.pallas_call(kernel, out_shape=outs, in_specs=place or [VMEM] * len(ins...  9.82 us
    ppermute x1, waiting for transfers between devices, shards(): lax.ppermute(short, 'tm', [(i, i + GROUP) for i in range(intervals - GROU...  8.31 us
    ppermute x3, starting transfers between devices, exchange(): far = lax.ppermute(far, 'space', outer)  8.11 us
    ppermute x1, waiting for transfers between devices, shards(): lax.ppermute(state, 'tm', [(i, i + 1) for i in range(1, intervals - 1)])  6.85 us
    ppermute x3, starting transfers between devices, exchange(): near = lax.ppermute(near, 'space', inner)  6.53 us
    ppermute x1, starting transfers between devices, shards(): lax.ppermute(short, 'tm', [(i, i + GROUP) for i in range(intervals - GROU...  4.26 us
  transfers between devices with their start and end apart: 11, of which 5 were waited for; matrix products, arithmetic and copies ran while one was open for 0% of the time, Pallas kernels for 1%

profile of v3, /device:TPU:48, one launch (start us, length us, event | category | flops | bytes accessed | tf_op | source)
XLA Modules:
  0.0 85.2 jit_solution(14055409348160682568)
XLA Ops:
  0.6 0.0 copy-start
  0.6 0.0 copy-start.1
  0.6 2.0 %prep_kernel.1 = (f32[336,128]{1,0:T(8,128)}, f32[336,128]{1,0:T(8,128)}) custom-call(f32[1152,128]{1,0:T(8,128)} %bitcast.17, f32[12,6,512]{2,1,0:T(8,128)} %forcing.3), custom_call_target="tpu_custom_call" | custom-call | tf_op jit(solution)/shard_map/prep_kernel/pallas_call | solution.py:309
  2.7 0.0 copy-start.4
  2.7 0.0 copy-start.5
  2.7 0.0 copy-start.6
  2.7 2.8 %collective-permute-start = (f32[336,128]{1,0:T(8,128)}, f32[336,128]{1,0:T(8,128)S(1)}, u32[]{:S(2)}, u32[]{:S(2)}) collective-permute-start(f32[336,128]{1,0:T(8,128)} %get-tuple-element.23), channel_id=1, source_target_pairs={{1,2},{2,1},{3,4},{4,3},{5,6},{6,5},{9,10},{10,9},{11,12},{12,11},... | collective-permute-start | bytes 516104 | tf_op jit(solution)/shard_map/ppermute | solution.py:324
  5.6 1.9 %collective-permute-start.1 = (f32[336,128]{1,0:T(8,128)}, f32[336,128]{1,0:T(8,128)S(1)}, u32[]{:S(2)}, u32[]{:S(2)}) collective-permute-start(f32[336,128]{1,0:T(8,128)} %get-tuple-element.24), channel_id=1, source_target_pairs={{0,1},{1,0},{2,3},{3,2},{4,5},{5,4},{6,7},{7,6},{8,9},{9,8},{10,11... | collective-permute-start | bytes 516104 | tf_op jit(solution)/shard_map/ppermute | solution.py:325
  7.5 0.0 copy-done
  7.5 0.0 copy-done.1
  7.5 0.0 copy-done.4
  7.5 0.0 copy-done.5
  7.5 0.0 copy-done.6
  7.5 0.0 copy-start.2
  7.5 0.9 %copy-done.2 = f32[12,6,512]{2,1,0:T(8,128)S(1)} copy-done((f32[12,6,512]{2,1,0:T(8,128)S(1)}, f32[12,6,512]{2,1,0:T(8,128)}, u32[]{:S(2)}) %copy-start.2) | copy-done | bytes 147480
  8.5 0.0 copy-start.3
  8.5 0.7 copy-done.3
  9.2 0.9 %setup_kernel.1 = (f32[24,24,128]{2,1,0:T(8,128)S(1)}, f32[320,128]{1,0:T(8,128)S(1)}, f32[144,8,128]{2,1,0:T(8,128)S(1)}, f32[12,8,128]{2,1,0:T(8,128)S(1)}, f3...) custom-call(f32[1152,128]{1,0:T(8,128)S(1)} %bitcast.18, f32[12,6,512]{2,1,0:T(8,128)S(1)} %copy-done.1, ...), custom_call_target="tpu_custom_call" | custom-call | tf_op jit(solution)/shard_map/setup_kernel/pallas_call | solution.py:309
  10.1 0.0 collective-permute-done.far
  10.1 0.0 collective-permute-done.1.near
  10.1 1.6 %first_kernel.1 = (f32[12,24,128]{2,1,0:T(8,128)S(1)}, f32[192,128]{1,0:T(8,128)S(1)}, f32[192,128]{1,0:T(8,128)S(1)}, f32[12,64,128]{2,1,0:T(8,128)S(1)}) custom-call(f32[24,24,128]{2,1,0:T(8,128)S(1)} %get-tuple-element.22.both, f32[336,128]{1,0:T(8,128)S(1)} %collective-permute-done.far, f32[336,128]{1,0:T(8,128)S(1)} %collective-permute-done.1.near, ...), custom_call_target="tpu_custom_call" | custom-call | tf_op jit(solution)/shard_map/first_kernel/pallas_call | solution.py:309
  11.7 3.4 %collective-permute-start.2 = (f32[192,128]{1,0:T(8,128)S(1)}, f32[192,128]{1,0:T(8,128)S(1)}, u32[]{:S(2)}, u32[]{:S(2)}) collective-permute-start(f32[192,128]{1,0:T(8,128)S(1)} %get-tuple-element.30), channel_id=1, source_target_pairs={{1,2},{2,1},{3,4},{4,3},{5,6},{6,5},{9,10},{10,9},{11,12},{12,11},... | collective-permute-start | bytes 294920 | tf_op jit(solution)/shard_map/ppermute | solution.py:324
  15.1 1.9 %collective-permute-start.3 = (f32[192,128]{1,0:T(8,128)S(1)}, f32[192,128]{1,0:T(8,128)S(1)}, u32[]{:S(2)}, u32[]{:S(2)}) collective-permute-start(f32[192,128]{1,0:T(8,128)S(1)} %get-tuple-element.31), channel_id=1, source_target_pairs={{0,1},{1,0},{2,3},{3,2},{4,5},{5,4},{6,7},{7,6},{8,9},{9,8},{10,11... | collective-permute-start | bytes 294920 | tf_op jit(solution)/shard_map/ppermute | solution.py:325
  17.0 0.6 collective-permute-done.2.far
  17.7 0.6 collective-permute-done.3.near
  18.3 1.6 %second_kernel.1 = f32[320,128]{1,0:T(8,128)S(1)} custom-call(f32[12,24,128]{2,1,0:T(8,128)S(1)} %get-tuple-element.29.state, f32[192,128]{1,0:T(8,128)S(1)} %collective-permute-done.2.far, f32[192,128]{1,0:T(8,128)S(1)} %collective-permute-done.3.near, f32[12,64,128]{2,1,0:T(8,128)S(1)} %get-tuple-element.32.fwin, f32[320,128]{1,0:T(8,128)S(1)} %get-tuple-element.33.gain, ...), custom_call_target="tpu_custom_call" | custom-call | tf_op jit(solution)/shard_map/second_kernel/pallas_call | solution.py:309
  19.9 12.7 %all_to_all.15 = f32[8,40,128]{2,1,0:T(8,128)S(1)} all-to-all(f32[8,40,128]{2,1,0:T(8,128)S(1)} %bitcast.22), channel_id=1, replica_groups={{0,8,16,24,32,40,48,56},{64,72,80,88,96,104,112,120},{128,136,144,152,1..., dimensions={0} | all-to-all | bytes 327680 | tf_op jit(solution)/shard_map/all_to_all | solution.py:334
  32.5 0.7 local_kernel.1
  33.2 14.8 %all-to-all-start.1 = ((f32[8,40,128]{2,1,0:T(8,128)}), f32[8,40,128]{2,1,0:T(8,128)S(1)}, u32[]{:S(2)}, u32[]{:S(2)}) async-start(f32[8,40,128]{2,1,0:T(8,128)} %bitcast.7), calls=%async_computation.1 | async-start | bytes 327680 | tf_op jit(solution)/shard_map/all_to_all | solution.py:334
  48.0 4.3 %collective-permute-start.4 = (f32[40,128]{1,0:T(8,128)S(1)}, f32[40,128]{1,0:T(8,128)S(1)}, u32[]{:S(2)}, u32[]{:S(2)}) collective-permute-start(f32[40,128]{1,0:T(8,128)S(1)} %get-tuple-element.35), channel_id=1, source_target_pairs={{0,64},{8,72},{16,80},{24,88},{32,96},{40,104},{48,112},{56,120},{... | collective-permute-start | bytes 61448 | tf_op jit(solution)/shard_map/ppermute | solution.py:369
  52.3 8.3 %collective-permute-done.4.short = f32[40,128]{1,0:T(8,128)S(1)} collective-permute-done((f32[40,128]{1,0:T(8,128)S(1)}, f32[40,128]{1,0:T(8,128)S(1)}, u32[]{:S(2)}, u32[]{:S(2)}) %collective-permute-start.4) | collective-permute-done | bytes 20512 | tf_op jit(solution)/shard_map/ppermute | solution.py:369
  60.6 0.0 all-to-all-done.1
  60.6 0.7 prefix_kernel.1
  61.3 3.4 %all-to-all-start.2 = ((f32[8,40,128]{2,1,0:T(8,128)}), f32[8,40,128]{2,1,0:T(8,128)S(1)}, u32[]{:S(2)}, u32[]{:S(2)}) async-start(f32[8,40,128]{2,1,0:T(8,128)} %bitcast.9), calls=%async_computation.2 | async-start | bytes 327680 | tf_op jit(solution)/shard_map/all_to_all | solution.py:334
  64.7 0.7 collective-permute-start.5
  65.4 3.8 %collective-permute-start.8 = (f32[12,24,128]{2,1,0:T(8,128)S(1)}, f32[12,24,128]{2,1,0:T(8,128)S(1)}, u32[]{:S(2)}, u32[]{:S(2)}) collective-permute-start(f32[12,24,128]{2,1,0:T(8,128)S(1)} %get-tuple-element.29.state), channel_id=1, source_target_pairs={{8,16},{16,24},{24,32},{32,40},{40,48},{48,56},{56,64},{64,72},{72... | collective-permute-start | bytes 442376 | tf_op jit(solution)/shard_map/ppermute | solution.py:364
  69.2 0.0 collective-permute-done.5.one
  69.2 2.2 %all-to-all-done.2 = f32[8,40,128]{2,1,0:T(8,128)S(1)} async-done(((f32[8,40,128]{2,1,0:T(8,128)}), f32[8,40,128]{2,1,0:T(8,128)S(1)}, u32[]{:S(2)}, u32[]{:S(2)}) %all-to-all-start.2) | async-done | bytes 163872 | tf_op jit(solution)/shard_map/all_to_all | solution.py:334
  71.4 1.9 %collective-permute-start.6 = (f32[144,128]{1,0:T(8,128)S(1)}, f32[144,128]{1,0:T(8,128)S(1)}, u32[]{:S(2)}, u32[]{:S(2)}) collective-permute-start(f32[144,128]{1,0:T(8,128)S(1)} %get-tuple-element.38), channel_id=1, source_target_pairs={{1,2},{2,1},{3,4},{4,3},{5,6},{6,5},{9,10},{10,9},{11,12},{12,11},... | collective-permute-start | bytes 221192 | tf_op jit(solution)/shard_map/ppermute | solution.py:324
  73.4 2.7 %collective-permute-start.7 = (f32[144,128]{1,0:T(8,128)S(1)}, f32[144,128]{1,0:T(8,128)S(1)}, u32[]{:S(2)}, u32[]{:S(2)}) collective-permute-start(f32[144,128]{1,0:T(8,128)S(1)} %get-tuple-element.39), channel_id=1, source_target_pairs={{0,1},{1,0},{2,3},{3,2},{4,5},{5,4},{6,7},{7,6},{8,9},{9,8},{10,11... | collective-permute-start | bytes 221192 | tf_op jit(solution)/shard_map/ppermute | solution.py:325
  76.1 6.9 %collective-permute-done.8.shifted = f32[12,24,128]{2,1,0:T(8,128)S(1)} collective-permute-done((f32[12,24,128]{2,1,0:T(8,128)S(1)}, f32[12,24,128]{2,1,0:T(8,128)S(1)}, u32[]{:S(2)}, u32[]{:S(2)}) %collective-permute-start.8) | collective-permute-done | bytes 147488 | tf_op jit(solution)/shard_map/ppermute | solution.py:364
  82.9 0.0 collective-permute-done.6.far
  82.9 0.0 collective-permute-done.7.near
  82.9 2.2 %last_kernel.1 = (f32[1152,128]{1,0:T(8,128)}, f32[288,128]{1,0:T(8,128)}) custom-call(f32[12,24,128]{2,1,0:T(8,128)S(1)} %get-tuple-element.37.state, f32[144,128]{1,0:T(8,128)S(1)} %collective-permute-done.6.far, f32[144,128]{1,0:T(8,128)S(1)} %collective-permute-done.7.near, f32[12,64,128]{2,1,0:T(8,128)S(1)} %get-tuple-element.32.fwin, ...), custom_call_target="tpu_custom_call" | custom-call | tf_op jit(solution)/shard_map/last_kernel/pallas_call | solution.py:309
  (1 shorter events, 0.0 us)
Async XLA Ops:
  0.6 6.9 %copy-start = (f32[4,12,6,512]{3,0,2,1:T(4,128)S(1)}, f32[4,12,6,512]{3,0,2,1:T(4,128)}, u32[]{:S(2)}) copy-start(f32[4,12,6,512]{3,0,2,1:T(4,128)} %param.7) | copy-start | bytes 1769476
  0.6 6.9 %copy-start.1 = (f32[12,6,512]{2,1,0:T(8,128)S(1)}, f32[12,6,512]{2,1,0:T(8,128)}, u32[]{:S(2)}) copy-start(f32[12,6,512]{2,1,0:T(8,128)} %forcing.3) | copy-start | bytes 442372
  2.7 4.8 %copy-start.4 = (f32[8]{0:T(128)S(1)}, f32[8]{0:T(128)}, u32[]{:S(2)}) copy-start(f32[8]{0:T(128)} %lv.1) | copy-start | bytes 100
  2.7 4.8 %copy-start.5 = (f32[4]{0:T(128)S(1)}, f32[4]{0:T(128)}, u32[]{:S(2)}) copy-start(f32[4]{0:T(128)} %st.1) | copy-start | bytes 52
  2.7 4.8 %copy-start.6 = (s32[12]{0:T(128)S(1)}, s32[12]{0:T(128)}, u32[]{:S(2)}) copy-start(s32[12]{0:T(128)} %kl.1) | copy-start | bytes 148
  2.7 7.4 %collective-permute-start = (f32[336,128]{1,0:T(8,128)}, f32[336,128]{1,0:T(8,128)S(1)}, u32[]{:S(2)}, u32[]{:S(2)}) collective-permute-start(f32[336,128]{1,0:T(8,128)} %get-tuple-element.23), channel_id=1, source_target_pairs={{1,2},{2,1},{3,4},{4,3},{5,6},{6,5},{9,10},{10,9},{11,12},{12,11},... | collective-permute-start | bytes 516104 | tf_op jit(solution)/shard_map/ppermute | solution.py:324
  5.6 4.5 %collective-permute-start.1 = (f32[336,128]{1,0:T(8,128)}, f32[336,128]{1,0:T(8,128)S(1)}, u32[]{:S(2)}, u32[]{:S(2)}) collective-permute-start(f32[336,128]{1,0:T(8,128)} %get-tuple-element.24), channel_id=1, source_target_pairs={{0,1},{1,0},{2,3},{3,2},{4,5},{5,4},{6,7},{7,6},{8,9},{9,8},{10,11... | collective-permute-start | bytes 516104 | tf_op jit(solution)/shard_map/ppermute | solution.py:325
  7.5 0.9 %copy-start.2 = (f32[12,6,512]{2,1,0:T(8,128)S(1)}, f32[12,6,512]{2,1,0:T(8,128)}, u32[]{:S(2)}) copy-start(f32[12,6,512]{2,1,0:T(8,128)} %raw.1) | copy-start | bytes 442372
  8.5 0.7 copy-start.3
  11.7 5.9 %collective-permute-start.2 = (f32[192,128]{1,0:T(8,128)S(1)}, f32[192,128]{1,0:T(8,128)S(1)}, u32[]{:S(2)}, u32[]{:S(2)}) collective-permute-start(f32[192,128]{1,0:T(8,128)S(1)} %get-tuple-element.30), channel_id=1, source_target_pairs={{1,2},{2,1},{3,4},{4,3},{5,6},{6,5},{9,10},{10,9},{11,12},{12,11},... | collective-permute-start | bytes 294920 | tf_op jit(solution)/shard_map/ppermute | solution.py:324
  15.1 3.2 %collective-permute-start.3 = (f32[192,128]{1,0:T(8,128)S(1)}, f32[192,128]{1,0:T(8,128)S(1)}, u32[]{:S(2)}, u32[]{:S(2)}) collective-permute-start(f32[192,128]{1,0:T(8,128)S(1)} %get-tuple-element.31), channel_id=1, source_target_pairs={{0,1},{1,0},{2,3},{3,2},{4,5},{5,4},{6,7},{7,6},{8,9},{9,8},{10,11... | collective-permute-start | bytes 294920 | tf_op jit(solution)/shard_map/ppermute | solution.py:325
  33.2 27.4 %all-to-all-start.1 = ((f32[8,40,128]{2,1,0:T(8,128)}), f32[8,40,128]{2,1,0:T(8,128)S(1)}, u32[]{:S(2)}, u32[]{:S(2)}) async-start(f32[8,40,128]{2,1,0:T(8,128)} %bitcast.7), calls=%async_computation.1 | async-start | bytes 327680 | tf_op jit(solution)/shard_map/all_to_all | solution.py:334
  48.0 12.6 %collective-permute-start.4 = (f32[40,128]{1,0:T(8,128)S(1)}, f32[40,128]{1,0:T(8,128)S(1)}, u32[]{:S(2)}, u32[]{:S(2)}) collective-permute-start(f32[40,128]{1,0:T(8,128)S(1)} %get-tuple-element.35), channel_id=1, source_target_pairs={{0,64},{8,72},{16,80},{24,88},{32,96},{40,104},{48,112},{56,120},{... | collective-permute-start | bytes 61448 | tf_op jit(solution)/shard_map/ppermute | solution.py:369
  61.3 10.1 %all-to-all-start.2 = ((f32[8,40,128]{2,1,0:T(8,128)}), f32[8,40,128]{2,1,0:T(8,128)S(1)}, u32[]{:S(2)}, u32[]{:S(2)}) async-start(f32[8,40,128]{2,1,0:T(8,128)} %bitcast.9), calls=%async_computation.2 | async-start | bytes 327680 | tf_op jit(solution)/shard_map/all_to_all | solution.py:334
  64.7 4.5 %collective-permute-start.5 = (f32[12,24,128]{2,1,0:T(8,128)S(1)}, f32[12,24,128]{2,1,0:T(8,128)S(1)}, u32[]{:S(2)}, u32[]{:S(2)}) collective-permute-start(f32[12,24,128]{2,1,0:T(8,128)S(1)} %get-tuple-element.29.state), channel_id=1, source_target_pairs={{0,8},{1,9},{2,10},{3,11},{4,12},{5,13},{6,14},{7,15}} | collective-permute-start | bytes 442376 | tf_op jit(solution)/shard_map/ppermute | solution.py:363
  65.4 17.5 %collective-permute-start.8 = (f32[12,24,128]{2,1,0:T(8,128)S(1)}, f32[12,24,128]{2,1,0:T(8,128)S(1)}, u32[]{:S(2)}, u32[]{:S(2)}) collective-permute-start(f32[12,24,128]{2,1,0:T(8,128)S(1)} %get-tuple-element.29.state), channel_id=1, source_target_pairs={{8,16},{16,24},{24,32},{32,40},{40,48},{48,56},{56,64},{64,72},{72... | collective-permute-start | bytes 442376 | tf_op jit(solution)/shard_map/ppermute | solution.py:364
  71.4 11.5 %collective-permute-start.6 = (f32[144,128]{1,0:T(8,128)S(1)}, f32[144,128]{1,0:T(8,128)S(1)}, u32[]{:S(2)}, u32[]{:S(2)}) collective-permute-start(f32[144,128]{1,0:T(8,128)S(1)} %get-tuple-element.38), channel_id=1, source_target_pairs={{1,2},{2,1},{3,4},{4,3},{5,6},{6,5},{9,10},{10,9},{11,12},{12,11},... | collective-permute-start | bytes 221192 | tf_op jit(solution)/shard_map/ppermute | solution.py:324
  73.4 9.6 %collective-permute-start.7 = (f32[144,128]{1,0:T(8,128)S(1)}, f32[144,128]{1,0:T(8,128)S(1)}, u32[]{:S(2)}, u32[]{:S(2)}) collective-permute-start(f32[144,128]{1,0:T(8,128)S(1)} %get-tuple-element.39), channel_id=1, source_target_pairs={{0,1},{1,0},{2,3},{3,2},{4,5},{5,4},{6,7},{7,6},{8,9},{9,8},{10,11... | collective-permute-start | bytes 221192 | tf_op jit(solution)/shard_map/ppermute | solution.py:325

commit v4 on v3

--- a/solution.py
+++ b/solution.py
@@ -9,6 +9,7 @@
 
 F32 = jnp.float32
 C = 12
+HALF = C // 2
 NY = 16
 NZ = 32
 PLANES = 6
@@ -67,53 +68,55 @@
         put(far, BASE + OWN)
 
 
-def pack(src, row, count, start, base=0):
+def pack(src, row, count, start):
     def into(dst):
         for c in range(C):
-            dst[start + c * count : start + (c + 1) * count, :] = src[base + c, row : row + count, :]
+            dst[start + c * count : start + (c + 1) * count, :] = src[c, row : row + count, :]
 
     return into
 
 
-def take_guess(raw, both):
+def take_guess(raw, own):
     for c in range(C):
-        both[c] = raw[pl.ds(c * OWN * SLICES, OWN, stride=SLICES), :]
-
-
-def take_forcing(raw, both):
+        own[c] = raw[pl.ds(c * OWN * SLICES, OWN, stride=SLICES), :]
+
+
+def take_forcing(raw, force):
     for c in range(C):
         for r in range(ROWS):
-            both[C + c, pl.ds(r, PLANES, stride=ROWS), :] = raw[c, :, 128 * r : 128 * r + 128] * 0.1
-
-
-def prep_kernel(guess, forcing, near, far, both, raw, fraw, sems):
+            force[c, pl.ds(r, PLANES, stride=ROWS), :] = raw[c, :, 128 * r : 128 * r + 128] * 0.1
+
+
+def prep_kernel(guess, forcing, near, far, own, force, raw, fraw, sems):
     one = pltpu.make_async_copy(forcing, fraw, sems.at[0])
     two = pltpu.make_async_copy(guess, raw, sems.at[1])
     one.start()
     two.start()
     one.wait()
-    take_forcing(fraw, both)
+    take_forcing(fraw, force)
     two.wait()
-    take_guess(raw, both)
+    take_guess(raw, own)
 
     def first(dst):
-        pack(both, 0, HALO, 0)(dst)
-        pack(both, 0, THREE, C * HALO, C)(dst)
+        pack(own, 0, HALO, 0)(dst)
+        pack(force, 0, THREE, C * HALO)(dst)
 
     def last(dst):
-        pack(both, OWN - HALO, HALO, 0)(dst)
-        pack(both, OWN - THREE, THREE, C * HALO, C)(dst)
+        pack(own, OWN - HALO, HALO, 0)(dst)
+        pack(force, OWN - THREE, THREE, C * HALO)(dst)
 
     put_sends(first, last, near, far)
 
 
-def setup_kernel(guess, forcing, raw, lv, cd, st, kl, both, gain_out, kv, wup, wfix, mask):
-    take_guess(guess, both)
-    take_forcing(forcing, both)
+def gain_kernel(raw, gain_out):
     for c in range(C):
         for r in range(ROWS):
             gain_out[pl.ds(c * OWN + r, PLANES, stride=ROWS), :] = raw[c, :, 128 * r : 128 * r + 128]
     gain_out[C * OWN :, :] = jnp.zeros((gain_out.shape[0] - C * OWN, 128), F32)
+
+
+def setup_kernel(forcing, lv, cd, st, kl, force, kv, wup, wfix, mask):
+    take_forcing(forcing, force)
     lane = lax.broadcasted_iota(jnp.int32, (8, 128), 1)
     row = lax.broadcasted_iota(jnp.int32, (8, 128), 0)
     z = lane % NZ
@@ -195,16 +198,19 @@
 FOUR = ((1, 3), (1, 3), (2, 2), (2, 2))
 
 
-def first_kernel(both, far, near, kv, wup, wfix, mask, state, send_near, send_far, fwin, a, b):
+def first_kernel(guess, force, far, near, kv, wup, wfix, mask, own, state, low, high, send_near, send_far, fwin, a, b):
     clear_edges(a)
     clear_edges(b)
     clear_edges(fwin)
-    a[:, BASE : BASE + OWN, :] = both[:C]
-    fwin[:, BASE : BASE + OWN, :] = both[C:]
+    take_guess(guess, own)
+    a[:, BASE : BASE + OWN, :] = own[...]
+    fwin[:, BASE : BASE + OWN, :] = force[...]
     put_halo(a, near, far, HALO, 0)
     put_halo(fwin, near, far, THREE, C * HALO)
     steps((a, b), fwin, FOUR, (kv, wup, wfix, mask))
     state[...] = a[:, BASE : BASE + OWN, :]
+    low[...] = a[:HALF, BASE : BASE + OWN, :]
+    high[...] = a[HALF:, BASE : BASE + OWN, :]
     put_sends(pack(state, 0, HALO, 0), pack(state, OWN - HALO, HALO, 0), send_near, send_far)
 
 
@@ -222,12 +228,12 @@
 
 
 def my_gain(gain):
-    place = lax.axis_index("tm") % GROUP
+    place = GROUP - 1 - lax.axis_index("tm") % GROUP
     return gain[pl.ds(pl.multiple_of(place * PIECE, 8), PIECE), :]
 
 
 def slot(i):
-    return slice(i * PIECE, (i + 1) * PIECE)
+    return slice((GROUP - 1 - i) * PIECE, (GROUP - i) * PIECE)
 
 
 def local_kernel(pieces, gain, sums, total, short):
@@ -243,7 +249,8 @@
         total[slot(i), :] = running
 
 
-def prefix_kernel(totals, short, sums, gain, out):
+def prefix_kernel(totals, cross, shifted, short, sums, gain, out):
+    del cross, shifted
     group = lax.axis_index("tm") // GROUP
     g1 = my_gain(gain)
     g2 = g1 * g1
@@ -262,12 +269,12 @@
         out[slot(i), :] = sums[slot(i - 2), :] + before
 
 
-def gather_kernel(pieces, one, both, state, near, far):
+def gather_kernel(pieces, one, own, state, near, far):
     k = lax.axis_index("tm")
 
     @pl.when(k == 0)
     def _():
-        state[...] = both[:C]
+        state[...] = own[...]
 
     @pl.when(k == 1)
     def _():
@@ -281,7 +288,7 @@
     put_sends(pack(state, 0, THREE, 0), pack(state, OWN - THREE, THREE, 0), near, far)
 
 
-def last_kernel(state, far, near, fwin, shifted, kv, wup, wfix, mask, out, corr, a, b):
+def last_kernel(state, far, near, fwin, shifted, cross, rest, kv, wup, wfix, mask, out, corr, a, b):
     clear_edges(a)
     clear_edges(b)
     a[:, BASE : BASE + OWN, :] = state[...]
@@ -299,7 +306,8 @@
         emit(dst, j + 1)
     late = lax.axis_index("tm") >= 2
     for c in range(C):
-        corr[c * OWN : (c + 1) * OWN, :] = jnp.where(late, state[c] - shifted[c], 0.0)
+        over = cross[c] if c < HALF else rest[c - HALF]
+        corr[c * OWN : (c + 1) * OWN, :] = jnp.where(late, state[c] - (shifted[c] + over), 0.0)
 
 
 WORK = [pltpu.VMEM((C, WIN, 128), F32), pltpu.VMEM((C, WIN, 128), F32)]
@@ -329,7 +337,7 @@
 def swap(value, stride):
     count = lax.axis_size("tm")
     firsts = [i for i in range(count) if (i // stride) % GROUP == 0]
-    groups = [[i + stride * j for j in range(GROUP)] for i in firsts]
+    groups = [[i + stride * j for j in reversed(range(GROUP))] for i in firsts]
     slots = value.reshape(GROUP, PIECE, 128)
     return lax.all_to_all(slots, "tm", 0, 0, tiled=True, axis_index_groups=groups).reshape(value.shape)
 
@@ -344,38 +352,45 @@
         prep_kernel,
         [rows, forcing],
         [wide, wide],
-        [pltpu.VMEM((2 * C, OWN, 128), F32), pltpu.VMEM(rows.shape, F32), pltpu.VMEM(forcing.shape, F32), pltpu.SemaphoreType.DMA((2,))],
+        [pltpu.VMEM(slab.shape, F32), pltpu.VMEM(slab.shape, F32), pltpu.VMEM(rows.shape, F32), pltpu.VMEM(forcing.shape, F32), pltpu.SemaphoreType.DMA((2,))],
         [HBM] * 2,
         60,
     )
     near, far = exchange(near, far)
     small = (kernel_levels, kernel_code, settle_levels, settle_class)
-    both, gain, *coefs = call(
+    force, *coefs = call(
         setup_kernel,
-        [rows, forcing, coarse_gain, *small],
-        [arr(2 * C, OWN, 128), pieces, arr(C * C, 8, 128), arr(C, 8, 128), arr(3, 8, 128), arr(WIN // 8, 8, 128)],
-        place=[VMEM] * 3 + [SMEM] * len(small),
-    )
-    state, near, far, fwin = call(
-        first_kernel, [both, far, near, *coefs], [slab, four, four, arr(C, WIN, 128)], WORK
+        [forcing, *small],
+        [slab, arr(C * C, 8, 128), arr(C, 8, 128), arr(3, 8, 128), arr(WIN // 8, 8, 128)],
+        place=[VMEM] + [SMEM] * len(small),
+    )
+    (gain,) = call(gain_kernel, [coarse_gain], [pieces])
+    half = arr(HALF, OWN, 128)
+    own, state, low, high, near, far, fwin = call(
+        first_kernel,
+        [rows, force, far, near, *coefs],
+        [slab, slab, half, half, four, four, arr(C, WIN, 128)],
+        WORK,
     )
     near, far = exchange(near, far)
-    one = lax.ppermute(state, "tm", [(0, 1)])
-    shifted = lax.ppermute(state, "tm", [(i, i + 1) for i in range(1, intervals - 1)])
+    middle = intervals // 2
+    shifted = lax.ppermute(state, "tm", [(i, i + 1) for i in range(intervals - 1) if i + 1 != middle])
+    cross = lax.ppermute(low, "tm", [(middle - 1, middle)])
+    rest = lax.ppermute(high, "tm", [(middle - 1, middle)])
     (element,) = call(second_kernel, [state, far, near, fwin, gain, *coefs], [pieces], WORK)
     spread = swap(element, 1)
     sums, totals, short = call(local_kernel, [spread, gain], [pieces, pieces, arr(PIECE, 128)])
     totals = swap(totals, GROUP)
     short = lax.ppermute(short, "tm", [(i, i + GROUP) for i in range(intervals - GROUP)])
-    (back,) = call(prefix_kernel, [totals, short, sums, gain], [pieces])
+    (back,) = call(prefix_kernel, [totals, cross, shifted, short, sums, gain], [pieces])
     back = swap(back, 1)
     state, near, far = call(
-        gather_kernel, [back, one, both], [slab, three, three]
+        gather_kernel, [back, shifted, own], [slab, three, three]
     )
     near, far = exchange(near, far)
     updated, corr = call(
         last_kernel,
-        [state, far, near, fwin, shifted, *coefs],
+        [state, far, near, fwin, shifted, cross, rest, *coefs],
         [arr(C * OWN * SLICES, 128), arr(C * OWN, 128)],
         WORK,
     )

time: 85.8 us -> 84.5 us (0.985)
  the two profiles are of different devices: /device:TPU:48 before, /device:TPU:56 now
where the time goes in v4:
time: 84.5 us; the launch traced here: 83.9 us
  starting transfers between devices  40.8 us (48%)
  waiting for transfers between devices  20.5 us (24%)
  blocking collectives  11.1 us (13%)
  Pallas kernels  9.85 us (12%)
  between operations  0.85 us (1%)
    all_to_all x2, starting transfers between devices, swap(): lax.all_to_all(slots, 'tm', 0, 0, tiled=True, axis_index_groups=groups)  18.8 us
    all_to_all x1, blocking collectives, swap(): lax.all_to_all(slots, 'tm', 0, 0, tiled=True, axis_index_groups=groups)  11.1 us
    pallas_call x9, Pallas kernels, call(): pl.pallas_call(kernel, out_shape=outs, in_specs=place or [VMEM] * len(ins...  9.85 us
    ppermute x1, waiting for transfers between devices, shards(): cross = lax.ppermute(low, 'tm', [(middle - 1, middle)])  9.43 us
    ppermute x3, starting transfers between devices, exchange(): far = lax.ppermute(far, 'space', outer)  7.73 us
    ppermute x1, waiting for transfers between devices, shards(): rest = lax.ppermute(high, 'tm', [(middle - 1, middle)])  6.42 us
    ppermute x3, starting transfers between devices, exchange(): near = lax.ppermute(near, 'space', inner)  5.76 us
    ppermute x1, starting transfers between devices, shards(): lax.ppermute(short, 'tm', [(i, i + GROUP) for i in range(intervals - GROU...  3.64 us
  transfers between devices with their start and end apart: 12, of which 6 were waited for; matrix products, arithmetic and copies ran while one was open for 0% of the time, Pallas kernels for 1%

profile of v4, /device:TPU:56, one launch (start us, length us, event | category | flops | bytes accessed | tf_op | source)
XLA Modules:
  0.0 83.9 jit_solution(3417251148580707009)
XLA Ops:
  0.6 0.0 copy-start
  0.6 0.0 copy-start.1
  0.6 2.0 %prep_kernel.1 = (f32[336,128]{1,0:T(8,128)}, f32[336,128]{1,0:T(8,128)}) custom-call(f32[1152,128]{1,0:T(8,128)} %bitcast.17, f32[12,6,512]{2,1,0:T(8,128)} %forcing.3), custom_call_target="tpu_custom_call" | custom-call | tf_op jit(solution)/shard_map/prep_kernel/pallas_call | solution.py:317
  2.7 0.0 copy-start.4
  2.7 0.0 copy-start.5
  2.7 0.0 copy-start.6
  2.7 2.8 %collective-permute-start = (f32[336,128]{1,0:T(8,128)}, f32[336,128]{1,0:T(8,128)S(1)}, u32[]{:S(2)}, u32[]{:S(2)}) collective-permute-start(f32[336,128]{1,0:T(8,128)} %get-tuple-element.25), channel_id=1, source_target_pairs={{1,2},{2,1},{3,4},{4,3},{5,6},{6,5},{9,10},{10,9},{11,12},{12,11},... | collective-permute-start | bytes 516104 | tf_op jit(solution)/shard_map/ppermute | solution.py:332
  5.6 1.9 %collective-permute-start.1 = (f32[336,128]{1,0:T(8,128)}, f32[336,128]{1,0:T(8,128)S(1)}, u32[]{:S(2)}, u32[]{:S(2)}) collective-permute-start(f32[336,128]{1,0:T(8,128)} %get-tuple-element.26), channel_id=1, source_target_pairs={{0,1},{1,0},{2,3},{3,2},{4,5},{5,4},{6,7},{7,6},{8,9},{9,8},{10,11... | collective-permute-start | bytes 516104 | tf_op jit(solution)/shard_map/ppermute | solution.py:333
  7.5 0.0 copy-done.1
  7.5 0.0 copy-done.4
  7.5 0.0 copy-done.5
  7.5 0.0 copy-done.6
  7.5 0.0 copy-start.3
  7.5 0.7 copy-done.3
  8.2 0.9 %setup_kernel.1 = (f32[12,24,128]{2,1,0:T(8,128)S(1)}, f32[144,8,128]{2,1,0:T(8,128)S(1)}, f32[12,8,128]{2,1,0:T(8,128)S(1)}, f32[3,8,128]{2,1,0:T(8,128)S(1)}, f32[8,8,128]{2,1,0:T(8,128)S(1)}) custom-call(f32[12,6,512]{2,1,0:T(8,128)S(1)} %copy-done.1, f32[8]{0:T(128)S(1)} %copy-done.4, s32[12,12]{1,0:T(8,128)S(1)} %copy-done.3, f32[4]{0:T(128)S(1)} %copy-done.5, ...), custom_call_target="tpu_custom_call" | custom-call | tf_op jit(solution)/shard_map/setup_kernel/pallas_call | solution.py:317
  9.1 0.7 collective-permute-done.far
  9.8 0.0 collective-permute-done.1.near
  9.8 0.0 copy-done
  9.8 0.0 copy-start.2
  9.8 1.6 %first_kernel.1 = (f32[12,24,128]{2,1,0:T(8,128)S(1)}, f32[12,24,128]{2,1,0:T(8,128)S(1)}, f32[6,24,128]{2,1,0:T(8,128)S(1)}, f32[6,24,128]{2,1,0:T(8,128)S(1)},...) custom-call(f32[1152,128]{1,0:T(8,128)S(1)} %bitcast.18, ...), custom_call_target="tpu_custom_call" | custom-call | tf_op jit(solution)/shard_map/first_kernel/pallas_call | solution.py:317
  11.4 3.0 %collective-permute-start.2 = (f32[192,128]{1,0:T(8,128)S(1)}, f32[192,128]{1,0:T(8,128)S(1)}, u32[]{:S(2)}, u32[]{:S(2)}) collective-permute-start(f32[192,128]{1,0:T(8,128)S(1)} %get-tuple-element.32), channel_id=1, source_target_pairs={{1,2},{2,1},{3,4},{4,3},{5,6},{6,5},{9,10},{10,9},{11,12},{12,11},... | collective-permute-start | bytes 294920 | tf_op jit(solution)/shard_map/ppermute | solution.py:332
  14.4 1.9 %collective-permute-start.3 = (f32[192,128]{1,0:T(8,128)S(1)}, f32[192,128]{1,0:T(8,128)S(1)}, u32[]{:S(2)}, u32[]{:S(2)}) collective-permute-start(f32[192,128]{1,0:T(8,128)S(1)} %get-tuple-element.33), channel_id=1, source_target_pairs={{0,1},{1,0},{2,3},{3,2},{4,5},{5,4},{6,7},{7,6},{8,9},{9,8},{10,11... | collective-permute-start | bytes 294920 | tf_op jit(solution)/shard_map/ppermute | solution.py:333
  16.4 0.0 copy-done.2
  16.4 1.0 %collective-permute-done.2.far = f32[192,128]{1,0:T(8,128)S(1)} collective-permute-done((f32[192,128]{1,0:T(8,128)S(1)}, f32[192,128]{1,0:T(8,128)S(1)}, u32[]{:S(2)}, u32[]{:S(2)}) %collective-permute-start.2) | collective-permute-done | bytes 98336 | tf_op jit(solution)/shard_map/ppermute | solution.py:332
  17.4 0.3 collective-permute-done.3.near
  17.6 1.6 %second_kernel.1 = f32[320,128]{1,0:T(8,128)S(1)} custom-call(f32[12,24,128]{2,1,0:T(8,128)S(1)} %get-tuple-element.31.state, f32[192,128]{1,0:T(8,128)S(1)} %collective-permute-done.2.far, f32[192,128]{1,0:T(8,128)S(1)} %collective-permute-done.3.near, f32[12,64,128]{2,1,0:T(8,128)S(1)} %get-tuple-element.34.fwin, f32[320,128]{1,0:T(8,128)S(1)} %gain_kernel.1.gain, ...), custom_call_target="tpu_custom_call" | custom-call | tf_op jit(solution)/shard_map/second_kernel/pallas_call | solution.py:317
  19.2 11.1 %all_to_all.15 = f32[8,40,128]{2,1,0:T(8,128)S(1)} all-to-all(f32[8,40,128]{2,1,0:T(8,128)S(1)} %bitcast.22), channel_id=1, replica_groups={{56,48,40,32,24,16,8,0},{120,112,104,96,88,80,72,64},{184,176,168,160,1..., dimensions={0} | all-to-all | bytes 327680 | tf_op jit(solution)/shard_map/all_to_all | solution.py:342
  30.3 0.7 local_kernel.1
  31.0 12.0 %all-to-all-start.1 = ((f32[8,40,128]{2,1,0:T(8,128)}), f32[8,40,128]{2,1,0:T(8,128)S(1)}, u32[]{:S(2)}, u32[]{:S(2)}) async-start(f32[8,40,128]{2,1,0:T(8,128)} %bitcast.7), calls=%async_computation.1 | async-start | bytes 327680 | tf_op jit(solution)/shard_map/all_to_all | solution.py:342
  43.0 2.2 %collective-permute-start.5 = (f32[12,24,128]{2,1,0:T(8,128)S(1)}, f32[12,24,128]{2,1,0:T(8,128)S(1)}, u32[]{:S(2)}, u32[]{:S(2)}) collective-permute-start(f32[12,24,128]{2,1,0:T(8,128)S(1)} %get-tuple-element.31.state), channel_id=1, source_target_pairs={{0,8},{8,16},{16,24},{24,32},{32,40},{40,48},{48,56},{56,64},{64,7... | collective-permute-start | bytes 442376 | tf_op jit(solution)/shard_map/ppermute | solution.py:377
  45.3 1.3 %collective-permute-start.4 = (f32[6,24,128]{2,1,0:T(8,128)S(1)}, f32[6,24,128]{2,1,0:T(8,128)S(1)}, u32[]{:S(2)}, u32[]{:S(2)}) collective-permute-start(f32[6,24,128]{2,1,0:T(8,128)S(1)} %get-tuple-element.36), channel_id=1, source_target_pairs={{248,256},{249,257},{250,258},{251,259},{252,260},{253,261},{254,2... | collective-permute-start | bytes 221192 | tf_op jit(solution)/shard_map/ppermute | solution.py:378
  46.6 3.6 %collective-permute-start.6 = (f32[40,128]{1,0:T(8,128)S(1)}, f32[40,128]{1,0:T(8,128)S(1)}, u32[]{:S(2)}, u32[]{:S(2)}) collective-permute-start(f32[40,128]{1,0:T(8,128)S(1)} %get-tuple-element.37), channel_id=1, source_target_pairs={{0,64},{8,72},{16,80},{24,88},{32,96},{40,104},{48,112},{56,120},{... | collective-permute-start | bytes 61448 | tf_op jit(solution)/shard_map/ppermute | solution.py:384
  50.2 9.4 %collective-permute-done.4.cross = f32[6,24,128]{2,1,0:T(8,128)S(1)} collective-permute-done((f32[6,24,128]{2,1,0:T(8,128)S(1)}, f32[6,24,128]{2,1,0:T(8,128)S(1)}, u32[]{:S(2)}, u32[]{:S(2)}) %collective-permute-start.4) | collective-permute-done | bytes 73760 | tf_op jit(solution)/shard_map/ppermute | solution.py:378
  59.6 0.0 collective-permute-done.5.shifted.one
  59.6 0.0 collective-permute-done.6.short
  59.6 0.0 all-to-all-done.1
  59.6 0.7 prefix_kernel.1
  60.4 6.9 %all-to-all-start.2 = ((f32[8,40,128]{2,1,0:T(8,128)}), f32[8,40,128]{2,1,0:T(8,128)S(1)}, u32[]{:S(2)}, u32[]{:S(2)}) async-start(f32[8,40,128]{2,1,0:T(8,128)} %bitcast.9), calls=%async_computation.2 | async-start | bytes 327680 | tf_op jit(solution)/shard_map/all_to_all | solution.py:342
  67.2 1.3 %collective-permute-start.9 = (f32[6,24,128]{2,1,0:T(8,128)S(1)}, f32[6,24,128]{2,1,0:T(8,128)S(1)}, u32[]{:S(2)}, u32[]{:S(2)}) collective-permute-start(f32[6,24,128]{2,1,0:T(8,128)S(1)} %get-tuple-element.43), channel_id=1, source_target_pairs={{248,256},{249,257},{250,258},{251,259},{252,260},{253,261},{254,2... | collective-permute-start | bytes 221192 | tf_op jit(solution)/shard_map/ppermute | solution.py:379
  68.5 2.8 %all-to-all-done.2 = f32[8,40,128]{2,1,0:T(8,128)S(1)} async-done(((f32[8,40,128]{2,1,0:T(8,128)}), f32[8,40,128]{2,1,0:T(8,128)S(1)}, u32[]{:S(2)}, u32[]{:S(2)}) %all-to-all-start.2) | async-done | bytes 163872 | tf_op jit(solution)/shard_map/all_to_all | solution.py:342
  71.3 1.9 %collective-permute-start.7 = (f32[144,128]{1,0:T(8,128)S(1)}, f32[144,128]{1,0:T(8,128)S(1)}, u32[]{:S(2)}, u32[]{:S(2)}) collective-permute-start(f32[144,128]{1,0:T(8,128)S(1)} %get-tuple-element.41), channel_id=1, source_target_pairs={{1,2},{2,1},{3,4},{4,3},{5,6},{6,5},{9,10},{10,9},{11,12},{12,11},... | collective-permute-start | bytes 221192 | tf_op jit(solution)/shard_map/ppermute | solution.py:332
  73.3 1.9 %collective-permute-start.8 = (f32[144,128]{1,0:T(8,128)S(1)}, f32[144,128]{1,0:T(8,128)S(1)}, u32[]{:S(2)}, u32[]{:S(2)}) collective-permute-start(f32[144,128]{1,0:T(8,128)S(1)} %get-tuple-element.42), channel_id=1, source_target_pairs={{0,1},{1,0},{2,3},{3,2},{4,5},{5,4},{6,7},{7,6},{8,9},{9,8},{10,11... | collective-permute-start | bytes 221192 | tf_op jit(solution)/shard_map/ppermute | solution.py:333
  75.2 6.4 %collective-permute-done.9.rest = f32[6,24,128]{2,1,0:T(8,128)S(1)} collective-permute-done((f32[6,24,128]{2,1,0:T(8,128)S(1)}, f32[6,24,128]{2,1,0:T(8,128)S(1)}, u32[]{:S(2)}, u32[]{:S(2)}) %collective-permute-start.9) | collective-permute-done | bytes 73760 | tf_op jit(solution)/shard_map/ppermute | solution.py:379
  81.6 0.0 collective-permute-done.7.far
  81.6 0.0 collective-permute-done.8.near
  81.6 2.2 %last_kernel.1 = (f32[1152,128]{1,0:T(8,128)}, f32[288,128]{1,0:T(8,128)}) custom-call(f32[12,24,128]{2,1,0:T(8,128)S(1)} %get-tuple-element.40.state, f32[144,128]{1,0:T(8,128)S(1)} %collective-permute-done.7.far, f32[144,128]{1,0:T(8,128)S(1)} %collective-permute-done.8.near, f32[12,64,128]{2,1,0:T(8,128)S(1)} %get-tuple-element.34.fwin, ...), custom_call_target="tpu_custom_call" | custom-call | tf_op jit(solution)/shard_map/last_kernel/pallas_call | solution.py:317
  (2 shorter events, 0.1 us)
Async XLA Ops:
  0.6 9.2 %copy-start = (f32[4,12,6,512]{3,0,2,1:T(4,128)S(1)}, f32[4,12,6,512]{3,0,2,1:T(4,128)}, u32[]{:S(2)}) copy-start(f32[4,12,6,512]{3,0,2,1:T(4,128)} %param.7) | copy-start | bytes 1769476
  0.6 6.9 %copy-start.1 = (f32[12,6,512]{2,1,0:T(8,128)S(1)}, f32[12,6,512]{2,1,0:T(8,128)}, u32[]{:S(2)}) copy-start(f32[12,6,512]{2,1,0:T(8,128)} %forcing.3) | copy-start | bytes 442372
  2.7 4.8 %copy-start.4 = (f32[8]{0:T(128)S(1)}, f32[8]{0:T(128)}, u32[]{:S(2)}) copy-start(f32[8]{0:T(128)} %lv.1) | copy-start | bytes 100
  2.7 4.8 %copy-start.5 = (f32[4]{0:T(128)S(1)}, f32[4]{0:T(128)}, u32[]{:S(2)}) copy-start(f32[4]{0:T(128)} %st.1) | copy-start | bytes 52
  2.7 4.8 %copy-start.6 = (s32[12]{0:T(128)S(1)}, s32[12]{0:T(128)}, u32[]{:S(2)}) copy-start(s32[12]{0:T(128)} %kl.1) | copy-start | bytes 148
  2.7 7.1 %collective-permute-start = (f32[336,128]{1,0:T(8,128)}, f32[336,128]{1,0:T(8,128)S(1)}, u32[]{:S(2)}, u32[]{:S(2)}) collective-permute-start(f32[336,128]{1,0:T(8,128)} %get-tuple-element.25), channel_id=1, source_target_pairs={{1,2},{2,1},{3,4},{4,3},{5,6},{6,5},{9,10},{10,9},{11,12},{12,11},... | collective-permute-start | bytes 516104 | tf_op jit(solution)/shard_map/ppermute | solution.py:332
  5.6 4.2 %collective-permute-start.1 = (f32[336,128]{1,0:T(8,128)}, f32[336,128]{1,0:T(8,128)S(1)}, u32[]{:S(2)}, u32[]{:S(2)}) collective-permute-start(f32[336,128]{1,0:T(8,128)} %get-tuple-element.26), channel_id=1, source_target_pairs={{0,1},{1,0},{2,3},{3,2},{4,5},{5,4},{6,7},{7,6},{8,9},{9,8},{10,11... | collective-permute-start | bytes 516104 | tf_op jit(solution)/shard_map/ppermute | solution.py:333
  7.5 0.7 copy-start.3
  9.8 6.6 %copy-start.2 = (f32[12,6,512]{2,1,0:T(8,128)S(1)}, f32[12,6,512]{2,1,0:T(8,128)}, u32[]{:S(2)}) copy-start(f32[12,6,512]{2,1,0:T(8,128)} %raw.1) | copy-start | bytes 442372
  11.4 5.9 %collective-permute-start.2 = (f32[192,128]{1,0:T(8,128)S(1)}, f32[192,128]{1,0:T(8,128)S(1)}, u32[]{:S(2)}, u32[]{:S(2)}) collective-permute-start(f32[192,128]{1,0:T(8,128)S(1)} %get-tuple-element.32), channel_id=1, source_target_pairs={{1,2},{2,1},{3,4},{4,3},{5,6},{6,5},{9,10},{10,9},{11,12},{12,11},... | collective-permute-start | bytes 294920 | tf_op jit(solution)/shard_map/ppermute | solution.py:332
  14.4 3.2 %collective-permute-start.3 = (f32[192,128]{1,0:T(8,128)S(1)}, f32[192,128]{1,0:T(8,128)S(1)}, u32[]{:S(2)}, u32[]{:S(2)}) collective-permute-start(f32[192,128]{1,0:T(8,128)S(1)} %get-tuple-element.33), channel_id=1, source_target_pairs={{0,1},{1,0},{2,3},{3,2},{4,5},{5,4},{6,7},{7,6},{8,9},{9,8},{10,11... | collective-permute-start | bytes 294920 | tf_op jit(solution)/shard_map/ppermute | solution.py:333
  31.0 28.6 %all-to-all-start.1 = ((f32[8,40,128]{2,1,0:T(8,128)}), f32[8,40,128]{2,1,0:T(8,128)S(1)}, u32[]{:S(2)}, u32[]{:S(2)}) async-start(f32[8,40,128]{2,1,0:T(8,128)} %bitcast.7), calls=%async_computation.1 | async-start | bytes 327680 | tf_op jit(solution)/shard_map/all_to_all | solution.py:342
  43.0 16.6 %collective-permute-start.5 = (f32[12,24,128]{2,1,0:T(8,128)S(1)}, f32[12,24,128]{2,1,0:T(8,128)S(1)}, u32[]{:S(2)}, u32[]{:S(2)}) collective-permute-start(f32[12,24,128]{2,1,0:T(8,128)S(1)} %get-tuple-element.31.state), channel_id=1, source_target_pairs={{0,8},{8,16},{16,24},{24,32},{32,40},{40,48},{48,56},{56,64},{64,7... | collective-permute-start | bytes 442376 | tf_op jit(solution)/shard_map/ppermute | solution.py:377
  45.3 14.4 %collective-permute-start.4 = (f32[6,24,128]{2,1,0:T(8,128)S(1)}, f32[6,24,128]{2,1,0:T(8,128)S(1)}, u32[]{:S(2)}, u32[]{:S(2)}) collective-permute-start(f32[6,24,128]{2,1,0:T(8,128)S(1)} %get-tuple-element.36), channel_id=1, source_target_pairs={{248,256},{249,257},{250,258},{251,259},{252,260},{253,261},{254,2... | collective-permute-start | bytes 221192 | tf_op jit(solution)/shard_map/ppermute | solution.py:378
  46.6 13.1 %collective-permute-start.6 = (f32[40,128]{1,0:T(8,128)S(1)}, f32[40,128]{1,0:T(8,128)S(1)}, u32[]{:S(2)}, u32[]{:S(2)}) collective-permute-start(f32[40,128]{1,0:T(8,128)S(1)} %get-tuple-element.37), channel_id=1, source_target_pairs={{0,64},{8,72},{16,80},{24,88},{32,96},{40,104},{48,112},{56,120},{... | collective-permute-start | bytes 61448 | tf_op jit(solution)/shard_map/ppermute | solution.py:384
  60.4 10.9 %all-to-all-start.2 = ((f32[8,40,128]{2,1,0:T(8,128)}), f32[8,40,128]{2,1,0:T(8,128)S(1)}, u32[]{:S(2)}, u32[]{:S(2)}) async-start(f32[8,40,128]{2,1,0:T(8,128)} %bitcast.9), calls=%async_computation.2 | async-start | bytes 327680 | tf_op jit(solution)/shard_map/all_to_all | solution.py:342
  67.2 14.4 %collective-permute-start.9 = (f32[6,24,128]{2,1,0:T(8,128)S(1)}, f32[6,24,128]{2,1,0:T(8,128)S(1)}, u32[]{:S(2)}, u32[]{:S(2)}) collective-permute-start(f32[6,24,128]{2,1,0:T(8,128)S(1)} %get-tuple-element.43), channel_id=1, source_target_pairs={{248,256},{249,257},{250,258},{251,259},{252,260},{253,261},{254,2... | collective-permute-start | bytes 221192 | tf_op jit(solution)/shard_map/ppermute | solution.py:379
  71.3 10.3 %collective-permute-start.7 = (f32[144,128]{1,0:T(8,128)S(1)}, f32[144,128]{1,0:T(8,128)S(1)}, u32[]{:S(2)}, u32[]{:S(2)}) collective-permute-start(f32[144,128]{1,0:T(8,128)S(1)} %get-tuple-element.41), channel_id=1, source_target_pairs={{1,2},{2,1},{3,4},{4,3},{5,6},{6,5},{9,10},{10,9},{11,12},{12,11},... | collective-permute-start | bytes 221192 | tf_op jit(solution)/shard_map/ppermute | solution.py:332
  73.3 8.4 %collective-permute-start.8 = (f32[144,128]{1,0:T(8,128)S(1)}, f32[144,128]{1,0:T(8,128)S(1)}, u32[]{:S(2)}, u32[]{:S(2)}) collective-permute-start(f32[144,128]{1,0:T(8,128)S(1)} %get-tuple-element.42), channel_id=1, source_target_pairs={{0,1},{1,0},{2,3},{3,2},{4,5},{5,4},{6,7},{7,6},{8,9},{9,8},{10,11... | collective-permute-start | bytes 221192 | tf_op jit(solution)/shard_map/ppermute | solution.py:333

commit v5 on v4

--- a/solution.py
+++ b/solution.py
@@ -9,7 +9,6 @@
 
 F32 = jnp.float32
 C = 12
-HALF = C // 2
 NY = 16
 NZ = 32
 PLANES = 6
@@ -23,6 +22,7 @@
 BASE = 5 * ROWS
 GROUP = 8
 PIECE = 40
+WIDE = 2 * PIECE
 VMEM = pl.BlockSpec(memory_space=pltpu.VMEM)
 SMEM = pl.BlockSpec(memory_space=pltpu.SMEM)
 HBM = pl.BlockSpec(memory_space=pl.ANY)
@@ -198,7 +198,7 @@
 FOUR = ((1, 3), (1, 3), (2, 2), (2, 2))
 
 
-def first_kernel(guess, force, far, near, kv, wup, wfix, mask, own, state, low, high, send_near, send_far, fwin, a, b):
+def first_kernel(guess, force, far, near, kv, wup, wfix, mask, own, state, send_near, send_far, fwin, a, b):
     clear_edges(a)
     clear_edges(b)
     clear_edges(fwin)
@@ -209,8 +209,6 @@
     put_halo(fwin, near, far, THREE, C * HALO)
     steps((a, b), fwin, FOUR, (kv, wup, wfix, mask))
     state[...] = a[:, BASE : BASE + OWN, :]
-    low[...] = a[:HALF, BASE : BASE + OWN, :]
-    high[...] = a[HALF:, BASE : BASE + OWN, :]
     put_sends(pack(state, 0, HALO, 0), pack(state, OWN - HALO, HALO, 0), send_near, send_far)
 
 
@@ -221,10 +219,20 @@
     put_halo(a, near, far, HALO, 0)
     steps((a, b), fwin, FOUR, (kv, wup, wfix, mask))
     use = jnp.where(lax.axis_index("tm") > 0, F32(1.0), F32(0.0))
-    for c in range(C):
-        here = pl.ds(c * OWN, OWN)
-        out[here, :] = a[c, BASE : BASE + OWN, :] - use * (gain[here, :] * state[c])
-    out[C * OWN :, :] = jnp.zeros((out.shape[0] - C * OWN, 128), F32)
+    tiles = OWN // 8
+    for t in range(GROUP * PIECE // 8):
+        p, r = divmod(t, PIECE // 8)
+        here = pl.ds(p * WIDE + r * 8, 8)
+        there = pl.ds(p * WIDE + PIECE + r * 8, 8)
+        if t < C * tiles:
+            c, x = divmod(t, tiles)
+            u = state[c, x * 8 : x * 8 + 8, :]
+            v = a[c, BASE + x * 8 : BASE + x * 8 + 8, :]
+            out[here, :] = v - use * (gain[t * 8 : t * 8 + 8, :] * u)
+            out[there, :] = u
+        else:
+            out[here, :] = jnp.zeros((8, 128), F32)
+            out[there, :] = jnp.zeros((8, 128), F32)
 
 
 def my_gain(gain):
@@ -232,25 +240,26 @@
     return gain[pl.ds(pl.multiple_of(place * PIECE, 8), PIECE), :]
 
 
-def slot(i):
-    return slice((GROUP - 1 - i) * PIECE, (GROUP - i) * PIECE)
-
-
-def local_kernel(pieces, gain, sums, total, short):
+def slot(i, width=PIECE, half=0):
+    start = (GROUP - 1 - i) * width + half * PIECE
+    return slice(start, start + PIECE)
+
+
+def local_kernel(pieces, gain, sums, total, tail):
     mine = my_gain(gain)
-    running = pieces[slot(0), :]
+    running = pieces[slot(0, WIDE), :]
     sums[slot(0), :] = running
     for i in range(1, GROUP):
-        running = mine * running + pieces[slot(i), :]
+        running = mine * running + pieces[slot(i, WIDE), :]
         sums[slot(i), :] = running
         if i == GROUP - 2:
-            short[...] = running
+            tail[:PIECE, :] = running
+    tail[PIECE:, :] = pieces[slot(GROUP - 1, WIDE, 1), :]
     for i in range(GROUP):
         total[slot(i), :] = running
 
 
-def prefix_kernel(totals, cross, shifted, short, sums, gain, out):
-    del cross, shifted
+def prefix_kernel(totals, tail, sums, pieces, gain, out):
     group = lax.axis_index("tm") // GROUP
     g1 = my_gain(gain)
     g2 = g1 * g1
@@ -262,33 +271,40 @@
         take = g < group
         ahead = jnp.where(take, before, ahead)
         before = jnp.where(take, g8 * before + totals[slot(g), :], before)
-    out[slot(0), :] = short[...] + (g4 * g2 * g1) * ahead
-    out[slot(1), :] = before
-    for i in range(2, GROUP):
-        before = g1 * before
-        out[slot(i), :] = sums[slot(i - 2), :] + before
-
-
-def gather_kernel(pieces, one, own, state, near, far):
-    k = lax.axis_index("tm")
-
-    @pl.when(k == 0)
+    for i in range(GROUP):
+        if i == 0:
+            base = tail[PIECE:, :]
+            value = tail[:PIECE, :] + (g4 * g2 * g1) * ahead
+        else:
+            base = pieces[slot(i - 1, WIDE, 1), :]
+            if i == 1:
+                value = jnp.where(group > 0, before, base)
+            else:
+                before = g1 * before
+                value = sums[slot(i - 2), :] + before
+        out[slot(i, WIDE), :] = value
+        out[slot(i, WIDE, 1), :] = value - base
+
+
+def gather_kernel(pieces, own, state, near, far):
+    first = lax.axis_index("tm") == 0
+
+    @pl.when(first)
     def _():
         state[...] = own[...]
 
-    @pl.when(k == 1)
-    def _():
-        state[...] = one[...]
-
-    @pl.when(k >= 2)
-    def _():
-        for c in range(C):
-            state[c] = pieces[c * OWN : (c + 1) * OWN, :]
+    @pl.when(jnp.logical_not(first))
+    def _():
+        tiles = OWN // 8
+        for t in range(C * tiles):
+            c, x = divmod(t, tiles)
+            p, r = divmod(t, PIECE // 8)
+            state[c, x * 8 : x * 8 + 8, :] = pieces[p * WIDE + r * 8 : p * WIDE + r * 8 + 8, :]
 
     put_sends(pack(state, 0, THREE, 0), pack(state, OWN - THREE, THREE, 0), near, far)
 
 
-def last_kernel(state, far, near, fwin, shifted, cross, rest, kv, wup, wfix, mask, out, corr, a, b):
+def last_kernel(state, far, near, fwin, pieces, kv, wup, wfix, mask, out, corr, a, b):
     clear_edges(a)
     clear_edges(b)
     a[:, BASE : BASE + OWN, :] = state[...]
@@ -304,10 +320,11 @@
         src, dst = bufs[j % 2], bufs[(j + 1) % 2]
         steps((src, dst), fwin, (one,), (kv, wup, wfix, mask))
         emit(dst, j + 1)
-    late = lax.axis_index("tm") >= 2
-    for c in range(C):
-        over = cross[c] if c < HALF else rest[c - HALF]
-        corr[c * OWN : (c + 1) * OWN, :] = jnp.where(late, state[c] - (shifted[c] + over), 0.0)
+    late = lax.axis_index("tm") >= 1
+    for t in range(C * OWN // 8):
+        p, r = divmod(t, PIECE // 8)
+        start = p * WIDE + PIECE + r * 8
+        corr[t * 8 : t * 8 + 8, :] = jnp.where(late, pieces[start : start + 8, :], 0.0)
 
 
 WORK = [pltpu.VMEM((C, WIN, 128), F32), pltpu.VMEM((C, WIN, 128), F32)]
@@ -338,7 +355,7 @@
     count = lax.axis_size("tm")
     firsts = [i for i in range(count) if (i // stride) % GROUP == 0]
     groups = [[i + stride * j for j in reversed(range(GROUP))] for i in firsts]
-    slots = value.reshape(GROUP, PIECE, 128)
+    slots = value.reshape(GROUP, -1, 128)
     return lax.all_to_all(slots, "tm", 0, 0, tiled=True, axis_index_groups=groups).reshape(value.shape)
 
 
@@ -347,7 +364,7 @@
     rows = guess.reshape(SLICES, C, PLANES, ROWS, 128).transpose(1, 2, 3, 0, 4).reshape(C * OWN * SLICES, 128)
     slab = arr(C, OWN, 128)
     wide, four, three = (arr(C * n, 128) for n in (HALO + THREE, HALO, THREE))
-    pieces = arr(GROUP * PIECE, 128)
+    pieces, double = arr(GROUP * PIECE, 128), arr(GROUP * WIDE, 128)
     near, far = call(
         prep_kernel,
         [rows, forcing],
@@ -365,32 +382,27 @@
         place=[VMEM] + [SMEM] * len(small),
     )
     (gain,) = call(gain_kernel, [coarse_gain], [pieces])
-    half = arr(HALF, OWN, 128)
-    own, state, low, high, near, far, fwin = call(
+    own, state, near, far, fwin = call(
         first_kernel,
         [rows, force, far, near, *coefs],
-        [slab, slab, half, half, four, four, arr(C, WIN, 128)],
+        [slab, slab, four, four, arr(C, WIN, 128)],
         WORK,
     )
     near, far = exchange(near, far)
-    middle = intervals // 2
-    shifted = lax.ppermute(state, "tm", [(i, i + 1) for i in range(intervals - 1) if i + 1 != middle])
-    cross = lax.ppermute(low, "tm", [(middle - 1, middle)])
-    rest = lax.ppermute(high, "tm", [(middle - 1, middle)])
-    (element,) = call(second_kernel, [state, far, near, fwin, gain, *coefs], [pieces], WORK)
+    (element,) = call(second_kernel, [state, far, near, fwin, gain, *coefs], [double], WORK)
     spread = swap(element, 1)
-    sums, totals, short = call(local_kernel, [spread, gain], [pieces, pieces, arr(PIECE, 128)])
+    sums, totals, tail = call(local_kernel, [spread, gain], [pieces, pieces, arr(WIDE, 128)])
     totals = swap(totals, GROUP)
-    short = lax.ppermute(short, "tm", [(i, i + GROUP) for i in range(intervals - GROUP)])
-    (back,) = call(prefix_kernel, [totals, cross, shifted, short, sums, gain], [pieces])
+    tail = lax.ppermute(tail, "tm", [(i, i + GROUP) for i in range(intervals - GROUP)])
+    (back,) = call(prefix_kernel, [totals, tail, sums, spread, gain], [double])
     back = swap(back, 1)
     state, near, far = call(
-        gather_kernel, [back, shifted, own], [slab, three, three]
+        gather_kernel, [back, own], [slab, three, three]
     )
     near, far = exchange(near, far)
     updated, corr = call(
         last_kernel,
-        [state, far, near, fwin, shifted, cross, rest, *coefs],
+        [state, far, near, fwin, back, *coefs],
         [arr(C * OWN * SLICES, 128), arr(C * OWN, 128)],
         WORK,
     )

time: 84.5 us -> 76.4 us (0.904)
  blocking collectives: 11.1 us -> 23 us
  starting transfers between devices: 40.8 us -> 29.2 us
  waiting for transfers between devices: 20.5 us -> 12.5 us
  Pallas kernels: 9.85 us -> 8.93 us
    all_to_all x1 -> x2, blocking collectives: 11.1 us -> 23 us  [swap(): lax.all_to_all(slots, 'tm', 0, 0, tiled=True, axis_index_groups=groups)]
    all_to_all x2 -> x1, starting transfers between devices: 18.8 us -> 11.4 us  [swap(): lax.all_to_all(slots, 'tm', 0, 0, tiled=True, axis_index_groups=groups)]
    ppermute x4 -> x1, waiting for transfers between devices: 15.9 us -> 8.81 us  [shards(): lax.ppermute(tail, 'tm', [(i, i + GROUP) for i in range(intervals - GROUP)])]
    ppermute x4 -> x1, starting transfers between devices: 8.46 us -> 4.26 us  [shards(): lax.ppermute(tail, 'tm', [(i, i + GROUP) for i in range(intervals - GROUP)])]
    all_to_all x2 -> x1, waiting for transfers between devices: 2.76 us -> 0.01 us  [swap(): lax.all_to_all(slots, 'tm', 0, 0, tiled=True, axis_index_groups=groups)]
    ppermute x3, waiting for transfers between devices: 1.66 us -> 3.47 us  [exchange(): far = lax.ppermute(far, 'space', outer)]
    pallas_call x9, Pallas kernels: 9.85 us -> 8.93 us  [call(): pl.pallas_call(kernel, out_shape=outs, in_specs=place or [VMEM] * len(ins...]
  transfers between devices with their start and end apart: 12 -> 8, of which waited for: 6 -> 5; matrix products, arithmetic and copies ran while one was open for 0% -> 0% of each run, Pallas kernels for 1% -> 1%
where the time goes in v5:
time: 76.4 us; the launch traced here: 75.3 us
  starting transfers between devices  29.2 us (38%)
  blocking collectives  23 us (30%)
  waiting for transfers between devices  12.5 us (16%)
  Pallas kernels  8.93 us (12%)
  between operations  0.82 us (1%)
    all_to_all x2, blocking collectives, swap(): lax.all_to_all(slots, 'tm', 0, 0, tiled=True, axis_index_groups=groups)  23 us
    all_to_all x1, starting transfers between devices, swap(): lax.all_to_all(slots, 'tm', 0, 0, tiled=True, axis_index_groups=groups)  11.4 us
    pallas_call x9, Pallas kernels, call(): pl.pallas_call(kernel, out_shape=outs, in_specs=place or [VMEM] * len(ins...  8.93 us
    ppermute x1, waiting for transfers between devices, shards(): lax.ppermute(tail, 'tm', [(i, i + GROUP) for i in range(intervals - GROUP)])  8.81 us
    ppermute x3, starting transfers between devices, exchange(): far = lax.ppermute(far, 'space', outer)  7.73 us
    ppermute x3, starting transfers between devices, exchange(): near = lax.ppermute(near, 'space', inner)  5.76 us
    ppermute x1, starting transfers between devices, shards(): lax.ppermute(tail, 'tm', [(i, i + GROUP) for i in range(intervals - GROUP)])  4.26 us
    ppermute x3, waiting for transfers between devices, exchange(): far = lax.ppermute(far, 'space', outer)  3.47 us
  transfers between devices with their start and end apart: 8, of which 5 were waited for; matrix products, arithmetic and copies ran while one was open for 0% of the time, Pallas kernels for 1%

profile of v5, /device:TPU:56, one launch (start us, length us, event | category | flops | bytes accessed | tf_op | source)
XLA Modules:
  0.0 75.3 jit_solution(10670252793962725758)
XLA Ops:
  0.6 0.0 copy-start
  0.6 0.0 copy-start.1
  0.6 2.0 %prep_kernel.1 = (f32[336,128]{1,0:T(8,128)}, f32[336,128]{1,0:T(8,128)}) custom-call(f32[1152,128]{1,0:T(8,128)} %bitcast.21, f32[12,6,512]{2,1,0:T(8,128)} %forcing.3), custom_call_target="tpu_custom_call" | custom-call | tf_op jit(solution)/shard_map/prep_kernel/pallas_call | solution.py:334
  2.7 0.0 copy-start.4
  2.7 0.0 copy-start.5
  2.7 0.0 copy-start.6
  2.7 2.8 %collective-permute-start = (f32[336,128]{1,0:T(8,128)}, f32[336,128]{1,0:T(8,128)S(1)}, u32[]{:S(2)}, u32[]{:S(2)}) collective-permute-start(f32[336,128]{1,0:T(8,128)} %get-tuple-element.23), channel_id=1, source_target_pairs={{1,2},{2,1},{3,4},{4,3},{5,6},{6,5},{9,10},{10,9},{11,12},{12,11},... | collective-permute-start | bytes 516104 | tf_op jit(solution)/shard_map/ppermute | solution.py:349
  5.5 1.9 %collective-permute-start.1 = (f32[336,128]{1,0:T(8,128)}, f32[336,128]{1,0:T(8,128)S(1)}, u32[]{:S(2)}, u32[]{:S(2)}) collective-permute-start(f32[336,128]{1,0:T(8,128)} %get-tuple-element.24), channel_id=1, source_target_pairs={{0,1},{1,0},{2,3},{3,2},{4,5},{5,4},{6,7},{7,6},{8,9},{9,8},{10,11... | collective-permute-start | bytes 516104 | tf_op jit(solution)/shard_map/ppermute | solution.py:350
  7.5 0.0 copy-done.1
  7.5 0.0 copy-done.4
  7.5 0.0 copy-done.5
  7.5 0.0 copy-done.6
  7.5 0.0 copy-start.3
  7.5 0.7 copy-done.3
  8.2 0.9 %setup_kernel.1 = (f32[12,24,128]{2,1,0:T(8,128)S(1)}, f32[144,8,128]{2,1,0:T(8,128)S(1)}, f32[12,8,128]{2,1,0:T(8,128)S(1)}, f32[3,8,128]{2,1,0:T(8,128)S(1)}, f32[8,8,128]{2,1,0:T(8,128)S(1)}) custom-call(f32[12,6,512]{2,1,0:T(8,128)S(1)} %copy-done.1, f32[8]{0:T(128)S(1)} %copy-done.4, s32[12,12]{1,0:T(8,128)S(1)} %copy-done.3, f32[4]{0:T(128)S(1)} %copy-done.5, ...), custom_call_target="tpu_custom_call" | custom-call | tf_op jit(solution)/shard_map/setup_kernel/pallas_call | solution.py:334
  9.1 0.7 collective-permute-done.far
  9.8 0.0 collective-permute-done.1.near
  9.8 0.0 copy-done
  9.8 0.0 copy-start.2
  9.8 1.6 %first_kernel.1 = (f32[12,24,128]{2,1,0:T(8,128)S(1)}, f32[12,24,128]{2,1,0:T(8,128)S(1)}, f32[192,128]{1,0:T(8,128)S(1)}, f32[192,128]{1,0:T(8,128)S(1)}, f32[12,64,128]{2,1,0:T(8,128)S(1)}) custom-call(f32[1152,128]{1,0:T(8,128)S(1)} %bitcast.22, f32[12,24,128]{2,1,0:T(8,128)S(1)} %get-tuple-element.22.force, f32[336,128]{1,0:T(8,128)S(1)} %collective-permute-done.far, ...), custom_call_target="tpu_custom_call" | custom-call | tf_op jit(solution)/shard_map/first_kernel/pallas_call | solution.py:334
  11.4 3.0 %collective-permute-start.2 = (f32[192,128]{1,0:T(8,128)S(1)}, f32[192,128]{1,0:T(8,128)S(1)}, u32[]{:S(2)}, u32[]{:S(2)}) collective-permute-start(f32[192,128]{1,0:T(8,128)S(1)} %get-tuple-element.30), channel_id=1, source_target_pairs={{1,2},{2,1},{3,4},{4,3},{5,6},{6,5},{9,10},{10,9},{11,12},{12,11},... | collective-permute-start | bytes 294920 | tf_op jit(solution)/shard_map/ppermute | solution.py:349
  14.4 1.9 %collective-permute-start.3 = (f32[192,128]{1,0:T(8,128)S(1)}, f32[192,128]{1,0:T(8,128)S(1)}, u32[]{:S(2)}, u32[]{:S(2)}) collective-permute-start(f32[192,128]{1,0:T(8,128)S(1)} %get-tuple-element.31), channel_id=1, source_target_pairs={{0,1},{1,0},{2,3},{3,2},{4,5},{5,4},{6,7},{7,6},{8,9},{9,8},{10,11... | collective-permute-start | bytes 294920 | tf_op jit(solution)/shard_map/ppermute | solution.py:350
  16.4 0.0 copy-done.2
  16.4 1.0 %collective-permute-done.2.far = f32[192,128]{1,0:T(8,128)S(1)} collective-permute-done((f32[192,128]{1,0:T(8,128)S(1)}, f32[192,128]{1,0:T(8,128)S(1)}, u32[]{:S(2)}, u32[]{:S(2)}) %collective-permute-start.2) | collective-permute-done | bytes 98336 | tf_op jit(solution)/shard_map/ppermute | solution.py:349
  17.4 0.3 collective-permute-done.3.near
  17.6 1.6 %second_kernel.1 = f32[640,128]{1,0:T(8,128)S(1)} custom-call(f32[12,24,128]{2,1,0:T(8,128)S(1)} %get-tuple-element.29.state, f32[192,128]{1,0:T(8,128)S(1)} %collective-permute-done.2.far, f32[192,128]{1,0:T(8,128)S(1)} %collective-permute-done.3.near, f32[12,64,128]{2,1,0:T(8,128)S(1)} %get-tuple-element.32.fwin, f32[320,128]{1,0:T(8,128)S(1)} %gain_kernel.1.gain, ...), custom_call_target="tpu_custom_call" | custom-call | tf_op jit(solution)/shard_map/second_kernel/pallas_call | solution.py:334
  19.2 12.8 %all_to_all.15 = f32[8,80,128]{2,1,0:T(8,128)S(1)} all-to-all(f32[8,80,128]{2,1,0:T(8,128)S(1)} %bitcast.24), channel_id=1, replica_groups={{56,48,40,32,24,16,8,0},{120,112,104,96,88,80,72,64},{184,176,168,160,1..., dimensions={0} | all-to-all | bytes 655360 | tf_op jit(solution)/shard_map/all_to_all | solution.py:359
  32.0 0.7 local_kernel.1
  32.7 11.4 %all-to-all-start.1 = ((f32[8,40,128]{2,1,0:T(8,128)}), f32[8,40,128]{2,1,0:T(8,128)S(1)}, u32[]{:S(2)}, u32[]{:S(2)}) async-start(f32[8,40,128]{2,1,0:T(8,128)} %bitcast.7), calls=%async_computation.1 | async-start | bytes 327680 | tf_op jit(solution)/shard_map/all_to_all | solution.py:359
  44.2 4.3 %collective-permute-start.4 = (f32[80,128]{1,0:T(8,128)S(1)}, f32[80,128]{1,0:T(8,128)S(1)}, u32[]{:S(2)}, u32[]{:S(2)}) collective-permute-start(f32[80,128]{1,0:T(8,128)S(1)} %get-tuple-element.34), channel_id=1, source_target_pairs={{0,64},{8,72},{16,80},{24,88},{32,96},{40,104},{48,112},{56,120},{... | collective-permute-start | bytes 122888 | tf_op jit(solution)/shard_map/ppermute | solution.py:396
  48.5 8.8 %collective-permute-done.4.tail = f32[80,128]{1,0:T(8,128)S(1)} collective-permute-done((f32[80,128]{1,0:T(8,128)S(1)}, f32[80,128]{1,0:T(8,128)S(1)}, u32[]{:S(2)}, u32[]{:S(2)}) %collective-permute-start.4) | collective-permute-done | bytes 40992 | tf_op jit(solution)/shard_map/ppermute | solution.py:396
  57.3 0.0 all-to-all-done.1
  57.3 10.2 %all_to_all.16 = f32[8,80,128]{2,1,0:T(8,128)S(1)} all-to-all(f32[8,80,128]{2,1,0:T(8,128)S(1)} %bitcast.23), channel_id=1, replica_groups={{56,48,40,32,24,16,8,0},{120,112,104,96,88,80,72,64},{184,176,168,160,1..., dimensions={0} | all-to-all | bytes 655360 | tf_op jit(solution)/shard_map/all_to_all | solution.py:359
  67.6 1.9 %collective-permute-start.5 = (f32[144,128]{1,0:T(8,128)S(1)}, f32[144,128]{1,0:T(8,128)S(1)}, u32[]{:S(2)}, u32[]{:S(2)}) collective-permute-start(f32[144,128]{1,0:T(8,128)S(1)} %get-tuple-element.38), channel_id=1, source_target_pairs={{1,2},{2,1},{3,4},{4,3},{5,6},{6,5},{9,10},{10,9},{11,12},{12,11},... | collective-permute-start | bytes 221192 | tf_op jit(solution)/shard_map/ppermute | solution.py:349
  69.5 1.9 %collective-permute-start.6 = (f32[144,128]{1,0:T(8,128)S(1)}, f32[144,128]{1,0:T(8,128)S(1)}, u32[]{:S(2)}, u32[]{:S(2)}) collective-permute-start(f32[144,128]{1,0:T(8,128)S(1)} %get-tuple-element.39), channel_id=1, source_target_pairs={{0,1},{1,0},{2,3},{3,2},{4,5},{5,4},{6,7},{7,6},{8,9},{9,8},{10,11... | collective-permute-start | bytes 221192 | tf_op jit(solution)/shard_map/ppermute | solution.py:350
  71.4 1.8 %collective-permute-done.5.far = f32[144,128]{1,0:T(8,128)S(1)} collective-permute-done((f32[144,128]{1,0:T(8,128)S(1)}, f32[144,128]{1,0:T(8,128)S(1)}, u32[]{:S(2)}, u32[]{:S(2)}) %collective-permute-start.5) | collective-permute-done | bytes 73760 | tf_op jit(solution)/shard_map/ppermute | solution.py:349
  73.2 0.0 collective-permute-done.6.near
  73.2 2.0 %last_kernel.1 = (f32[1152,128]{1,0:T(8,128)}, f32[288,128]{1,0:T(8,128)}) custom-call(f32[12,24,128]{2,1,0:T(8,128)S(1)} %get-tuple-element.37.state, f32[144,128]{1,0:T(8,128)S(1)} %collective-permute-done.5.far, f32[144,128]{1,0:T(8,128)S(1)} %collective-permute-done.6.near, f32[12,64,128]{2,1,0:T(8,128)S(1)} %get-tuple-element.32.fwin, ...), custom_call_target="tpu_custom_call" | custom-call | tf_op jit(solution)/shard_map/last_kernel/pallas_call | solution.py:334
  (3 shorter events, 0.1 us)
Async XLA Ops:
  0.6 9.2 %copy-start = (f32[4,12,6,512]{3,0,2,1:T(4,128)S(1)}, f32[4,12,6,512]{3,0,2,1:T(4,128)}, u32[]{:S(2)}) copy-start(f32[4,12,6,512]{3,0,2,1:T(4,128)} %param.7) | copy-start | bytes 1769476
  0.6 6.8 %copy-start.1 = (f32[12,6,512]{2,1,0:T(8,128)S(1)}, f32[12,6,512]{2,1,0:T(8,128)}, u32[]{:S(2)}) copy-start(f32[12,6,512]{2,1,0:T(8,128)} %forcing.3) | copy-start | bytes 442372
  2.7 4.8 %copy-start.4 = (f32[8]{0:T(128)S(1)}, f32[8]{0:T(128)}, u32[]{:S(2)}) copy-start(f32[8]{0:T(128)} %lv.1) | copy-start | bytes 100
  2.7 4.8 %copy-start.5 = (f32[4]{0:T(128)S(1)}, f32[4]{0:T(128)}, u32[]{:S(2)}) copy-start(f32[4]{0:T(128)} %st.1) | copy-start | bytes 52
  2.7 4.8 %copy-start.6 = (s32[12]{0:T(128)S(1)}, s32[12]{0:T(128)}, u32[]{:S(2)}) copy-start(s32[12]{0:T(128)} %kl.1) | copy-start | bytes 148
  2.7 7.1 %collective-permute-start = (f32[336,128]{1,0:T(8,128)}, f32[336,128]{1,0:T(8,128)S(1)}, u32[]{:S(2)}, u32[]{:S(2)}) collective-permute-start(f32[336,128]{1,0:T(8,128)} %get-tuple-element.23), channel_id=1, source_target_pairs={{1,2},{2,1},{3,4},{4,3},{5,6},{6,5},{9,10},{10,9},{11,12},{12,11},... | collective-permute-start | bytes 516104 | tf_op jit(solution)/shard_map/ppermute | solution.py:349
  5.5 4.2 %collective-permute-start.1 = (f32[336,128]{1,0:T(8,128)}, f32[336,128]{1,0:T(8,128)S(1)}, u32[]{:S(2)}, u32[]{:S(2)}) collective-permute-start(f32[336,128]{1,0:T(8,128)} %get-tuple-element.24), channel_id=1, source_target_pairs={{0,1},{1,0},{2,3},{3,2},{4,5},{5,4},{6,7},{7,6},{8,9},{9,8},{10,11... | collective-permute-start | bytes 516104 | tf_op jit(solution)/shard_map/ppermute | solution.py:350
  7.5 0.7 copy-start.3
  9.8 6.6 %copy-start.2 = (f32[12,6,512]{2,1,0:T(8,128)S(1)}, f32[12,6,512]{2,1,0:T(8,128)}, u32[]{:S(2)}) copy-start(f32[12,6,512]{2,1,0:T(8,128)} %raw.1) | copy-start | bytes 442372
  11.4 5.9 %collective-permute-start.2 = (f32[192,128]{1,0:T(8,128)S(1)}, f32[192,128]{1,0:T(8,128)S(1)}, u32[]{:S(2)}, u32[]{:S(2)}) collective-permute-start(f32[192,128]{1,0:T(8,128)S(1)} %get-tuple-element.30), channel_id=1, source_target_pairs={{1,2},{2,1},{3,4},{4,3},{5,6},{6,5},{9,10},{10,9},{11,12},{12,11},... | collective-permute-start | bytes 294920 | tf_op jit(solution)/shard_map/ppermute | solution.py:349
  14.4 3.2 %collective-permute-start.3 = (f32[192,128]{1,0:T(8,128)S(1)}, f32[192,128]{1,0:T(8,128)S(1)}, u32[]{:S(2)}, u32[]{:S(2)}) collective-permute-start(f32[192,128]{1,0:T(8,128)S(1)} %get-tuple-element.31), channel_id=1, source_target_pairs={{0,1},{1,0},{2,3},{3,2},{4,5},{5,4},{6,7},{7,6},{8,9},{9,8},{10,11... | collective-permute-start | bytes 294920 | tf_op jit(solution)/shard_map/ppermute | solution.py:350
  32.7 24.5 %all-to-all-start.1 = ((f32[8,40,128]{2,1,0:T(8,128)}), f32[8,40,128]{2,1,0:T(8,128)S(1)}, u32[]{:S(2)}, u32[]{:S(2)}) async-start(f32[8,40,128]{2,1,0:T(8,128)} %bitcast.7), calls=%async_computation.1 | async-start | bytes 327680 | tf_op jit(solution)/shard_map/all_to_all | solution.py:359
  44.2 13.1 %collective-permute-start.4 = (f32[80,128]{1,0:T(8,128)S(1)}, f32[80,128]{1,0:T(8,128)S(1)}, u32[]{:S(2)}, u32[]{:S(2)}) collective-permute-start(f32[80,128]{1,0:T(8,128)S(1)} %get-tuple-element.34), channel_id=1, source_target_pairs={{0,64},{8,72},{16,80},{24,88},{32,96},{40,104},{48,112},{56,120},{... | collective-permute-start | bytes 122888 | tf_op jit(solution)/shard_map/ppermute | solution.py:396
  67.6 5.7 %collective-permute-start.5 = (f32[144,128]{1,0:T(8,128)S(1)}, f32[144,128]{1,0:T(8,128)S(1)}, u32[]{:S(2)}, u32[]{:S(2)}) collective-permute-start(f32[144,128]{1,0:T(8,128)S(1)} %get-tuple-element.38), channel_id=1, source_target_pairs={{1,2},{2,1},{3,4},{4,3},{5,6},{6,5},{9,10},{10,9},{11,12},{12,11},... | collective-permute-start | bytes 221192 | tf_op jit(solution)/shard_map/ppermute | solution.py:349
  69.5 3.7 %collective-permute-start.6 = (f32[144,128]{1,0:T(8,128)S(1)}, f32[144,128]{1,0:T(8,128)S(1)}, u32[]{:S(2)}, u32[]{:S(2)}) collective-permute-start(f32[144,128]{1,0:T(8,128)S(1)} %get-tuple-element.39), channel_id=1, source_target_pairs={{0,1},{1,0},{2,3},{3,2},{4,5},{5,4},{6,7},{7,6},{8,9},{9,8},{10,11... | collective-permute-start | bytes 221192 | tf_op jit(solution)/shard_map/ppermute | solution.py:350

commit v6 on v5

--- a/solution.py
+++ b/solution.py
@@ -21,8 +21,10 @@
 WIN = 64
 BASE = 5 * ROWS
 GROUP = 8
-PIECE = 40
+PIECE = C * OWN // GROUP
 WIDE = 2 * PIECE
+SPACED = 40
+CHUNK = 12
 VMEM = pl.BlockSpec(memory_space=pltpu.VMEM)
 SMEM = pl.BlockSpec(memory_space=pltpu.SMEM)
 HBM = pl.BlockSpec(memory_space=pl.ANY)
@@ -87,7 +89,7 @@
             force[c, pl.ds(r, PLANES, stride=ROWS), :] = raw[c, :, 128 * r : 128 * r + 128] * 0.1
 
 
-def prep_kernel(guess, forcing, near, far, own, force, raw, fraw, sems):
+def prep_kernel(guess, forcing, own, force, near, far, raw, fraw, sems):
     one = pltpu.make_async_copy(forcing, fraw, sems.at[0])
     two = pltpu.make_async_copy(guess, raw, sems.at[1])
     one.start()
@@ -108,15 +110,15 @@
     put_sends(first, last, near, far)
 
 
-def gain_kernel(raw, gain_out):
+def gain_kernel(raw, rows, spaced):
     for c in range(C):
         for r in range(ROWS):
-            gain_out[pl.ds(c * OWN + r, PLANES, stride=ROWS), :] = raw[c, :, 128 * r : 128 * r + 128]
-    gain_out[C * OWN :, :] = jnp.zeros((gain_out.shape[0] - C * OWN, 128), F32)
-
-
-def setup_kernel(forcing, lv, cd, st, kl, force, kv, wup, wfix, mask):
-    take_forcing(forcing, force)
+            rows[pl.ds(c * OWN + r, PLANES, stride=ROWS), :] = raw[c, :, 128 * r : 128 * r + 128]
+    for p in range(GROUP):
+        spaced[p * SPACED : p * SPACED + PIECE, :] = rows[p * PIECE : (p + 1) * PIECE, :]
+
+
+def setup_kernel(lv, cd, st, kl, kv, wup, wfix, mask):
     lane = lax.broadcasted_iota(jnp.int32, (8, 128), 1)
     row = lax.broadcasted_iota(jnp.int32, (8, 128), 0)
     z = lane % NZ
@@ -198,11 +200,17 @@
 FOUR = ((1, 3), (1, 3), (2, 2), (2, 2))
 
 
-def first_kernel(guess, force, far, near, kv, wup, wfix, mask, own, state, send_near, send_far, fwin, a, b):
+def chunks():
+    for t in range(C * OWN // CHUNK):
+        c, x = divmod(t * CHUNK, OWN)
+        p, r = divmod(t * CHUNK, PIECE)
+        yield c, x, p, r
+
+
+def first_kernel(own, force, far, near, kv, wup, wfix, mask, state, send_near, send_far, fwin, a, b):
     clear_edges(a)
     clear_edges(b)
     clear_edges(fwin)
-    take_guess(guess, own)
     a[:, BASE : BASE + OWN, :] = own[...]
     fwin[:, BASE : BASE + OWN, :] = force[...]
     put_halo(a, near, far, HALO, 0)
@@ -219,25 +227,17 @@
     put_halo(a, near, far, HALO, 0)
     steps((a, b), fwin, FOUR, (kv, wup, wfix, mask))
     use = jnp.where(lax.axis_index("tm") > 0, F32(1.0), F32(0.0))
-    tiles = OWN // 8
-    for t in range(GROUP * PIECE // 8):
-        p, r = divmod(t, PIECE // 8)
-        here = pl.ds(p * WIDE + r * 8, 8)
-        there = pl.ds(p * WIDE + PIECE + r * 8, 8)
-        if t < C * tiles:
-            c, x = divmod(t, tiles)
-            u = state[c, x * 8 : x * 8 + 8, :]
-            v = a[c, BASE + x * 8 : BASE + x * 8 + 8, :]
-            out[here, :] = v - use * (gain[t * 8 : t * 8 + 8, :] * u)
-            out[there, :] = u
-        else:
-            out[here, :] = jnp.zeros((8, 128), F32)
-            out[there, :] = jnp.zeros((8, 128), F32)
+    for c, x, p, r in chunks():
+        u = state[c, x : x + CHUNK, :]
+        v = a[c, BASE + x : BASE + x + CHUNK, :]
+        row = p * WIDE + r
+        out[row : row + CHUNK, :] = v - use * (gain[c * OWN + x : c * OWN + x + CHUNK, :] * u)
+        out[row + PIECE : row + PIECE + CHUNK, :] = u
 
 
 def my_gain(gain):
     place = GROUP - 1 - lax.axis_index("tm") % GROUP
-    return gain[pl.ds(pl.multiple_of(place * PIECE, 8), PIECE), :]
+    return gain[pl.ds(pl.multiple_of(place * SPACED, 8), PIECE), :]
 
 
 def slot(i, width=PIECE, half=0):
@@ -295,11 +295,8 @@
 
     @pl.when(jnp.logical_not(first))
     def _():
-        tiles = OWN // 8
-        for t in range(C * tiles):
-            c, x = divmod(t, tiles)
-            p, r = divmod(t, PIECE // 8)
-            state[c, x * 8 : x * 8 + 8, :] = pieces[p * WIDE + r * 8 : p * WIDE + r * 8 + 8, :]
+        for c, x, p, r in chunks():
+            state[c, x : x + CHUNK, :] = pieces[p * WIDE + r : p * WIDE + r + CHUNK, :]
 
     put_sends(pack(state, 0, THREE, 0), pack(state, OWN - THREE, THREE, 0), near, far)
 
@@ -321,10 +318,9 @@
         steps((src, dst), fwin, (one,), (kv, wup, wfix, mask))
         emit(dst, j + 1)
     late = lax.axis_index("tm") >= 1
-    for t in range(C * OWN // 8):
-        p, r = divmod(t, PIECE // 8)
-        start = p * WIDE + PIECE + r * 8
-        corr[t * 8 : t * 8 + 8, :] = jnp.where(late, pieces[start : start + 8, :], 0.0)
+    for c, x, p, r in chunks():
+        row, start = c * OWN + x, p * WIDE + PIECE + r
+        corr[row : row + CHUNK, :] = jnp.where(late, pieces[start : start + CHUNK, :], 0.0)
 
 
 WORK = [pltpu.VMEM((C, WIN, 128), F32), pltpu.VMEM((C, WIN, 128), F32)]
@@ -337,7 +333,7 @@
         in_specs=place or [VMEM] * len(ins),
         out_specs=[VMEM] * len(outs),
         scratch_shapes=list(scratch),
-        compiler_params=pltpu.CompilerParams(vmem_limit_bytes=grant * 1024 * 1024),
+        compiler_params=pltpu.CompilerParams(vmem_limit_bytes=int(grant * 1024 * 1024)),
         name=kernel.__name__,
     )(*ins)
 
@@ -355,7 +351,7 @@
     count = lax.axis_size("tm")
     firsts = [i for i in range(count) if (i // stride) % GROUP == 0]
     groups = [[i + stride * j for j in reversed(range(GROUP))] for i in firsts]
-    slots = value.reshape(GROUP, -1, 128)
+    slots = value.reshape(GROUP, -1)
     return lax.all_to_all(slots, "tm", 0, 0, tiled=True, axis_index_groups=groups).reshape(value.shape)
 
 
@@ -365,36 +361,36 @@
     slab = arr(C, OWN, 128)
     wide, four, three = (arr(C * n, 128) for n in (HALO + THREE, HALO, THREE))
     pieces, double = arr(GROUP * PIECE, 128), arr(GROUP * WIDE, 128)
-    near, far = call(
+    own, force, near, far = call(
         prep_kernel,
         [rows, forcing],
-        [wide, wide],
-        [pltpu.VMEM(slab.shape, F32), pltpu.VMEM(slab.shape, F32), pltpu.VMEM(rows.shape, F32), pltpu.VMEM(forcing.shape, F32), pltpu.SemaphoreType.DMA((2,))],
+        [slab, slab, wide, wide],
+        [pltpu.VMEM(rows.shape, F32), pltpu.VMEM(forcing.shape, F32), pltpu.SemaphoreType.DMA((2,))],
         [HBM] * 2,
-        60,
+        53.25,
     )
     near, far = exchange(near, far)
     small = (kernel_levels, kernel_code, settle_levels, settle_class)
-    force, *coefs = call(
+    coefs = call(
         setup_kernel,
-        [forcing, *small],
-        [slab, arr(C * C, 8, 128), arr(C, 8, 128), arr(3, 8, 128), arr(WIN // 8, 8, 128)],
-        place=[VMEM] + [SMEM] * len(small),
-    )
-    (gain,) = call(gain_kernel, [coarse_gain], [pieces])
-    own, state, near, far, fwin = call(
+        list(small),
+        [arr(C * C, 8, 128), arr(C, 8, 128), arr(3, 8, 128), arr(WIN // 8, 8, 128)],
+        place=[SMEM] * len(small),
+    )
+    gain, spaced = call(gain_kernel, [coarse_gain], [pieces, arr(GROUP * SPACED, 128)])
+    state, near, far, fwin = call(
         first_kernel,
-        [rows, force, far, near, *coefs],
-        [slab, slab, four, four, arr(C, WIN, 128)],
+        [own, force, far, near, *coefs],
+        [slab, four, four, arr(C, WIN, 128)],
         WORK,
     )
     near, far = exchange(near, far)
     (element,) = call(second_kernel, [state, far, near, fwin, gain, *coefs], [double], WORK)
     spread = swap(element, 1)
-    sums, totals, tail = call(local_kernel, [spread, gain], [pieces, pieces, arr(WIDE, 128)])
+    sums, totals, tail = call(local_kernel, [spread, spaced], [pieces, pieces, arr(WIDE, 128)])
     totals = swap(totals, GROUP)
     tail = lax.ppermute(tail, "tm", [(i, i + GROUP) for i in range(intervals - GROUP)])
-    (back,) = call(prefix_kernel, [totals, tail, sums, spread, gain], [double])
+    (back,) = call(prefix_kernel, [totals, tail, sums, spread, spaced], [double])
     back = swap(back, 1)
     state, near, far = call(
         gather_kernel, [back, own], [slab, three, three]

time: 76.4 us -> 74.9 us (0.980)
  no operation moved by 1% of the time
where the time goes in v6:
time: 74.9 us; the launch traced here: 73.8 us
  starting transfers between devices  29.2 us (39%)
  blocking collectives  22.5 us (30%)
  waiting for transfers between devices  13 us (17%)
  Pallas kernels  8.19 us (11%)
  between operations  0.81 us (1%)
    all_to_all x2, blocking collectives, swap(): lax.all_to_all(slots, 'tm', 0, 0, tiled=True, axis_index_groups=groups)  22.5 us
    all_to_all x1, starting transfers between devices, swap(): lax.all_to_all(slots, 'tm', 0, 0, tiled=True, axis_index_groups=groups)  11.4 us
    ppermute x1, waiting for transfers between devices, shards(): lax.ppermute(tail, 'tm', [(i, i + GROUP) for i in range(intervals - GROUP)])  8.82 us
    pallas_call x9, Pallas kernels, call(): pl.pallas_call(kernel, out_shape=outs, in_specs=place or [VMEM] * len(ins...  8.19 us
    ppermute x3, starting transfers between devices, exchange(): far = lax.ppermute(far, 'space', outer)  7.73 us
    ppermute x3, starting transfers between devices, exchange(): near = lax.ppermute(near, 'space', inner)  5.76 us
    ppermute x1, starting transfers between devices, shards(): lax.ppermute(tail, 'tm', [(i, i + GROUP) for i in range(intervals - GROUP)])  4.25 us
    ppermute x3, waiting for transfers between devices, exchange(): far = lax.ppermute(far, 'space', outer)  3.96 us
  transfers between devices with their start and end apart: 8, of which 5 were waited for; matrix products, arithmetic and copies ran while one was open for 0% of the time, Pallas kernels for 1%

profile of v6, /device:TPU:56, one launch (start us, length us, event | category | flops | bytes accessed | tf_op | source)
XLA Modules:
  0.0 73.8 jit_solution(9313991956054749618)
XLA Ops:
  0.6 0.0 copy-start.1
  0.6 1.2 %prep_kernel.1 = (f32[12,24,128]{2,1,0:T(8,128)S(1)}, f32[12,24,128]{2,1,0:T(8,128)S(1)}, f32[336,128]{1,0:T(8,128)S(1)}, f32[336,128]{1,0:T(8,128)S(1)}) custom-call(f32[1152,128]{1,0:T(8,128)} %bitcast.24, f32[12,6,512]{2,1,0:T(8,128)} %forcing.1), custom_call_target="tpu_custom_call" | custom-call | tf_op jit(solution)/shard_map/prep_kernel/pallas_call | solution.py:330
  1.9 0.0 copy-start.2
  1.9 0.0 copy-start.3
  1.9 0.0 copy-start.4
  1.9 2.8 %collective-permute-start = (f32[336,128]{1,0:T(8,128)S(1)}, f32[336,128]{1,0:T(8,128)S(1)}, u32[]{:S(2)}, u32[]{:S(2)}) collective-permute-start(f32[336,128]{1,0:T(8,128)S(1)} %get-tuple-element.26), channel_id=1, source_target_pairs={{1,2},{2,1},{3,4},{4,3},{5,6},{6,5},{9,10},{10,9},{11,12},{12,11},... | collective-permute-start | bytes 516104 | tf_op jit(solution)/shard_map/ppermute | solution.py:345
  4.8 1.9 %collective-permute-start.1 = (f32[336,128]{1,0:T(8,128)S(1)}, f32[336,128]{1,0:T(8,128)S(1)}, u32[]{:S(2)}, u32[]{:S(2)}) collective-permute-start(f32[336,128]{1,0:T(8,128)S(1)} %get-tuple-element.27), channel_id=1, source_target_pairs={{0,1},{1,0},{2,3},{3,2},{4,5},{5,4},{6,7},{7,6},{8,9},{9,8},{10,11... | collective-permute-start | bytes 516104 | tf_op jit(solution)/shard_map/ppermute | solution.py:346
  6.7 0.0 copy-done.1
  6.7 0.0 copy-done.2
  6.7 0.0 copy-done.3
  6.7 0.0 copy-done.4
  6.7 0.9 %setup_kernel.1 = (f32[144,8,128]{2,1,0:T(8,128)S(1)}, f32[12,8,128]{2,1,0:T(8,128)S(1)}, f32[3,8,128]{2,1,0:T(8,128)S(1)}, f32[8,8,128]{2,1,0:T(8,128)S(1)}) custom-call(f32[8]{0:T(128)S(1)} %copy-done.2, s32[12,12]{1,0:T(8,128)S(1)} %copy-done.1, f32[4]{0:T(128)S(1)} %copy-done.3, s32[12]{0:T(128)S(1)} %copy-done.4), custom_call_target="tpu_custom_call" | custom-call | tf_op jit(solution)/shard_map/setup_kernel/pallas_call | solution.py:330
  7.6 1.2 %collective-permute-done.far = f32[336,128]{1,0:T(8,128)S(1)} collective-permute-done((f32[336,128]{1,0:T(8,128)S(1)}, f32[336,128]{1,0:T(8,128)S(1)}, u32[]{:S(2)}, u32[]{:S(2)}) %collective-permute-start) | collective-permute-done | bytes 172064 | tf_op jit(solution)/shard_map/ppermute | solution.py:345
  8.8 0.0 collective-permute-done.1.near
  8.8 0.0 copy-start
  8.8 1.6 %first_kernel.1 = (f32[12,24,128]{2,1,0:T(8,128)S(1)}, f32[192,128]{1,0:T(8,128)S(1)}, f32[192,128]{1,0:T(8,128)S(1)}, f32[12,64,128]{2,1,0:T(8,128)S(1)}) custom-call(f32[12,24,128]{2,1,0:T(8,128)S(1)} %get-tuple-element.24.own, f32[12,24,128]{2,1,0:T(8,128)S(1)} %get-tuple-element.25.force, f32[336,128]{1,0:T(8,128)S(1)} %collective-permute-done.far, ...), custom_call_target="tpu_custom_call" | custom-call | tf_op jit(solution)/shard_map/first_kernel/pallas_call | solution.py:330
  10.4 3.0 %collective-permute-start.2 = (f32[192,128]{1,0:T(8,128)S(1)}, f32[192,128]{1,0:T(8,128)S(1)}, u32[]{:S(2)}, u32[]{:S(2)}) collective-permute-start(f32[192,128]{1,0:T(8,128)S(1)} %get-tuple-element.33), channel_id=1, source_target_pairs={{1,2},{2,1},{3,4},{4,3},{5,6},{6,5},{9,10},{10,9},{11,12},{12,11},... | collective-permute-start | bytes 294920 | tf_op jit(solution)/shard_map/ppermute | solution.py:345
  13.4 1.9 %collective-permute-start.3 = (f32[192,128]{1,0:T(8,128)S(1)}, f32[192,128]{1,0:T(8,128)S(1)}, u32[]{:S(2)}, u32[]{:S(2)}) collective-permute-start(f32[192,128]{1,0:T(8,128)S(1)} %get-tuple-element.34), channel_id=1, source_target_pairs={{0,1},{1,0},{2,3},{3,2},{4,5},{5,4},{6,7},{7,6},{8,9},{9,8},{10,11... | collective-permute-start | bytes 294920 | tf_op jit(solution)/shard_map/ppermute | solution.py:346
  15.3 0.0 copy-done
  15.4 1.0 %collective-permute-done.2.far = f32[192,128]{1,0:T(8,128)S(1)} collective-permute-done((f32[192,128]{1,0:T(8,128)S(1)}, f32[192,128]{1,0:T(8,128)S(1)}, u32[]{:S(2)}, u32[]{:S(2)}) %collective-permute-start.2) | collective-permute-done | bytes 98336 | tf_op jit(solution)/shard_map/ppermute | solution.py:345
  16.3 0.3 collective-permute-done.3.near
  16.6 1.6 %second_kernel.1 = f32[576,128]{1,0:T(8,128)S(1)} custom-call(f32[12,24,128]{2,1,0:T(8,128)S(1)} %get-tuple-element.32.state, f32[192,128]{1,0:T(8,128)S(1)} %collective-permute-done.2.far, f32[192,128]{1,0:T(8,128)S(1)} %collective-permute-done.3.near, f32[12,64,128]{2,1,0:T(8,128)S(1)} %get-tuple-element.35.fwin, f32[288,128]{1,0:T(8,128)S(1)} %get-tuple-element.36.gain, ...), custom_call_target="tpu_custom_call" | custom-call | tf_op jit(solution)/shard_map/second_kernel/pallas_call | solution.py:330
  18.2 12.5 %all_to_all.27 = f32[8,1,9216]{2,1,0:T(1,128)S(1)} all-to-all(f32[8,1,9216]{2,1,0:T(1,128)S(1)} %bitcast.21), channel_id=1, replica_groups={{56,48,40,32,24,16,8,0},{120,112,104,96,88,80,72,64},{184,176,168,160,1..., dimensions={0} | all-to-all | bytes 589824 | tf_op jit(solution)/shard_map/all_to_all | solution.py:355
  30.7 0.7 local_kernel.1
  31.4 11.4 %all-to-all-start.1 = ((f32[8,1,4608]{2,1,0:T(1,128)}), f32[8,1,4608]{2,1,0:T(1,128)S(1)}, u32[]{:S(2)}, u32[]{:S(2)}) async-start(f32[8,1,4608]{2,1,0:T(1,128)} %bitcast.5), calls=%async_computation.1 | async-start | bytes 294912 | tf_op jit(solution)/shard_map/all_to_all | solution.py:355
  42.8 4.3 %collective-permute-start.4 = (f32[72,128]{1,0:T(8,128)S(1)}, f32[72,128]{1,0:T(8,128)S(1)}, u32[]{:S(2)}, u32[]{:S(2)}) collective-permute-start(f32[72,128]{1,0:T(8,128)S(1)} %get-tuple-element.39), channel_id=1, source_target_pairs={{0,64},{8,72},{16,80},{24,88},{32,96},{40,104},{48,112},{56,120},{... | collective-permute-start | bytes 110600 | tf_op jit(solution)/shard_map/ppermute | solution.py:392
  47.0 8.8 %collective-permute-done.4.tail = f32[72,128]{1,0:T(8,128)S(1)} collective-permute-done((f32[72,128]{1,0:T(8,128)S(1)}, f32[72,128]{1,0:T(8,128)S(1)}, u32[]{:S(2)}, u32[]{:S(2)}) %collective-permute-start.4) | collective-permute-done | bytes 36896 | tf_op jit(solution)/shard_map/ppermute | solution.py:392
  55.9 0.0 all-to-all-done.1
  55.9 0.1 prefix_kernel.1
  55.9 10.1 %all_to_all.28 = f32[8,1,9216]{2,1,0:T(1,128)S(1)} all-to-all(f32[8,1,9216]{2,1,0:T(1,128)S(1)} %bitcast.22), channel_id=1, replica_groups={{56,48,40,32,24,16,8,0},{120,112,104,96,88,80,72,64},{184,176,168,160,1..., dimensions={0} | all-to-all | bytes 589824 | tf_op jit(solution)/shard_map/all_to_all | solution.py:355
  66.0 1.9 %collective-permute-start.5 = (f32[144,128]{1,0:T(8,128)S(1)}, f32[144,128]{1,0:T(8,128)S(1)}, u32[]{:S(2)}, u32[]{:S(2)}) collective-permute-start(f32[144,128]{1,0:T(8,128)S(1)} %get-tuple-element.42), channel_id=1, source_target_pairs={{1,2},{2,1},{3,4},{4,3},{5,6},{6,5},{9,10},{10,9},{11,12},{12,11},... | collective-permute-start | bytes 221192 | tf_op jit(solution)/shard_map/ppermute | solution.py:345
  68.0 1.9 %collective-permute-start.6 = (f32[144,128]{1,0:T(8,128)S(1)}, f32[144,128]{1,0:T(8,128)S(1)}, u32[]{:S(2)}, u32[]{:S(2)}) collective-permute-start(f32[144,128]{1,0:T(8,128)S(1)} %get-tuple-element.43), channel_id=1, source_target_pairs={{0,1},{1,0},{2,3},{3,2},{4,5},{5,4},{6,7},{7,6},{8,9},{9,8},{10,11... | collective-permute-start | bytes 221192 | tf_op jit(solution)/shard_map/ppermute | solution.py:346
  69.9 1.8 %collective-permute-done.5.far = f32[144,128]{1,0:T(8,128)S(1)} collective-permute-done((f32[144,128]{1,0:T(8,128)S(1)}, f32[144,128]{1,0:T(8,128)S(1)}, u32[]{:S(2)}, u32[]{:S(2)}) %collective-permute-start.5) | collective-permute-done | bytes 73760 | tf_op jit(solution)/shard_map/ppermute | solution.py:345
  71.7 0.0 collective-permute-done.6.near
  71.7 2.1 %last_kernel.1 = (f32[1152,128]{1,0:T(8,128)}, f32[288,128]{1,0:T(8,128)}) custom-call(f32[12,24,128]{2,1,0:T(8,128)S(1)} %get-tuple-element.41.state, f32[144,128]{1,0:T(8,128)S(1)} %collective-permute-done.5.far, f32[144,128]{1,0:T(8,128)S(1)} %collective-permute-done.6.near, f32[12,64,128]{2,1,0:T(8,128)S(1)} %get-tuple-element.35.fwin, ...), custom_call_target="tpu_custom_call" | custom-call | tf_op jit(solution)/shard_map/last_kernel/pallas_call | solution.py:330
  (2 shorter events, 0.1 us)
Async XLA Ops:
  0.6 6.1 %copy-start.1 = (s32[12,12]{1,0:T(8,128)S(1)}, s32[12,12]{1,0:T(8,128)}, u32[]{:S(2)}) copy-start(s32[12,12]{1,0:T(8,128)} %cd.1) | copy-start | bytes 1732
  1.9 4.8 %copy-start.2 = (f32[8]{0:T(128)S(1)}, f32[8]{0:T(128)}, u32[]{:S(2)}) copy-start(f32[8]{0:T(128)} %lv.1) | copy-start | bytes 100
  1.9 4.8 %copy-start.3 = (f32[4]{0:T(128)S(1)}, f32[4]{0:T(128)}, u32[]{:S(2)}) copy-start(f32[4]{0:T(128)} %st.1) | copy-start | bytes 52
  1.9 4.8 %copy-start.4 = (s32[12]{0:T(128)S(1)}, s32[12]{0:T(128)}, u32[]{:S(2)}) copy-start(s32[12]{0:T(128)} %kl.1) | copy-start | bytes 148
  1.9 6.9 %collective-permute-start = (f32[336,128]{1,0:T(8,128)S(1)}, f32[336,128]{1,0:T(8,128)S(1)}, u32[]{:S(2)}, u32[]{:S(2)}) collective-permute-start(f32[336,128]{1,0:T(8,128)S(1)} %get-tuple-element.26), channel_id=1, source_target_pairs={{1,2},{2,1},{3,4},{4,3},{5,6},{6,5},{9,10},{10,9},{11,12},{12,11},... | collective-permute-start | bytes 516104 | tf_op jit(solution)/shard_map/ppermute | solution.py:345
  4.8 4.0 %collective-permute-start.1 = (f32[336,128]{1,0:T(8,128)S(1)}, f32[336,128]{1,0:T(8,128)S(1)}, u32[]{:S(2)}, u32[]{:S(2)}) collective-permute-start(f32[336,128]{1,0:T(8,128)S(1)} %get-tuple-element.27), channel_id=1, source_target_pairs={{0,1},{1,0},{2,3},{3,2},{4,5},{5,4},{6,7},{7,6},{8,9},{9,8},{10,11... | collective-permute-start | bytes 516104 | tf_op jit(solution)/shard_map/ppermute | solution.py:346
  8.8 6.5 %copy-start = (f32[12,6,512]{2,1,0:T(8,128)S(1)}, f32[12,6,512]{2,1,0:T(8,128)}, u32[]{:S(2)}) copy-start(f32[12,6,512]{2,1,0:T(8,128)} %raw.1) | copy-start | bytes 442372
  10.4 5.9 %collective-permute-start.2 = (f32[192,128]{1,0:T(8,128)S(1)}, f32[192,128]{1,0:T(8,128)S(1)}, u32[]{:S(2)}, u32[]{:S(2)}) collective-permute-start(f32[192,128]{1,0:T(8,128)S(1)} %get-tuple-element.33), channel_id=1, source_target_pairs={{1,2},{2,1},{3,4},{4,3},{5,6},{6,5},{9,10},{10,9},{11,12},{12,11},... | collective-permute-start | bytes 294920 | tf_op jit(solution)/shard_map/ppermute | solution.py:345
  13.4 3.2 %collective-permute-start.3 = (f32[192,128]{1,0:T(8,128)S(1)}, f32[192,128]{1,0:T(8,128)S(1)}, u32[]{:S(2)}, u32[]{:S(2)}) collective-permute-start(f32[192,128]{1,0:T(8,128)S(1)} %get-tuple-element.34), channel_id=1, source_target_pairs={{0,1},{1,0},{2,3},{3,2},{4,5},{5,4},{6,7},{7,6},{8,9},{9,8},{10,11... | collective-permute-start | bytes 294920 | tf_op jit(solution)/shard_map/ppermute | solution.py:346
  31.4 24.5 %all-to-all-start.1 = ((f32[8,1,4608]{2,1,0:T(1,128)}), f32[8,1,4608]{2,1,0:T(1,128)S(1)}, u32[]{:S(2)}, u32[]{:S(2)}) async-start(f32[8,1,4608]{2,1,0:T(1,128)} %bitcast.5), calls=%async_computation.1 | async-start | bytes 294912 | tf_op jit(solution)/shard_map/all_to_all | solution.py:355
  42.8 13.1 %collective-permute-start.4 = (f32[72,128]{1,0:T(8,128)S(1)}, f32[72,128]{1,0:T(8,128)S(1)}, u32[]{:S(2)}, u32[]{:S(2)}) collective-permute-start(f32[72,128]{1,0:T(8,128)S(1)} %get-tuple-element.39), channel_id=1, source_target_pairs={{0,64},{8,72},{16,80},{24,88},{32,96},{40,104},{48,112},{56,120},{... | collective-permute-start | bytes 110600 | tf_op jit(solution)/shard_map/ppermute | solution.py:392
  66.0 5.7 %collective-permute-start.5 = (f32[144,128]{1,0:T(8,128)S(1)}, f32[144,128]{1,0:T(8,128)S(1)}, u32[]{:S(2)}, u32[]{:S(2)}) collective-permute-start(f32[144,128]{1,0:T(8,128)S(1)} %get-tuple-element.42), channel_id=1, source_target_pairs={{1,2},{2,1},{3,4},{4,3},{5,6},{6,5},{9,10},{10,9},{11,12},{12,11},... | collective-permute-start | bytes 221192 | tf_op jit(solution)/shard_map/ppermute | solution.py:345
  68.0 3.7 %collective-permute-start.6 = (f32[144,128]{1,0:T(8,128)S(1)}, f32[144,128]{1,0:T(8,128)S(1)}, u32[]{:S(2)}, u32[]{:S(2)}) collective-permute-start(f32[144,128]{1,0:T(8,128)S(1)} %get-tuple-element.43), channel_id=1, source_target_pairs={{0,1},{1,0},{2,3},{3,2},{4,5},{5,4},{6,7},{7,6},{8,9},{9,8},{10,11... | collective-permute-start | bytes 221192 | tf_op jit(solution)/shard_map/ppermute | solution.py:346

commit v7 on v6

--- a/solution.py
+++ b/solution.py
@@ -21,6 +21,8 @@
 WIN = 64
 BASE = 5 * ROWS
 GROUP = 8
+DOWN = (7, 6, 5, 4, 3, 2, 1, 0)
+MIDDLE = (4, 7, 6, 5, 3, 2, 1, 0)
 PIECE = C * OWN // GROUP
 WIDE = 2 * PIECE
 SPACED = 40
@@ -256,7 +258,7 @@
             tail[:PIECE, :] = running
     tail[PIECE:, :] = pieces[slot(GROUP - 1, WIDE, 1), :]
     for i in range(GROUP):
-        total[slot(i), :] = running
+        total[i * PIECE : (i + 1) * PIECE, :] = running
 
 
 def prefix_kernel(totals, tail, sums, pieces, gain, out):
@@ -270,7 +272,8 @@
     for g in range(GROUP - 1):
         take = g < group
         ahead = jnp.where(take, before, ahead)
-        before = jnp.where(take, g8 * before + totals[slot(g), :], before)
+        start = MIDDLE.index(g) * PIECE
+        before = jnp.where(take, g8 * before + totals[start : start + PIECE, :], before)
     for i in range(GROUP):
         if i == 0:
             base = tail[PIECE:, :]
@@ -347,10 +350,10 @@
     return near, far
 
 
-def swap(value, stride):
+def swap(value, stride, order):
     count = lax.axis_size("tm")
     firsts = [i for i in range(count) if (i // stride) % GROUP == 0]
-    groups = [[i + stride * j for j in reversed(range(GROUP))] for i in firsts]
+    groups = [[i + stride * j for j in order] for i in firsts]
     slots = value.reshape(GROUP, -1)
     return lax.all_to_all(slots, "tm", 0, 0, tiled=True, axis_index_groups=groups).reshape(value.shape)
 
@@ -386,12 +389,12 @@
     )
     near, far = exchange(near, far)
     (element,) = call(second_kernel, [state, far, near, fwin, gain, *coefs], [double], WORK)
-    spread = swap(element, 1)
+    spread = swap(element, 1, DOWN)
     sums, totals, tail = call(local_kernel, [spread, spaced], [pieces, pieces, arr(WIDE, 128)])
-    totals = swap(totals, GROUP)
+    totals = swap(totals, GROUP, MIDDLE)
     tail = lax.ppermute(tail, "tm", [(i, i + GROUP) for i in range(intervals - GROUP)])
     (back,) = call(prefix_kernel, [totals, tail, sums, spread, spaced], [double])
-    back = swap(back, 1)
+    back = swap(back, 1, DOWN)
     state, near, far = call(
         gather_kernel, [back, own], [slab, three, three]
     )

time: 74.9 us -> 76.1 us (1.016)
  the two profiles are of different devices: /device:TPU:56 before, /device:TPU:1 now
where the time goes in v7:
time: 76.1 us; the launch traced here: 75.7 us
  starting transfers between devices  40.7 us (53%)
  blocking collectives  18.9 us (25%)
  Pallas kernels  8.19 us (11%)
  waiting for transfers between devices  7.01 us (9%)
  between operations  0.82 us (1%)
    all_to_all x2, blocking collectives, swap(): lax.all_to_all(slots, 'tm', 0, 0, tiled=True, axis_index_groups=groups)  18.9 us
    all_to_all x1, starting transfers between devices, swap(): lax.all_to_all(slots, 'tm', 0, 0, tiled=True, axis_index_groups=groups)  14.2 us
    ppermute x3, starting transfers between devices, exchange(): far = lax.ppermute(far, 'space', outer)  13.8 us
    ppermute x3, starting transfers between devices, exchange(): near = lax.ppermute(near, 'space', inner)  8.7 us
    pallas_call x9, Pallas kernels, call(): pl.pallas_call(kernel, out_shape=outs, in_specs=place or [VMEM] * len(ins...  8.19 us
    ppermute x1, starting transfers between devices, shards(): lax.ppermute(tail, 'tm', [(i, i + GROUP) for i in range(intervals - GROUP)])  3.97 us
    all_to_all x1, waiting for transfers between devices, swap(): lax.all_to_all(slots, 'tm', 0, 0, tiled=True, axis_index_groups=groups)  2.6 us
    ppermute x3, waiting for transfers between devices, exchange(): far = lax.ppermute(far, 'space', outer)  2.12 us
  transfers between devices with their start and end apart: 8, of which 6 were waited for; matrix products, arithmetic and copies ran while one was open for 0% of the time, Pallas kernels for 1%

profile of v7, /device:TPU:1, one launch (start us, length us, event | category | flops | bytes accessed | tf_op | source)
XLA Modules:
  0.0 75.7 jit_solution(1618759219682997185)
XLA Ops:
  0.6 0.0 copy-start.1
  0.6 1.2 %prep_kernel.1 = (f32[12,24,128]{2,1,0:T(8,128)S(1)}, f32[12,24,128]{2,1,0:T(8,128)S(1)}, f32[336,128]{1,0:T(8,128)S(1)}, f32[336,128]{1,0:T(8,128)S(1)}) custom-call(f32[1152,128]{1,0:T(8,128)} %bitcast.24, f32[12,6,512]{2,1,0:T(8,128)} %forcing.1), custom_call_target="tpu_custom_call" | custom-call | tf_op jit(solution)/shard_map/prep_kernel/pallas_call | solution.py:333
  1.9 0.0 copy-start.2
  1.9 0.0 copy-start.3
  1.9 0.0 copy-start.4
  1.9 4.7 %collective-permute-start = (f32[336,128]{1,0:T(8,128)S(1)}, f32[336,128]{1,0:T(8,128)S(1)}, u32[]{:S(2)}, u32[]{:S(2)}) collective-permute-start(f32[336,128]{1,0:T(8,128)S(1)} %get-tuple-element.26), channel_id=1, source_target_pairs={{1,2},{2,1},{3,4},{4,3},{5,6},{6,5},{9,10},{10,9},{11,12},{12,11},... | collective-permute-start | bytes 516104 | tf_op jit(solution)/shard_map/ppermute | solution.py:348
  6.7 4.9 %collective-permute-start.1 = (f32[336,128]{1,0:T(8,128)S(1)}, f32[336,128]{1,0:T(8,128)S(1)}, u32[]{:S(2)}, u32[]{:S(2)}) collective-permute-start(f32[336,128]{1,0:T(8,128)S(1)} %get-tuple-element.27), channel_id=1, source_target_pairs={{0,1},{1,0},{2,3},{3,2},{4,5},{5,4},{6,7},{7,6},{8,9},{9,8},{10,11... | collective-permute-start | bytes 516104 | tf_op jit(solution)/shard_map/ppermute | solution.py:349
  11.5 0.0 copy-done.1
  11.5 0.0 copy-done.2
  11.5 0.0 copy-done.3
  11.6 0.0 copy-done.4
  11.6 0.9 %setup_kernel.1 = (f32[144,8,128]{2,1,0:T(8,128)S(1)}, f32[12,8,128]{2,1,0:T(8,128)S(1)}, f32[3,8,128]{2,1,0:T(8,128)S(1)}, f32[8,8,128]{2,1,0:T(8,128)S(1)}) custom-call(f32[8]{0:T(128)S(1)} %copy-done.2, s32[12,12]{1,0:T(8,128)S(1)} %copy-done.1, f32[4]{0:T(128)S(1)} %copy-done.3, s32[12]{0:T(128)S(1)} %copy-done.4), custom_call_target="tpu_custom_call" | custom-call | tf_op jit(solution)/shard_map/setup_kernel/pallas_call | solution.py:333
  12.4 0.0 collective-permute-done.far
  12.4 0.1 collective-permute-done.1.near
  12.5 0.0 copy-start
  12.5 1.6 %first_kernel.1 = (f32[12,24,128]{2,1,0:T(8,128)S(1)}, f32[192,128]{1,0:T(8,128)S(1)}, f32[192,128]{1,0:T(8,128)S(1)}, f32[12,64,128]{2,1,0:T(8,128)S(1)}) custom-call(f32[12,24,128]{2,1,0:T(8,128)S(1)} %get-tuple-element.24.own, f32[12,24,128]{2,1,0:T(8,128)S(1)} %get-tuple-element.25.force, f32[336,128]{1,0:T(8,128)S(1)} %collective-permute-done.far, ...), custom_call_target="tpu_custom_call" | custom-call | tf_op jit(solution)/shard_map/first_kernel/pallas_call | solution.py:333
  14.2 1.9 %collective-permute-start.2 = (f32[192,128]{1,0:T(8,128)S(1)}, f32[192,128]{1,0:T(8,128)S(1)}, u32[]{:S(2)}, u32[]{:S(2)}) collective-permute-start(f32[192,128]{1,0:T(8,128)S(1)} %get-tuple-element.33), channel_id=1, source_target_pairs={{1,2},{2,1},{3,4},{4,3},{5,6},{6,5},{9,10},{10,9},{11,12},{12,11},... | collective-permute-start | bytes 294920 | tf_op jit(solution)/shard_map/ppermute | solution.py:348
  16.1 1.9 %collective-permute-start.3 = (f32[192,128]{1,0:T(8,128)S(1)}, f32[192,128]{1,0:T(8,128)S(1)}, u32[]{:S(2)}, u32[]{:S(2)}) collective-permute-start(f32[192,128]{1,0:T(8,128)S(1)} %get-tuple-element.34), channel_id=1, source_target_pairs={{0,1},{1,0},{2,3},{3,2},{4,5},{5,4},{6,7},{7,6},{8,9},{9,8},{10,11... | collective-permute-start | bytes 294920 | tf_op jit(solution)/shard_map/ppermute | solution.py:349
  18.0 0.0 copy-done
  18.1 2.0 %collective-permute-done.2.far = f32[192,128]{1,0:T(8,128)S(1)} collective-permute-done((f32[192,128]{1,0:T(8,128)S(1)}, f32[192,128]{1,0:T(8,128)S(1)}, u32[]{:S(2)}, u32[]{:S(2)}) %collective-permute-start.2) | collective-permute-done | bytes 98336 | tf_op jit(solution)/shard_map/ppermute | solution.py:348
  20.1 0.0 collective-permute-done.3.near
  20.1 1.6 %second_kernel.1 = f32[576,128]{1,0:T(8,128)S(1)} custom-call(f32[12,24,128]{2,1,0:T(8,128)S(1)} %get-tuple-element.32.state, f32[192,128]{1,0:T(8,128)S(1)} %collective-permute-done.2.far, f32[192,128]{1,0:T(8,128)S(1)} %collective-permute-done.3.near, f32[12,64,128]{2,1,0:T(8,128)S(1)} %get-tuple-element.35.fwin, f32[288,128]{1,0:T(8,128)S(1)} %get-tuple-element.36.gain, ...), custom_call_target="tpu_custom_call" | custom-call | tf_op jit(solution)/shard_map/second_kernel/pallas_call | solution.py:333
  21.7 10.4 %all_to_all.27 = f32[8,1,9216]{2,1,0:T(1,128)S(1)} all-to-all(f32[8,1,9216]{2,1,0:T(1,128)S(1)} %bitcast.21), channel_id=1, replica_groups={{56,48,40,32,24,16,8,0},{120,112,104,96,88,80,72,64},{184,176,168,160,1..., dimensions={0} | all-to-all | bytes 589824 | tf_op jit(solution)/shard_map/all_to_all | solution.py:358
  32.1 0.7 local_kernel.1
  32.8 14.2 %all-to-all-start.1 = ((f32[8,1,4608]{2,1,0:T(1,128)}), f32[8,1,4608]{2,1,0:T(1,128)S(1)}, u32[]{:S(2)}, u32[]{:S(2)}) async-start(f32[8,1,4608]{2,1,0:T(1,128)} %bitcast.5), calls=%async_computation.1 | async-start | bytes 294912 | tf_op jit(solution)/shard_map/all_to_all | solution.py:358
  47.0 4.0 %collective-permute-start.4 = (f32[72,128]{1,0:T(8,128)S(1)}, f32[72,128]{1,0:T(8,128)S(1)}, u32[]{:S(2)}, u32[]{:S(2)}) collective-permute-start(f32[72,128]{1,0:T(8,128)S(1)} %get-tuple-element.39), channel_id=1, source_target_pairs={{0,64},{8,72},{16,80},{24,88},{32,96},{40,104},{48,112},{56,120},{... | collective-permute-start | bytes 110600 | tf_op jit(solution)/shard_map/ppermute | solution.py:395
  51.0 1.0 %collective-permute-done.4.tail = f32[72,128]{1,0:T(8,128)S(1)} collective-permute-done((f32[72,128]{1,0:T(8,128)S(1)}, f32[72,128]{1,0:T(8,128)S(1)}, u32[]{:S(2)}, u32[]{:S(2)}) %collective-permute-start.4) | collective-permute-done | bytes 36896 | tf_op jit(solution)/shard_map/ppermute | solution.py:395
  52.0 2.6 %all-to-all-done.1 = f32[8,1,4608]{2,1,0:T(1,128)S(1)} async-done(((f32[8,1,4608]{2,1,0:T(1,128)}), f32[8,1,4608]{2,1,0:T(1,128)S(1)}, u32[]{:S(2)}, u32[]{:S(2)}) %all-to-all-start.1) | async-done | bytes 147488 | tf_op jit(solution)/shard_map/all_to_all | solution.py:358
  54.6 0.1 prefix_kernel.1
  54.7 8.6 %all_to_all.28 = f32[8,1,9216]{2,1,0:T(1,128)S(1)} all-to-all(f32[8,1,9216]{2,1,0:T(1,128)S(1)} %bitcast.22), channel_id=1, replica_groups={{56,48,40,32,24,16,8,0},{120,112,104,96,88,80,72,64},{184,176,168,160,1..., dimensions={0} | all-to-all | bytes 589824 | tf_op jit(solution)/shard_map/all_to_all | solution.py:358
  63.3 7.1 %collective-permute-start.5 = (f32[144,128]{1,0:T(8,128)S(1)}, f32[144,128]{1,0:T(8,128)S(1)}, u32[]{:S(2)}, u32[]{:S(2)}) collective-permute-start(f32[144,128]{1,0:T(8,128)S(1)} %get-tuple-element.42), channel_id=1, source_target_pairs={{1,2},{2,1},{3,4},{4,3},{5,6},{6,5},{9,10},{10,9},{11,12},{12,11},... | collective-permute-start | bytes 221192 | tf_op jit(solution)/shard_map/ppermute | solution.py:348
  70.4 1.9 %collective-permute-start.6 = (f32[144,128]{1,0:T(8,128)S(1)}, f32[144,128]{1,0:T(8,128)S(1)}, u32[]{:S(2)}, u32[]{:S(2)}) collective-permute-start(f32[144,128]{1,0:T(8,128)S(1)} %get-tuple-element.43), channel_id=1, source_target_pairs={{0,1},{1,0},{2,3},{3,2},{4,5},{5,4},{6,7},{7,6},{8,9},{9,8},{10,11... | collective-permute-start | bytes 221192 | tf_op jit(solution)/shard_map/ppermute | solution.py:349
  72.3 0.1 collective-permute-done.5.far
  72.4 1.1 %collective-permute-done.6.near = f32[144,128]{1,0:T(8,128)S(1)} collective-permute-done((f32[144,128]{1,0:T(8,128)S(1)}, f32[144,128]{1,0:T(8,128)S(1)}, u32[]{:S(2)}, u32[]{:S(2)}) %collective-permute-start.6) | collective-permute-done | bytes 73760 | tf_op jit(solution)/shard_map/ppermute | solution.py:349
  73.6 2.1 %last_kernel.1 = (f32[1152,128]{1,0:T(8,128)}, f32[288,128]{1,0:T(8,128)}) custom-call(f32[12,24,128]{2,1,0:T(8,128)S(1)} %get-tuple-element.41.state, f32[144,128]{1,0:T(8,128)S(1)} %collective-permute-done.5.far, f32[144,128]{1,0:T(8,128)S(1)} %collective-permute-done.6.near, f32[12,64,128]{2,1,0:T(8,128)S(1)} %get-tuple-element.35.fwin, ...), custom_call_target="tpu_custom_call" | custom-call | tf_op jit(solution)/shard_map/last_kernel/pallas_call | solution.py:333
  (2 shorter events, 0.1 us)
Async XLA Ops:
  0.6 10.9 %copy-start.1 = (s32[12,12]{1,0:T(8,128)S(1)}, s32[12,12]{1,0:T(8,128)}, u32[]{:S(2)}) copy-start(s32[12,12]{1,0:T(8,128)} %cd.1) | copy-start | bytes 1732
  1.9 9.7 %copy-start.2 = (f32[8]{0:T(128)S(1)}, f32[8]{0:T(128)}, u32[]{:S(2)}) copy-start(f32[8]{0:T(128)} %lv.1) | copy-start | bytes 100
  1.9 9.7 %copy-start.3 = (f32[4]{0:T(128)S(1)}, f32[4]{0:T(128)}, u32[]{:S(2)}) copy-start(f32[4]{0:T(128)} %st.1) | copy-start | bytes 52
  1.9 9.7 %copy-start.4 = (s32[12]{0:T(128)S(1)}, s32[12]{0:T(128)}, u32[]{:S(2)}) copy-start(s32[12]{0:T(128)} %kl.1) | copy-start | bytes 148
  1.9 10.5 %collective-permute-start = (f32[336,128]{1,0:T(8,128)S(1)}, f32[336,128]{1,0:T(8,128)S(1)}, u32[]{:S(2)}, u32[]{:S(2)}) collective-permute-start(f32[336,128]{1,0:T(8,128)S(1)} %get-tuple-element.26), channel_id=1, source_target_pairs={{1,2},{2,1},{3,4},{4,3},{5,6},{6,5},{9,10},{10,9},{11,12},{12,11},... | collective-permute-start | bytes 516104 | tf_op jit(solution)/shard_map/ppermute | solution.py:348
  6.7 5.9 %collective-permute-start.1 = (f32[336,128]{1,0:T(8,128)S(1)}, f32[336,128]{1,0:T(8,128)S(1)}, u32[]{:S(2)}, u32[]{:S(2)}) collective-permute-start(f32[336,128]{1,0:T(8,128)S(1)} %get-tuple-element.27), channel_id=1, source_target_pairs={{0,1},{1,0},{2,3},{3,2},{4,5},{5,4},{6,7},{7,6},{8,9},{9,8},{10,11... | collective-permute-start | bytes 516104 | tf_op jit(solution)/shard_map/ppermute | solution.py:349
  12.5 5.5 %copy-start = (f32[12,6,512]{2,1,0:T(8,128)S(1)}, f32[12,6,512]{2,1,0:T(8,128)}, u32[]{:S(2)}) copy-start(f32[12,6,512]{2,1,0:T(8,128)} %raw.1) | copy-start | bytes 442372
  14.2 5.9 %collective-permute-start.2 = (f32[192,128]{1,0:T(8,128)S(1)}, f32[192,128]{1,0:T(8,128)S(1)}, u32[]{:S(2)}, u32[]{:S(2)}) collective-permute-start(f32[192,128]{1,0:T(8,128)S(1)} %get-tuple-element.33), channel_id=1, source_target_pairs={{1,2},{2,1},{3,4},{4,3},{5,6},{6,5},{9,10},{10,9},{11,12},{12,11},... | collective-permute-start | bytes 294920 | tf_op jit(solution)/shard_map/ppermute | solution.py:348
  16.1 4.0 %collective-permute-start.3 = (f32[192,128]{1,0:T(8,128)S(1)}, f32[192,128]{1,0:T(8,128)S(1)}, u32[]{:S(2)}, u32[]{:S(2)}) collective-permute-start(f32[192,128]{1,0:T(8,128)S(1)} %get-tuple-element.34), channel_id=1, source_target_pairs={{0,1},{1,0},{2,3},{3,2},{4,5},{5,4},{6,7},{7,6},{8,9},{9,8},{10,11... | collective-permute-start | bytes 294920 | tf_op jit(solution)/shard_map/ppermute | solution.py:349
  32.8 21.8 %all-to-all-start.1 = ((f32[8,1,4608]{2,1,0:T(1,128)}), f32[8,1,4608]{2,1,0:T(1,128)S(1)}, u32[]{:S(2)}, u32[]{:S(2)}) async-start(f32[8,1,4608]{2,1,0:T(1,128)} %bitcast.5), calls=%async_computation.1 | async-start | bytes 294912 | tf_op jit(solution)/shard_map/all_to_all | solution.py:358
  47.0 5.0 %collective-permute-start.4 = (f32[72,128]{1,0:T(8,128)S(1)}, f32[72,128]{1,0:T(8,128)S(1)}, u32[]{:S(2)}, u32[]{:S(2)}) collective-permute-start(f32[72,128]{1,0:T(8,128)S(1)} %get-tuple-element.39), channel_id=1, source_target_pairs={{0,64},{8,72},{16,80},{24,88},{32,96},{40,104},{48,112},{56,120},{... | collective-permute-start | bytes 110600 | tf_op jit(solution)/shard_map/ppermute | solution.py:395
  63.3 9.2 %collective-permute-start.5 = (f32[144,128]{1,0:T(8,128)S(1)}, f32[144,128]{1,0:T(8,128)S(1)}, u32[]{:S(2)}, u32[]{:S(2)}) collective-permute-start(f32[144,128]{1,0:T(8,128)S(1)} %get-tuple-element.42), channel_id=1, source_target_pairs={{1,2},{2,1},{3,4},{4,3},{5,6},{6,5},{9,10},{10,9},{11,12},{12,11},... | collective-permute-start | bytes 221192 | tf_op jit(solution)/shard_map/ppermute | solution.py:348
  70.4 3.2 %collective-permute-start.6 = (f32[144,128]{1,0:T(8,128)S(1)}, f32[144,128]{1,0:T(8,128)S(1)}, u32[]{:S(2)}, u32[]{:S(2)}) collective-permute-start(f32[144,128]{1,0:T(8,128)S(1)} %get-tuple-element.43), channel_id=1, source_target_pairs={{0,1},{1,0},{2,3},{3,2},{4,5},{5,4},{6,7},{7,6},{8,9},{9,8},{10,11... | collective-permute-start | bytes 221192 | tf_op jit(solution)/shard_map/ppermute | solution.py:349

commit v8 on v6

--- a/solution.py
+++ b/solution.py
@@ -83,19 +83,22 @@
         own[c] = raw[pl.ds(c * OWN * SLICES, OWN, stride=SLICES), :]
 
 
-def take_forcing(raw, force):
+def to_rows(raw, rows, scale):
     for c in range(C):
         for r in range(ROWS):
-            force[c, pl.ds(r, PLANES, stride=ROWS), :] = raw[c, :, 128 * r : 128 * r + 128] * 0.1
-
-
-def prep_kernel(guess, forcing, own, force, near, far, raw, fraw, sems):
+            value = raw[c, :, 128 * r : 128 * r + 128]
+            rows[pl.ds(c * OWN + r, PLANES, stride=ROWS), :] = value if scale is None else value * scale
+
+
+def prep_kernel(guess, forcing, own, force, near, far, raw, fraw, frows, sems):
     one = pltpu.make_async_copy(forcing, fraw, sems.at[0])
     two = pltpu.make_async_copy(guess, raw, sems.at[1])
     one.start()
     two.start()
     one.wait()
-    take_forcing(fraw, force)
+    to_rows(fraw, frows, 0.1)
+    for c in range(C):
+        force[c] = frows[c * OWN : (c + 1) * OWN, :]
     two.wait()
     take_guess(raw, own)
 
@@ -110,10 +113,9 @@
     put_sends(first, last, near, far)
 
 
-def gain_kernel(raw, rows, spaced):
-    for c in range(C):
-        for r in range(ROWS):
-            rows[pl.ds(c * OWN + r, PLANES, stride=ROWS), :] = raw[c, :, 128 * r : 128 * r + 128]
+def gain_kernel(raw, rows, spaced, wide):
+    to_rows(raw, wide, None)
+    rows[...] = wide[: C * OWN, :]
     for p in range(GROUP):
         spaced[p * SPACED : p * SPACED + PIECE, :] = rows[p * PIECE : (p + 1) * PIECE, :]
 
@@ -323,6 +325,7 @@
         corr[row : row + CHUNK, :] = jnp.where(late, pieces[start : start + CHUNK, :], 0.0)
 
 
+ROOMY = pltpu.VMEM((C * OWN + 16, 128), F32)
 WORK = [pltpu.VMEM((C, WIN, 128), F32), pltpu.VMEM((C, WIN, 128), F32)]
 
 
@@ -365,7 +368,7 @@
         prep_kernel,
         [rows, forcing],
         [slab, slab, wide, wide],
-        [pltpu.VMEM(rows.shape, F32), pltpu.VMEM(forcing.shape, F32), pltpu.SemaphoreType.DMA((2,))],
+        [pltpu.VMEM(rows.shape, F32), pltpu.VMEM(forcing.shape, F32), ROOMY, pltpu.SemaphoreType.DMA((2,))],
         [HBM] * 2,
         53.25,
     )
@@ -377,7 +380,7 @@
         [arr(C * C, 8, 128), arr(C, 8, 128), arr(3, 8, 128), arr(WIN // 8, 8, 128)],
         place=[SMEM] * len(small),
     )
-    gain, spaced = call(gain_kernel, [coarse_gain], [pieces, arr(GROUP * SPACED, 128)])
+    gain, spaced = call(gain_kernel, [coarse_gain], [pieces, arr(GROUP * SPACED, 128)], [ROOMY])
     state, near, far, fwin = call(
         first_kernel,
         [own, force, far, near, *coefs],

time: 74.9 us -> 74.9 us (level)
  no operation moved by 1% of the time
where the time goes in v8:
time: 74.9 us; the launch traced here: 73.8 us
  starting transfers between devices  29.2 us (39%)
  blocking collectives  22.5 us (30%)
  waiting for transfers between devices  13 us (17%)
  Pallas kernels  8.2 us (11%)
  between operations  0.8 us (1%)
    all_to_all x2, blocking collectives, swap(): lax.all_to_all(slots, 'tm', 0, 0, tiled=True, axis_index_groups=groups)  22.5 us
    all_to_all x1, starting transfers between devices, swap(): lax.all_to_all(slots, 'tm', 0, 0, tiled=True, axis_index_groups=groups)  11.4 us
    ppermute x1, waiting for transfers between devices, shards(): lax.ppermute(tail, 'tm', [(i, i + GROUP) for i in range(intervals - GROUP)])  8.82 us
    pallas_call x9, Pallas kernels, call(): pl.pallas_call(kernel, out_shape=outs, in_specs=place or [VMEM] * len(ins...  8.2 us
    ppermute x3, starting transfers between devices, exchange(): far = lax.ppermute(far, 'space', outer)  7.73 us
    ppermute x3, starting transfers between devices, exchange(): near = lax.ppermute(near, 'space', inner)  5.76 us
    ppermute x1, starting transfers between devices, shards(): lax.ppermute(tail, 'tm', [(i, i + GROUP) for i in range(intervals - GROUP)])  4.25 us
    ppermute x3, waiting for transfers between devices, exchange(): far = lax.ppermute(far, 'space', outer)  3.96 us
  transfers between devices with their start and end apart: 8, of which 5 were waited for; matrix products, arithmetic and copies ran while one was open for 0% of the time, Pallas kernels for 1%

profile of v8, /device:TPU:56, one launch (start us, length us, event | category | flops | bytes accessed | tf_op | source)
XLA Modules:
  0.0 73.8 jit_solution(16916829516451972924)
XLA Ops:
  0.6 0.0 copy-start.1
  0.6 1.2 %prep_kernel.1 = (f32[12,24,128]{2,1,0:T(8,128)S(1)}, f32[12,24,128]{2,1,0:T(8,128)S(1)}, f32[336,128]{1,0:T(8,128)S(1)}, f32[336,128]{1,0:T(8,128)S(1)}) custom-call(f32[1152,128]{1,0:T(8,128)} %bitcast.24, f32[12,6,512]{2,1,0:T(8,128)} %forcing.1), custom_call_target="tpu_custom_call" | custom-call | tf_op jit(solution)/shard_map/prep_kernel/pallas_call | solution.py:333
  1.9 0.0 copy-start.2
  1.9 0.0 copy-start.3
  1.9 0.0 copy-start.4
  1.9 2.8 %collective-permute-start = (f32[336,128]{1,0:T(8,128)S(1)}, f32[336,128]{1,0:T(8,128)S(1)}, u32[]{:S(2)}, u32[]{:S(2)}) collective-permute-start(f32[336,128]{1,0:T(8,128)S(1)} %get-tuple-element.26), channel_id=1, source_target_pairs={{1,2},{2,1},{3,4},{4,3},{5,6},{6,5},{9,10},{10,9},{11,12},{12,11},... | collective-permute-start | bytes 516104 | tf_op jit(solution)/shard_map/ppermute | solution.py:348
  4.8 1.9 %collective-permute-start.1 = (f32[336,128]{1,0:T(8,128)S(1)}, f32[336,128]{1,0:T(8,128)S(1)}, u32[]{:S(2)}, u32[]{:S(2)}) collective-permute-start(f32[336,128]{1,0:T(8,128)S(1)} %get-tuple-element.27), channel_id=1, source_target_pairs={{0,1},{1,0},{2,3},{3,2},{4,5},{5,4},{6,7},{7,6},{8,9},{9,8},{10,11... | collective-permute-start | bytes 516104 | tf_op jit(solution)/shard_map/ppermute | solution.py:349
  6.7 0.0 copy-done.1
  6.7 0.0 copy-done.2
  6.7 0.0 copy-done.3
  6.7 0.0 copy-done.4
  6.7 0.9 %setup_kernel.1 = (f32[144,8,128]{2,1,0:T(8,128)S(1)}, f32[12,8,128]{2,1,0:T(8,128)S(1)}, f32[3,8,128]{2,1,0:T(8,128)S(1)}, f32[8,8,128]{2,1,0:T(8,128)S(1)}) custom-call(f32[8]{0:T(128)S(1)} %copy-done.2, s32[12,12]{1,0:T(8,128)S(1)} %copy-done.1, f32[4]{0:T(128)S(1)} %copy-done.3, s32[12]{0:T(128)S(1)} %copy-done.4), custom_call_target="tpu_custom_call" | custom-call | tf_op jit(solution)/shard_map/setup_kernel/pallas_call | solution.py:333
  7.6 1.2 %collective-permute-done.far = f32[336,128]{1,0:T(8,128)S(1)} collective-permute-done((f32[336,128]{1,0:T(8,128)S(1)}, f32[336,128]{1,0:T(8,128)S(1)}, u32[]{:S(2)}, u32[]{:S(2)}) %collective-permute-start) | collective-permute-done | bytes 172064 | tf_op jit(solution)/shard_map/ppermute | solution.py:348
  8.8 0.0 collective-permute-done.1.near
  8.8 0.0 copy-start
  8.8 1.6 %first_kernel.1 = (f32[12,24,128]{2,1,0:T(8,128)S(1)}, f32[192,128]{1,0:T(8,128)S(1)}, f32[192,128]{1,0:T(8,128)S(1)}, f32[12,64,128]{2,1,0:T(8,128)S(1)}) custom-call(f32[12,24,128]{2,1,0:T(8,128)S(1)} %get-tuple-element.24.own, f32[12,24,128]{2,1,0:T(8,128)S(1)} %get-tuple-element.25.force, f32[336,128]{1,0:T(8,128)S(1)} %collective-permute-done.far, ...), custom_call_target="tpu_custom_call" | custom-call | tf_op jit(solution)/shard_map/first_kernel/pallas_call | solution.py:333
  10.4 3.0 %collective-permute-start.2 = (f32[192,128]{1,0:T(8,128)S(1)}, f32[192,128]{1,0:T(8,128)S(1)}, u32[]{:S(2)}, u32[]{:S(2)}) collective-permute-start(f32[192,128]{1,0:T(8,128)S(1)} %get-tuple-element.33), channel_id=1, source_target_pairs={{1,2},{2,1},{3,4},{4,3},{5,6},{6,5},{9,10},{10,9},{11,12},{12,11},... | collective-permute-start | bytes 294920 | tf_op jit(solution)/shard_map/ppermute | solution.py:348
  13.4 1.9 %collective-permute-start.3 = (f32[192,128]{1,0:T(8,128)S(1)}, f32[192,128]{1,0:T(8,128)S(1)}, u32[]{:S(2)}, u32[]{:S(2)}) collective-permute-start(f32[192,128]{1,0:T(8,128)S(1)} %get-tuple-element.34), channel_id=1, source_target_pairs={{0,1},{1,0},{2,3},{3,2},{4,5},{5,4},{6,7},{7,6},{8,9},{9,8},{10,11... | collective-permute-start | bytes 294920 | tf_op jit(solution)/shard_map/ppermute | solution.py:349
  15.3 0.0 copy-done
  15.4 1.0 %collective-permute-done.2.far = f32[192,128]{1,0:T(8,128)S(1)} collective-permute-done((f32[192,128]{1,0:T(8,128)S(1)}, f32[192,128]{1,0:T(8,128)S(1)}, u32[]{:S(2)}, u32[]{:S(2)}) %collective-permute-start.2) | collective-permute-done | bytes 98336 | tf_op jit(solution)/shard_map/ppermute | solution.py:348
  16.3 0.3 collective-permute-done.3.near
  16.6 1.6 %second_kernel.1 = f32[576,128]{1,0:T(8,128)S(1)} custom-call(f32[12,24,128]{2,1,0:T(8,128)S(1)} %get-tuple-element.32.state, f32[192,128]{1,0:T(8,128)S(1)} %collective-permute-done.2.far, f32[192,128]{1,0:T(8,128)S(1)} %collective-permute-done.3.near, f32[12,64,128]{2,1,0:T(8,128)S(1)} %get-tuple-element.35.fwin, f32[288,128]{1,0:T(8,128)S(1)} %get-tuple-element.36.gain, ...), custom_call_target="tpu_custom_call" | custom-call | tf_op jit(solution)/shard_map/second_kernel/pallas_call | solution.py:333
  18.2 12.5 %all_to_all.27 = f32[8,1,9216]{2,1,0:T(1,128)S(1)} all-to-all(f32[8,1,9216]{2,1,0:T(1,128)S(1)} %bitcast.21), channel_id=1, replica_groups={{56,48,40,32,24,16,8,0},{120,112,104,96,88,80,72,64},{184,176,168,160,1..., dimensions={0} | all-to-all | bytes 589824 | tf_op jit(solution)/shard_map/all_to_all | solution.py:358
  30.7 0.7 local_kernel.1
  31.4 11.4 %all-to-all-start.1 = ((f32[8,1,4608]{2,1,0:T(1,128)}), f32[8,1,4608]{2,1,0:T(1,128)S(1)}, u32[]{:S(2)}, u32[]{:S(2)}) async-start(f32[8,1,4608]{2,1,0:T(1,128)} %bitcast.5), calls=%async_computation.1 | async-start | bytes 294912 | tf_op jit(solution)/shard_map/all_to_all | solution.py:358
  42.8 4.3 %collective-permute-start.4 = (f32[72,128]{1,0:T(8,128)S(1)}, f32[72,128]{1,0:T(8,128)S(1)}, u32[]{:S(2)}, u32[]{:S(2)}) collective-permute-start(f32[72,128]{1,0:T(8,128)S(1)} %get-tuple-element.39), channel_id=1, source_target_pairs={{0,64},{8,72},{16,80},{24,88},{32,96},{40,104},{48,112},{56,120},{... | collective-permute-start | bytes 110600 | tf_op jit(solution)/shard_map/ppermute | solution.py:395
  47.0 8.8 %collective-permute-done.4.tail = f32[72,128]{1,0:T(8,128)S(1)} collective-permute-done((f32[72,128]{1,0:T(8,128)S(1)}, f32[72,128]{1,0:T(8,128)S(1)}, u32[]{:S(2)}, u32[]{:S(2)}) %collective-permute-start.4) | collective-permute-done | bytes 36896 | tf_op jit(solution)/shard_map/ppermute | solution.py:395
  55.9 0.0 all-to-all-done.1
  55.9 0.1 prefix_kernel.1
  55.9 10.1 %all_to_all.28 = f32[8,1,9216]{2,1,0:T(1,128)S(1)} all-to-all(f32[8,1,9216]{2,1,0:T(1,128)S(1)} %bitcast.22), channel_id=1, replica_groups={{56,48,40,32,24,16,8,0},{120,112,104,96,88,80,72,64},{184,176,168,160,1..., dimensions={0} | all-to-all | bytes 589824 | tf_op jit(solution)/shard_map/all_to_all | solution.py:358
  66.0 1.9 %collective-permute-start.5 = (f32[144,128]{1,0:T(8,128)S(1)}, f32[144,128]{1,0:T(8,128)S(1)}, u32[]{:S(2)}, u32[]{:S(2)}) collective-permute-start(f32[144,128]{1,0:T(8,128)S(1)} %get-tuple-element.42), channel_id=1, source_target_pairs={{1,2},{2,1},{3,4},{4,3},{5,6},{6,5},{9,10},{10,9},{11,12},{12,11},... | collective-permute-start | bytes 221192 | tf_op jit(solution)/shard_map/ppermute | solution.py:348
  68.0 1.9 %collective-permute-start.6 = (f32[144,128]{1,0:T(8,128)S(1)}, f32[144,128]{1,0:T(8,128)S(1)}, u32[]{:S(2)}, u32[]{:S(2)}) collective-permute-start(f32[144,128]{1,0:T(8,128)S(1)} %get-tuple-element.43), channel_id=1, source_target_pairs={{0,1},{1,0},{2,3},{3,2},{4,5},{5,4},{6,7},{7,6},{8,9},{9,8},{10,11... | collective-permute-start | bytes 221192 | tf_op jit(solution)/shard_map/ppermute | solution.py:349
  69.9 1.8 %collective-permute-done.5.far = f32[144,128]{1,0:T(8,128)S(1)} collective-permute-done((f32[144,128]{1,0:T(8,128)S(1)}, f32[144,128]{1,0:T(8,128)S(1)}, u32[]{:S(2)}, u32[]{:S(2)}) %collective-permute-start.5) | collective-permute-done | bytes 73760 | tf_op jit(solution)/shard_map/ppermute | solution.py:348
  71.7 0.0 collective-permute-done.6.near
  71.7 2.1 %last_kernel.1 = (f32[1152,128]{1,0:T(8,128)}, f32[288,128]{1,0:T(8,128)}) custom-call(f32[12,24,128]{2,1,0:T(8,128)S(1)} %get-tuple-element.41.state, f32[144,128]{1,0:T(8,128)S(1)} %collective-permute-done.5.far, f32[144,128]{1,0:T(8,128)S(1)} %collective-permute-done.6.near, f32[12,64,128]{2,1,0:T(8,128)S(1)} %get-tuple-element.35.fwin, ...), custom_call_target="tpu_custom_call" | custom-call | tf_op jit(solution)/shard_map/last_kernel/pallas_call | solution.py:333
  (2 shorter events, 0.1 us)
Async XLA Ops:
  0.6 6.1 %copy-start.1 = (s32[12,12]{1,0:T(8,128)S(1)}, s32[12,12]{1,0:T(8,128)}, u32[]{:S(2)}) copy-start(s32[12,12]{1,0:T(8,128)} %cd.1) | copy-start | bytes 1732
  1.9 4.8 %copy-start.2 = (f32[8]{0:T(128)S(1)}, f32[8]{0:T(128)}, u32[]{:S(2)}) copy-start(f32[8]{0:T(128)} %lv.1) | copy-start | bytes 100
  1.9 4.8 %copy-start.3 = (f32[4]{0:T(128)S(1)}, f32[4]{0:T(128)}, u32[]{:S(2)}) copy-start(f32[4]{0:T(128)} %st.1) | copy-start | bytes 52
  1.9 4.8 %copy-start.4 = (s32[12]{0:T(128)S(1)}, s32[12]{0:T(128)}, u32[]{:S(2)}) copy-start(s32[12]{0:T(128)} %kl.1) | copy-start | bytes 148
  1.9 6.9 %collective-permute-start = (f32[336,128]{1,0:T(8,128)S(1)}, f32[336,128]{1,0:T(8,128)S(1)}, u32[]{:S(2)}, u32[]{:S(2)}) collective-permute-start(f32[336,128]{1,0:T(8,128)S(1)} %get-tuple-element.26), channel_id=1, source_target_pairs={{1,2},{2,1},{3,4},{4,3},{5,6},{6,5},{9,10},{10,9},{11,12},{12,11},... | collective-permute-start | bytes 516104 | tf_op jit(solution)/shard_map/ppermute | solution.py:348
  4.8 4.0 %collective-permute-start.1 = (f32[336,128]{1,0:T(8,128)S(1)}, f32[336,128]{1,0:T(8,128)S(1)}, u32[]{:S(2)}, u32[]{:S(2)}) collective-permute-start(f32[336,128]{1,0:T(8,128)S(1)} %get-tuple-element.27), channel_id=1, source_target_pairs={{0,1},{1,0},{2,3},{3,2},{4,5},{5,4},{6,7},{7,6},{8,9},{9,8},{10,11... | collective-permute-start | bytes 516104 | tf_op jit(solution)/shard_map/ppermute | solution.py:349
  8.8 6.5 %copy-start = (f32[12,6,512]{2,1,0:T(8,128)S(1)}, f32[12,6,512]{2,1,0:T(8,128)}, u32[]{:S(2)}) copy-start(f32[12,6,512]{2,1,0:T(8,128)} %raw.1) | copy-start | bytes 442372
  10.4 5.9 %collective-permute-start.2 = (f32[192,128]{1,0:T(8,128)S(1)}, f32[192,128]{1,0:T(8,128)S(1)}, u32[]{:S(2)}, u32[]{:S(2)}) collective-permute-start(f32[192,128]{1,0:T(8,128)S(1)} %get-tuple-element.33), channel_id=1, source_target_pairs={{1,2},{2,1},{3,4},{4,3},{5,6},{6,5},{9,10},{10,9},{11,12},{12,11},... | collective-permute-start | bytes 294920 | tf_op jit(solution)/shard_map/ppermute | solution.py:348
  13.4 3.2 %collective-permute-start.3 = (f32[192,128]{1,0:T(8,128)S(1)}, f32[192,128]{1,0:T(8,128)S(1)}, u32[]{:S(2)}, u32[]{:S(2)}) collective-permute-start(f32[192,128]{1,0:T(8,128)S(1)} %get-tuple-element.34), channel_id=1, source_target_pairs={{0,1},{1,0},{2,3},{3,2},{4,5},{5,4},{6,7},{7,6},{8,9},{9,8},{10,11... | collective-permute-start | bytes 294920 | tf_op jit(solution)/shard_map/ppermute | solution.py:349
  31.4 24.5 %all-to-all-start.1 = ((f32[8,1,4608]{2,1,0:T(1,128)}), f32[8,1,4608]{2,1,0:T(1,128)S(1)}, u32[]{:S(2)}, u32[]{:S(2)}) async-start(f32[8,1,4608]{2,1,0:T(1,128)} %bitcast.5), calls=%async_computation.1 | async-start | bytes 294912 | tf_op jit(solution)/shard_map/all_to_all | solution.py:358
  42.8 13.1 %collective-permute-start.4 = (f32[72,128]{1,0:T(8,128)S(1)}, f32[72,128]{1,0:T(8,128)S(1)}, u32[]{:S(2)}, u32[]{:S(2)}) collective-permute-start(f32[72,128]{1,0:T(8,128)S(1)} %get-tuple-element.39), channel_id=1, source_target_pairs={{0,64},{8,72},{16,80},{24,88},{32,96},{40,104},{48,112},{56,120},{... | collective-permute-start | bytes 110600 | tf_op jit(solution)/shard_map/ppermute | solution.py:395
  66.0 5.7 %collective-permute-start.5 = (f32[144,128]{1,0:T(8,128)S(1)}, f32[144,128]{1,0:T(8,128)S(1)}, u32[]{:S(2)}, u32[]{:S(2)}) collective-permute-start(f32[144,128]{1,0:T(8,128)S(1)} %get-tuple-element.42), channel_id=1, source_target_pairs={{1,2},{2,1},{3,4},{4,3},{5,6},{6,5},{9,10},{10,9},{11,12},{12,11},... | collective-permute-start | bytes 221192 | tf_op jit(solution)/shard_map/ppermute | solution.py:348
  68.0 3.7 %collective-permute-start.6 = (f32[144,128]{1,0:T(8,128)S(1)}, f32[144,128]{1,0:T(8,128)S(1)}, u32[]{:S(2)}, u32[]{:S(2)}) collective-permute-start(f32[144,128]{1,0:T(8,128)S(1)} %get-tuple-element.43), channel_id=1, source_target_pairs={{0,1},{1,0},{2,3},{3,2},{4,5},{5,4},{6,7},{7,6},{8,9},{9,8},{10,11... | collective-permute-start | bytes 221192 | tf_op jit(solution)/shard_map/ppermute | solution.py:349

commit v9 on v8

--- a/solution.py
+++ b/solution.py
@@ -14,6 +14,7 @@
 PLANES = 6
 NX = 48
 SLICES = 4
+DIFFUSION = 0.08
 ROWS = 4
 OWN = PLANES * ROWS
 HALO = 4 * ROWS
@@ -78,8 +79,8 @@
     return into
 
 
-def take_guess(raw, own):
-    for c in range(C):
+def take_guess(raw, own, classes):
+    for c in classes:
         own[c] = raw[pl.ds(c * OWN * SLICES, OWN, stride=SLICES), :]
 
 
@@ -91,16 +92,20 @@
 
 
 def prep_kernel(guess, forcing, own, force, near, far, raw, fraw, frows, sems):
+    size = C * OWN * SLICES // 2
+    halves = [pl.ds(n * size, size) for n in (0, 1)]
     one = pltpu.make_async_copy(forcing, fraw, sems.at[0])
-    two = pltpu.make_async_copy(guess, raw, sems.at[1])
+    parts = [pltpu.make_async_copy(guess.at[h], raw.at[h], sems.at[n + 1]) for n, h in enumerate(halves)]
     one.start()
-    two.start()
+    for part in parts:
+        part.start()
     one.wait()
-    to_rows(fraw, frows, 0.1)
+    to_rows(fraw, frows, 0.1 / DIFFUSION)
     for c in range(C):
         force[c] = frows[c * OWN : (c + 1) * OWN, :]
-    two.wait()
-    take_guess(raw, own)
+    for n, part in enumerate(parts):
+        part.wait()
+        take_guess(raw, own, range(n * C // 2, (n + 1) * C // 2))
 
     def first(dst):
         pack(own, 0, HALO, 0)(dst)
@@ -130,17 +135,17 @@
         total = functools.reduce(lambda x, y: x + y, col)
         speed = st[kl[j]]
         for i in range(C):
-            v = (col[i] - total) + (1.0 - 0.48) - speed if i == j else col[i]
-            kv[i * C + j] = jnp.full((8, 128), v, F32)
-        wup[j] = jnp.where(z < NZ - 1, 0.08 + speed, 0.0)
-    wfix[0] = jnp.where(z > 0, F32(0.08), F32(0.0))
-    wfix[1] = jnp.where(jnp.logical_and(lane >= 96, edge_row == ROWS - 1), F32(0.0), F32(0.08))
-    wfix[2] = jnp.where(jnp.logical_and(lane < 32, edge_row == 0), F32(0.0), F32(0.08))
+            v = (col[i] - total) + (1.0 - 6.0 * DIFFUSION) - speed if i == j else col[i]
+            kv[i * C + j] = jnp.full((8, 128), v * (1.0 / DIFFUSION), F32)
+        wup[j] = jnp.where(z < NZ - 1, 1.0 + speed * (1.0 / DIFFUSION), 0.0)
+    wfix[0] = jnp.where(z > 0, F32(1.0), F32(0.0))
+    wfix[1] = jnp.where(jnp.logical_and(lane >= 96, edge_row == ROWS - 1), F32(0.0), F32(1.0))
+    wfix[2] = jnp.where(jnp.logical_and(lane < 32, edge_row == 0), F32(0.0), F32(1.0))
     start = lax.axis_index("space") * PLANES - 5
     for t in range(WIN // 8):
         plane = start + 2 * t + row // ROWS
         inside = jnp.logical_and(plane >= 0, plane < NX)
-        mask[t] = jnp.where(inside, F32(1.0), F32(0.0))
+        mask[t] = jnp.where(inside, F32(DIFFUSION), F32(0.0))
 
 
 def clear_edges(buf):
@@ -149,7 +154,7 @@
     buf[:, WIN - 8 : WIN, :] = z
 
 
-def block_step(src, dst, fwin, t, kv, wup, wfix, mask):
+def block_step(src, dst, fwin, t, classes, kv, wup, wfix, mask):
     lane = lax.broadcasted_iota(jnp.int32, (8, 128), 1)
     row = lax.broadcasted_iota(jnp.int32, (8, 128), 0)
     low = row < ROWS
@@ -160,8 +165,8 @@
     def rows(k):
         return pl.ds((t + k) * 8, 8)
 
-    acc = []
-    for i in range(C):
+    acc = {}
+    for i in classes:
         p = [src[i, rows(k), :] for k in (-1, 0, 1, 2)]
         q = [pltpu.roll(v, 4, 0) for v in p]
         pair = []
@@ -174,29 +179,29 @@
             rb = pltpu.roll(c, 32, 1)
             ah = jnp.where(right, pltpu.roll(ra, 7, 0), ra)
             be = jnp.where(left, pltpu.roll(rb, 1, 0), rb)
-            new = fwin[i, rows(k), :] + 0.08 * xs
+            new = fwin[i, rows(k), :] + xs
             new = new + wup[i] * up
             new = new + wdn * dn
             new = new + wah * ah
             new = new + wbe * be
             pair.append(new)
-        acc.append(pair)
+        acc[i] = pair
     for j in range(C):
         c = [src[j, rows(k), :] for k in (0, 1)]
-        for i in range(C):
+        for i in classes:
             w = kv[i * C + j]
             acc[i] = [acc[i][k] + w * c[k] for k in (0, 1)]
     for k in (0, 1):
         m = mask[t + k]
-        for i in range(C):
+        for i in classes:
             dst[i, rows(k), :] = acc[i][k] * m
 
 
-def steps(bufs, fwin, plan, coefs):
+def steps(bufs, fwin, plan, coefs, classes=range(C)):
     for s, (first, count) in enumerate(plan):
         src, dst = bufs[s % 2], bufs[(s + 1) % 2]
         for b in range(count):
-            block_step(src, dst, fwin, first + 2 * b, *coefs)
+            block_step(src, dst, fwin, first + 2 * b, classes, *coefs)
 
 
 FOUR = ((1, 3), (1, 3), (2, 2), (2, 2))
@@ -303,38 +308,50 @@
     put_sends(pack(state, 0, THREE, 0), pack(state, OWN - THREE, THREE, 0), near, far)
 
 
-def last_kernel(state, far, near, fwin, pieces, kv, wup, wfix, mask, out, corr, a, b):
+def last_kernel(state, far, near, fwin, pieces, kv, wup, wfix, mask, out, corr, a, b, held, fixed, sems):
+    late = lax.axis_index("tm") >= 1
+    for c, x, p, r in chunks():
+        row, start = c * OWN + x, p * WIDE + PIECE + r
+        fixed[row : row + CHUNK, :] = jnp.where(late, pieces[start : start + CHUNK, :], 0.0)
+    copies = [pltpu.make_async_copy(fixed, corr, sems.at[0])]
+    copies[0].start()
     clear_edges(a)
     clear_edges(b)
     a[:, BASE : BASE + OWN, :] = state[...]
     put_halo(a, near, far, THREE, 0)
-
-    def emit(buf, j):
-        for c in range(C):
-            out[pl.ds(c * OWN * SLICES + j, OWN, stride=SLICES), :] = buf[c, BASE : BASE + OWN, :]
+    coefs = (kv, wup, wfix, mask)
+
+    def emit(buf, j, classes=range(C)):
+        for c in classes:
+            held[pl.ds(c * OWN * SLICES + j, OWN, stride=SLICES), :] = buf[c, BASE : BASE + OWN, :]
 
     emit(a, 0)
-    bufs = (a, b)
-    for j, one in enumerate(((1, 3), (2, 2), (2, 2))):
-        src, dst = bufs[j % 2], bufs[(j + 1) % 2]
-        steps((src, dst), fwin, (one,), (kv, wup, wfix, mask))
-        emit(dst, j + 1)
-    late = lax.axis_index("tm") >= 1
-    for c, x, p, r in chunks():
-        row, start = c * OWN + x, p * WIDE + PIECE + r
-        corr[row : row + CHUNK, :] = jnp.where(late, pieces[start : start + CHUNK, :], 0.0)
+    steps((a, b), fwin, ((1, 3),), coefs)
+    emit(b, 1)
+    steps((b, a), fwin, ((2, 2),), coefs)
+    emit(a, 2)
+    for n in (0, 1):
+        classes = range(n * C // 2, (n + 1) * C // 2)
+        steps((a, b), fwin, ((2, 2),), coefs, classes)
+        emit(b, 3, classes)
+        size = C * OWN * SLICES // 2
+        half = pl.ds(n * size, size)
+        copies.append(pltpu.make_async_copy(held.at[half], out.at[half], sems.at[n + 1]))
+        copies[-1].start()
+    for one in copies:
+        one.wait()
 
 
 ROOMY = pltpu.VMEM((C * OWN + 16, 128), F32)
 WORK = [pltpu.VMEM((C, WIN, 128), F32), pltpu.VMEM((C, WIN, 128), F32)]
 
 
-def call(kernel, ins, outs, scratch=(), place=None, grant=32):
+def call(kernel, ins, outs, scratch=(), place=None, grant=32, results=VMEM):
     return pl.pallas_call(
         kernel,
         out_shape=outs,
         in_specs=place or [VMEM] * len(ins),
-        out_specs=[VMEM] * len(outs),
+        out_specs=[results] * len(outs),
         scratch_shapes=list(scratch),
         compiler_params=pltpu.CompilerParams(vmem_limit_bytes=int(grant * 1024 * 1024)),
         name=kernel.__name__,
@@ -368,7 +385,7 @@
         prep_kernel,
         [rows, forcing],
         [slab, slab, wide, wide],
-        [pltpu.VMEM(rows.shape, F32), pltpu.VMEM(forcing.shape, F32), ROOMY, pltpu.SemaphoreType.DMA((2,))],
+        [pltpu.VMEM(rows.shape, F32), pltpu.VMEM(forcing.shape, F32), ROOMY, pltpu.SemaphoreType.DMA((3,))],
         [HBM] * 2,
         53.25,
     )
@@ -399,11 +416,13 @@
         gather_kernel, [back, own], [slab, three, three]
     )
     near, far = exchange(near, far)
+    sizes = (C * OWN * SLICES, 128), (C * OWN, 128)
     updated, corr = call(
         last_kernel,
         [state, far, near, fwin, back, *coefs],
-        [arr(C * OWN * SLICES, 128), arr(C * OWN, 128)],
-        WORK,
+        [arr(*size) for size in sizes],
+        WORK + [pltpu.VMEM(size, F32) for size in sizes] + [pltpu.SemaphoreType.DMA((3,))],
+        results=HBM,
     )
     updated = updated.reshape(C, PLANES, ROWS, SLICES, 128).transpose(3, 0, 1, 2, 4)
     return (

time: 74.9 us -> 74.9 us (level)
  no operation moved by 1% of the time
where the time goes in v9:
time: 74.9 us; the launch traced here: 73.8 us
  starting transfers between devices  29.2 us (39%)
  blocking collectives  22.5 us (30%)
  waiting for transfers between devices  13 us (17%)
  Pallas kernels  8.22 us (11%)
  between operations  0.81 us (1%)
    all_to_all x2, blocking collectives, swap(): lax.all_to_all(slots, 'tm', 0, 0, tiled=True, axis_index_groups=groups)  22.5 us
    all_to_all x1, starting transfers between devices, swap(): lax.all_to_all(slots, 'tm', 0, 0, tiled=True, axis_index_groups=groups)  11.4 us
    ppermute x1, waiting for transfers between devices, shards(): lax.ppermute(tail, 'tm', [(i, i + GROUP) for i in range(intervals - GROUP)])  8.82 us
    pallas_call x9, Pallas kernels, call(): pl.pallas_call(kernel, out_shape=outs, in_specs=place or [VMEM] * len(ins...  8.22 us
    ppermute x3, starting transfers between devices, exchange(): far = lax.ppermute(far, 'space', outer)  7.74 us
    ppermute x3, starting transfers between devices, exchange(): near = lax.ppermute(near, 'space', inner)  5.76 us
    ppermute x1, starting transfers between devices, shards(): lax.ppermute(tail, 'tm', [(i, i + GROUP) for i in range(intervals - GROUP)])  4.25 us
    ppermute x3, waiting for transfers between devices, exchange(): far = lax.ppermute(far, 'space', outer)  3.92 us
  transfers between devices with their start and end apart: 8, of which 5 were waited for; matrix products, arithmetic and copies ran while one was open for 0% of the time, Pallas kernels for 1%

profile of v9, /device:TPU:56, one launch (start us, length us, event | category | flops | bytes accessed | tf_op | source)
XLA Modules:
  0.0 73.8 jit_solution(16649574826377288672)
XLA Ops:
  0.6 0.0 copy-start.1
  0.6 1.2 %prep_kernel.1 = (f32[12,24,128]{2,1,0:T(8,128)S(1)}, f32[12,24,128]{2,1,0:T(8,128)S(1)}, f32[336,128]{1,0:T(8,128)S(1)}, f32[336,128]{1,0:T(8,128)S(1)}) custom-call(f32[1152,128]{1,0:T(8,128)} %bitcast.24, f32[12,6,512]{2,1,0:T(8,128)} %forcing.1), custom_call_target="tpu_custom_call" | custom-call | tf_op jit(solution)/shard_map/prep_kernel/pallas_call | solution.py:350
  1.9 0.0 copy-start.2
  1.9 0.0 copy-start.3
  1.9 0.0 copy-start.4
  1.9 2.8 %collective-permute-start = (f32[336,128]{1,0:T(8,128)S(1)}, f32[336,128]{1,0:T(8,128)S(1)}, u32[]{:S(2)}, u32[]{:S(2)}) collective-permute-start(f32[336,128]{1,0:T(8,128)S(1)} %get-tuple-element.26), channel_id=1, source_target_pairs={{1,2},{2,1},{3,4},{4,3},{5,6},{6,5},{9,10},{10,9},{11,12},{12,11},... | collective-permute-start | bytes 516104 | tf_op jit(solution)/shard_map/ppermute | solution.py:365
  4.7 1.9 %collective-permute-start.1 = (f32[336,128]{1,0:T(8,128)S(1)}, f32[336,128]{1,0:T(8,128)S(1)}, u32[]{:S(2)}, u32[]{:S(2)}) collective-permute-start(f32[336,128]{1,0:T(8,128)S(1)} %get-tuple-element.27), channel_id=1, source_target_pairs={{0,1},{1,0},{2,3},{3,2},{4,5},{5,4},{6,7},{7,6},{8,9},{9,8},{10,11... | collective-permute-start | bytes 516104 | tf_op jit(solution)/shard_map/ppermute | solution.py:366
  6.7 0.0 copy-done.1
  6.7 0.0 copy-done.2
  6.7 0.0 copy-done.3
  6.7 0.0 copy-done.4
  6.7 0.9 %setup_kernel.1 = (f32[144,8,128]{2,1,0:T(8,128)S(1)}, f32[12,8,128]{2,1,0:T(8,128)S(1)}, f32[3,8,128]{2,1,0:T(8,128)S(1)}, f32[8,8,128]{2,1,0:T(8,128)S(1)}) custom-call(f32[8]{0:T(128)S(1)} %copy-done.2, s32[12,12]{1,0:T(8,128)S(1)} %copy-done.1, f32[4]{0:T(128)S(1)} %copy-done.3, s32[12]{0:T(128)S(1)} %copy-done.4), custom_call_target="tpu_custom_call" | custom-call | tf_op jit(solution)/shard_map/setup_kernel/pallas_call | solution.py:350
  7.6 1.2 %collective-permute-done.far = f32[336,128]{1,0:T(8,128)S(1)} collective-permute-done((f32[336,128]{1,0:T(8,128)S(1)}, f32[336,128]{1,0:T(8,128)S(1)}, u32[]{:S(2)}, u32[]{:S(2)}) %collective-permute-start) | collective-permute-done | bytes 172064 | tf_op jit(solution)/shard_map/ppermute | solution.py:365
  8.8 0.0 collective-permute-done.1.near
  8.8 0.0 copy-start
  8.8 1.7 %first_kernel.1 = (f32[12,24,128]{2,1,0:T(8,128)S(1)}, f32[192,128]{1,0:T(8,128)S(1)}, f32[192,128]{1,0:T(8,128)S(1)}, f32[12,64,128]{2,1,0:T(8,128)S(1)}) custom-call(f32[12,24,128]{2,1,0:T(8,128)S(1)} %get-tuple-element.24.own, f32[12,24,128]{2,1,0:T(8,128)S(1)} %get-tuple-element.25.force, f32[336,128]{1,0:T(8,128)S(1)} %collective-permute-done.far, ...), custom_call_target="tpu_custom_call" | custom-call | tf_op jit(solution)/shard_map/first_kernel/pallas_call | solution.py:350
  10.4 3.0 %collective-permute-start.2 = (f32[192,128]{1,0:T(8,128)S(1)}, f32[192,128]{1,0:T(8,128)S(1)}, u32[]{:S(2)}, u32[]{:S(2)}) collective-permute-start(f32[192,128]{1,0:T(8,128)S(1)} %get-tuple-element.33), channel_id=1, source_target_pairs={{1,2},{2,1},{3,4},{4,3},{5,6},{6,5},{9,10},{10,9},{11,12},{12,11},... | collective-permute-start | bytes 294920 | tf_op jit(solution)/shard_map/ppermute | solution.py:365
  13.4 1.9 %collective-permute-start.3 = (f32[192,128]{1,0:T(8,128)S(1)}, f32[192,128]{1,0:T(8,128)S(1)}, u32[]{:S(2)}, u32[]{:S(2)}) collective-permute-start(f32[192,128]{1,0:T(8,128)S(1)} %get-tuple-element.34), channel_id=1, source_target_pairs={{0,1},{1,0},{2,3},{3,2},{4,5},{5,4},{6,7},{7,6},{8,9},{9,8},{10,11... | collective-permute-start | bytes 294920 | tf_op jit(solution)/shard_map/ppermute | solution.py:366
  15.4 0.0 copy-done
  15.4 1.0 %collective-permute-done.2.far = f32[192,128]{1,0:T(8,128)S(1)} collective-permute-done((f32[192,128]{1,0:T(8,128)S(1)}, f32[192,128]{1,0:T(8,128)S(1)}, u32[]{:S(2)}, u32[]{:S(2)}) %collective-permute-start.2) | collective-permute-done | bytes 98336 | tf_op jit(solution)/shard_map/ppermute | solution.py:365
  16.4 0.3 collective-permute-done.3.near
  16.6 1.6 %second_kernel.1 = f32[576,128]{1,0:T(8,128)S(1)} custom-call(f32[12,24,128]{2,1,0:T(8,128)S(1)} %get-tuple-element.32.state, f32[192,128]{1,0:T(8,128)S(1)} %collective-permute-done.2.far, f32[192,128]{1,0:T(8,128)S(1)} %collective-permute-done.3.near, f32[12,64,128]{2,1,0:T(8,128)S(1)} %get-tuple-element.35.fwin, f32[288,128]{1,0:T(8,128)S(1)} %get-tuple-element.36.gain, ...), custom_call_target="tpu_custom_call" | custom-call | tf_op jit(solution)/shard_map/second_kernel/pallas_call | solution.py:350
  18.2 12.5 %all_to_all.27 = f32[8,1,9216]{2,1,0:T(1,128)S(1)} all-to-all(f32[8,1,9216]{2,1,0:T(1,128)S(1)} %bitcast.21), channel_id=1, replica_groups={{56,48,40,32,24,16,8,0},{120,112,104,96,88,80,72,64},{184,176,168,160,1..., dimensions={0} | all-to-all | bytes 589824 | tf_op jit(solution)/shard_map/all_to_all | solution.py:375
  30.7 0.7 local_kernel.1
  31.4 11.4 %all-to-all-start.1 = ((f32[8,1,4608]{2,1,0:T(1,128)}), f32[8,1,4608]{2,1,0:T(1,128)S(1)}, u32[]{:S(2)}, u32[]{:S(2)}) async-start(f32[8,1,4608]{2,1,0:T(1,128)} %bitcast.5), calls=%async_computation.1 | async-start | bytes 294912 | tf_op jit(solution)/shard_map/all_to_all | solution.py:375
  42.8 4.3 %collective-permute-start.4 = (f32[72,128]{1,0:T(8,128)S(1)}, f32[72,128]{1,0:T(8,128)S(1)}, u32[]{:S(2)}, u32[]{:S(2)}) collective-permute-start(f32[72,128]{1,0:T(8,128)S(1)} %get-tuple-element.39), channel_id=1, source_target_pairs={{0,64},{8,72},{16,80},{24,88},{32,96},{40,104},{48,112},{56,120},{... | collective-permute-start | bytes 110600 | tf_op jit(solution)/shard_map/ppermute | solution.py:412
  47.1 8.8 %collective-permute-done.4.tail = f32[72,128]{1,0:T(8,128)S(1)} collective-permute-done((f32[72,128]{1,0:T(8,128)S(1)}, f32[72,128]{1,0:T(8,128)S(1)}, u32[]{:S(2)}, u32[]{:S(2)}) %collective-permute-start.4) | collective-permute-done | bytes 36896 | tf_op jit(solution)/shard_map/ppermute | solution.py:412
  55.9 0.0 all-to-all-done.1
  55.9 0.1 prefix_kernel.1
  56.0 10.1 %all_to_all.28 = f32[8,1,9216]{2,1,0:T(1,128)S(1)} all-to-all(f32[8,1,9216]{2,1,0:T(1,128)S(1)} %bitcast.22), channel_id=1, replica_groups={{56,48,40,32,24,16,8,0},{120,112,104,96,88,80,72,64},{184,176,168,160,1..., dimensions={0} | all-to-all | bytes 589824 | tf_op jit(solution)/shard_map/all_to_all | solution.py:375
  66.1 1.9 %collective-permute-start.5 = (f32[144,128]{1,0:T(8,128)S(1)}, f32[144,128]{1,0:T(8,128)S(1)}, u32[]{:S(2)}, u32[]{:S(2)}) collective-permute-start(f32[144,128]{1,0:T(8,128)S(1)} %get-tuple-element.42), channel_id=1, source_target_pairs={{1,2},{2,1},{3,4},{4,3},{5,6},{6,5},{9,10},{10,9},{11,12},{12,11},... | collective-permute-start | bytes 221192 | tf_op jit(solution)/shard_map/ppermute | solution.py:365
  68.0 1.9 %collective-permute-start.6 = (f32[144,128]{1,0:T(8,128)S(1)}, f32[144,128]{1,0:T(8,128)S(1)}, u32[]{:S(2)}, u32[]{:S(2)}) collective-permute-start(f32[144,128]{1,0:T(8,128)S(1)} %get-tuple-element.43), channel_id=1, source_target_pairs={{0,1},{1,0},{2,3},{3,2},{4,5},{5,4},{6,7},{7,6},{8,9},{9,8},{10,11... | collective-permute-start | bytes 221192 | tf_op jit(solution)/shard_map/ppermute | solution.py:366
  69.9 1.8 %collective-permute-done.5.far = f32[144,128]{1,0:T(8,128)S(1)} collective-permute-done((f32[144,128]{1,0:T(8,128)S(1)}, f32[144,128]{1,0:T(8,128)S(1)}, u32[]{:S(2)}, u32[]{:S(2)}) %collective-permute-start.5) | collective-permute-done | bytes 73760 | tf_op jit(solution)/shard_map/ppermute | solution.py:365
  71.8 0.0 collective-permute-done.6.near
  71.8 2.0 %last_kernel.1 = (f32[1152,128]{1,0:T(8,128)}, f32[288,128]{1,0:T(8,128)}) custom-call(f32[12,24,128]{2,1,0:T(8,128)S(1)} %get-tuple-element.41.state, f32[144,128]{1,0:T(8,128)S(1)} %collective-permute-done.5.far, f32[144,128]{1,0:T(8,128)S(1)} %collective-permute-done.6.near, f32[12,64,128]{2,1,0:T(8,128)S(1)} %get-tuple-element.35.fwin, ...), custom_call_target="tpu_custom_call" | custom-call | tf_op jit(solution)/shard_map/last_kernel/pallas_call | solution.py:350
  (2 shorter events, 0.1 us)
Async XLA Ops:
  0.6 6.0 %copy-start.1 = (s32[12,12]{1,0:T(8,128)S(1)}, s32[12,12]{1,0:T(8,128)}, u32[]{:S(2)}) copy-start(s32[12,12]{1,0:T(8,128)} %cd.1) | copy-start | bytes 1732
  1.9 4.8 %copy-start.2 = (f32[8]{0:T(128)S(1)}, f32[8]{0:T(128)}, u32[]{:S(2)}) copy-start(f32[8]{0:T(128)} %lv.1) | copy-start | bytes 100
  1.9 4.8 %copy-start.3 = (f32[4]{0:T(128)S(1)}, f32[4]{0:T(128)}, u32[]{:S(2)}) copy-start(f32[4]{0:T(128)} %st.1) | copy-start | bytes 52
  1.9 4.8 %copy-start.4 = (s32[12]{0:T(128)S(1)}, s32[12]{0:T(128)}, u32[]{:S(2)}) copy-start(s32[12]{0:T(128)} %kl.1) | copy-start | bytes 148
  1.9 6.9 %collective-permute-start = (f32[336,128]{1,0:T(8,128)S(1)}, f32[336,128]{1,0:T(8,128)S(1)}, u32[]{:S(2)}, u32[]{:S(2)}) collective-permute-start(f32[336,128]{1,0:T(8,128)S(1)} %get-tuple-element.26), channel_id=1, source_target_pairs={{1,2},{2,1},{3,4},{4,3},{5,6},{6,5},{9,10},{10,9},{11,12},{12,11},... | collective-permute-start | bytes 516104 | tf_op jit(solution)/shard_map/ppermute | solution.py:365
  4.7 4.0 %collective-permute-start.1 = (f32[336,128]{1,0:T(8,128)S(1)}, f32[336,128]{1,0:T(8,128)S(1)}, u32[]{:S(2)}, u32[]{:S(2)}) collective-permute-start(f32[336,128]{1,0:T(8,128)S(1)} %get-tuple-element.27), channel_id=1, source_target_pairs={{0,1},{1,0},{2,3},{3,2},{4,5},{5,4},{6,7},{7,6},{8,9},{9,8},{10,11... | collective-permute-start | bytes 516104 | tf_op jit(solution)/shard_map/ppermute | solution.py:366
  8.8 6.6 %copy-start = (f32[12,6,512]{2,1,0:T(8,128)S(1)}, f32[12,6,512]{2,1,0:T(8,128)}, u32[]{:S(2)}) copy-start(f32[12,6,512]{2,1,0:T(8,128)} %raw.1) | copy-start | bytes 442372
  10.4 5.9 %collective-permute-start.2 = (f32[192,128]{1,0:T(8,128)S(1)}, f32[192,128]{1,0:T(8,128)S(1)}, u32[]{:S(2)}, u32[]{:S(2)}) collective-permute-start(f32[192,128]{1,0:T(8,128)S(1)} %get-tuple-element.33), channel_id=1, source_target_pairs={{1,2},{2,1},{3,4},{4,3},{5,6},{6,5},{9,10},{10,9},{11,12},{12,11},... | collective-permute-start | bytes 294920 | tf_op jit(solution)/shard_map/ppermute | solution.py:365
  13.4 3.2 %collective-permute-start.3 = (f32[192,128]{1,0:T(8,128)S(1)}, f32[192,128]{1,0:T(8,128)S(1)}, u32[]{:S(2)}, u32[]{:S(2)}) collective-permute-start(f32[192,128]{1,0:T(8,128)S(1)} %get-tuple-element.34), channel_id=1, source_target_pairs={{0,1},{1,0},{2,3},{3,2},{4,5},{5,4},{6,7},{7,6},{8,9},{9,8},{10,11... | collective-permute-start | bytes 294920 | tf_op jit(solution)/shard_map/ppermute | solution.py:366
  31.4 24.5 %all-to-all-start.1 = ((f32[8,1,4608]{2,1,0:T(1,128)}), f32[8,1,4608]{2,1,0:T(1,128)S(1)}, u32[]{:S(2)}, u32[]{:S(2)}) async-start(f32[8,1,4608]{2,1,0:T(1,128)} %bitcast.5), calls=%async_computation.1 | async-start | bytes 294912 | tf_op jit(solution)/shard_map/all_to_all | solution.py:375
  42.8 13.1 %collective-permute-start.4 = (f32[72,128]{1,0:T(8,128)S(1)}, f32[72,128]{1,0:T(8,128)S(1)}, u32[]{:S(2)}, u32[]{:S(2)}) collective-permute-start(f32[72,128]{1,0:T(8,128)S(1)} %get-tuple-element.39), channel_id=1, source_target_pairs={{0,64},{8,72},{16,80},{24,88},{32,96},{40,104},{48,112},{56,120},{... | collective-permute-start | bytes 110600 | tf_op jit(solution)/shard_map/ppermute | solution.py:412
  66.1 5.7 %collective-permute-start.5 = (f32[144,128]{1,0:T(8,128)S(1)}, f32[144,128]{1,0:T(8,128)S(1)}, u32[]{:S(2)}, u32[]{:S(2)}) collective-permute-start(f32[144,128]{1,0:T(8,128)S(1)} %get-tuple-element.42), channel_id=1, source_target_pairs={{1,2},{2,1},{3,4},{4,3},{5,6},{6,5},{9,10},{10,9},{11,12},{12,11},... | collective-permute-start | bytes 221192 | tf_op jit(solution)/shard_map/ppermute | solution.py:365
  68.0 3.7 %collective-permute-start.6 = (f32[144,128]{1,0:T(8,128)S(1)}, f32[144,128]{1,0:T(8,128)S(1)}, u32[]{:S(2)}, u32[]{:S(2)}) collective-permute-start(f32[144,128]{1,0:T(8,128)S(1)} %get-tuple-element.43), channel_id=1, source_target_pairs={{0,1},{1,0},{2,3},{3,2},{4,5},{5,4},{6,7},{7,6},{8,9},{9,8},{10,11... | collective-permute-start | bytes 221192 | tf_op jit(solution)/shard_map/ppermute | solution.py:366

commit v10 on v8

--- a/solution.py
+++ b/solution.py
@@ -21,6 +21,7 @@
 WIN = 64
 BASE = 5 * ROWS
 GROUP = 8
+DOWN = (7, 3, 4, 0, 5, 1, 6, 2)
 PIECE = C * OWN // GROUP
 WIDE = 2 * PIECE
 SPACED = 40
@@ -238,12 +239,13 @@
 
 
 def my_gain(gain):
-    place = GROUP - 1 - lax.axis_index("tm") % GROUP
+    member = lax.axis_index("tm") % GROUP
+    place = sum(jnp.where(member == i, at, 0) for at, i in enumerate(DOWN))
     return gain[pl.ds(pl.multiple_of(place * SPACED, 8), PIECE), :]
 
 
 def slot(i, width=PIECE, half=0):
-    start = (GROUP - 1 - i) * width + half * PIECE
+    start = DOWN.index(i) * width + half * PIECE
     return slice(start, start + PIECE)
 
 
@@ -258,7 +260,7 @@
             tail[:PIECE, :] = running
     tail[PIECE:, :] = pieces[slot(GROUP - 1, WIDE, 1), :]
     for i in range(GROUP):
-        total[slot(i), :] = running
+        total[i * PIECE : (i + 1) * PIECE, :] = running
 
 
 def prefix_kernel(totals, tail, sums, pieces, gain, out):
@@ -272,7 +274,7 @@
     for g in range(GROUP - 1):
         take = g < group
         ahead = jnp.where(take, before, ahead)
-        before = jnp.where(take, g8 * before + totals[slot(g), :], before)
+        before = jnp.where(take, g8 * before + totals[(GROUP - 1 - g) * PIECE : (GROUP - g) * PIECE, :], before)
     for i in range(GROUP):
         if i == 0:
             base = tail[PIECE:, :]
@@ -353,7 +355,7 @@
 def swap(value, stride):
     count = lax.axis_size("tm")
     firsts = [i for i in range(count) if (i // stride) % GROUP == 0]
-    groups = [[i + stride * j for j in reversed(range(GROUP))] for i in firsts]
+    groups = [[i + stride * j for j in (DOWN if stride == 1 else reversed(range(GROUP)))] for i in firsts]
     slots = value.reshape(GROUP, -1)
     return lax.all_to_all(slots, "tm", 0, 0, tiled=True, axis_index_groups=groups).reshape(value.shape)
 

time: 74.9 us -> 74.9 us (level)
  no operation moved by 1% of the time
where the time goes in v10:
time: 74.9 us; the launch traced here: 73.8 us
  starting transfers between devices  29.2 us (39%)
  blocking collectives  22.5 us (30%)
  waiting for transfers between devices  13 us (17%)
  Pallas kernels  8.21 us (11%)
  between operations  0.8 us (1%)
    all_to_all x2, blocking collectives, swap(): lax.all_to_all(slots, 'tm', 0, 0, tiled=True, axis_index_groups=groups)  22.5 us
    all_to_all x1, starting transfers between devices, swap(): lax.all_to_all(slots, 'tm', 0, 0, tiled=True, axis_index_groups=groups)  11.4 us
    ppermute x1, waiting for transfers between devices, shards(): lax.ppermute(tail, 'tm', [(i, i + GROUP) for i in range(intervals - GROUP)])  8.8 us
    pallas_call x9, Pallas kernels, call(): pl.pallas_call(kernel, out_shape=outs, in_specs=place or [VMEM] * len(ins...  8.21 us
    ppermute x3, starting transfers between devices, exchange(): far = lax.ppermute(far, 'space', outer)  7.73 us
    ppermute x3, starting transfers between devices, exchange(): near = lax.ppermute(near, 'space', inner)  5.76 us
    ppermute x1, starting transfers between devices, shards(): lax.ppermute(tail, 'tm', [(i, i + GROUP) for i in range(intervals - GROUP)])  4.25 us
    ppermute x3, waiting for transfers between devices, exchange(): far = lax.ppermute(far, 'space', outer)  3.96 us
  transfers between devices with their start and end apart: 8, of which 5 were waited for; matrix products, arithmetic and copies ran while one was open for 0% of the time, Pallas kernels for 1%

profile of v10, /device:TPU:56, one launch (start us, length us, event | category | flops | bytes accessed | tf_op | source)
XLA Modules:
  0.0 73.8 jit_solution(8259271458002024161)
XLA Ops:
  0.6 0.0 copy-start.1
  0.6 1.2 %prep_kernel.1 = (f32[12,24,128]{2,1,0:T(8,128)S(1)}, f32[12,24,128]{2,1,0:T(8,128)S(1)}, f32[336,128]{1,0:T(8,128)S(1)}, f32[336,128]{1,0:T(8,128)S(1)}) custom-call(f32[1152,128]{1,0:T(8,128)} %bitcast.24, f32[12,6,512]{2,1,0:T(8,128)} %forcing.1), custom_call_target="tpu_custom_call" | custom-call | tf_op jit(solution)/shard_map/prep_kernel/pallas_call | solution.py:335
  1.9 0.0 copy-start.2
  1.9 0.0 copy-start.3
  1.9 0.0 copy-start.4
  1.9 2.8 %collective-permute-start = (f32[336,128]{1,0:T(8,128)S(1)}, f32[336,128]{1,0:T(8,128)S(1)}, u32[]{:S(2)}, u32[]{:S(2)}) collective-permute-start(f32[336,128]{1,0:T(8,128)S(1)} %get-tuple-element.26), channel_id=1, source_target_pairs={{1,2},{2,1},{3,4},{4,3},{5,6},{6,5},{9,10},{10,9},{11,12},{12,11},... | collective-permute-start | bytes 516104 | tf_op jit(solution)/shard_map/ppermute | solution.py:350
  4.8 1.9 %collective-permute-start.1 = (f32[336,128]{1,0:T(8,128)S(1)}, f32[336,128]{1,0:T(8,128)S(1)}, u32[]{:S(2)}, u32[]{:S(2)}) collective-permute-start(f32[336,128]{1,0:T(8,128)S(1)} %get-tuple-element.27), channel_id=1, source_target_pairs={{0,1},{1,0},{2,3},{3,2},{4,5},{5,4},{6,7},{7,6},{8,9},{9,8},{10,11... | collective-permute-start | bytes 516104 | tf_op jit(solution)/shard_map/ppermute | solution.py:351
  6.7 0.0 copy-done.1
  6.7 0.0 copy-done.2
  6.7 0.0 copy-done.3
  6.7 0.0 copy-done.4
  6.7 0.9 %setup_kernel.1 = (f32[144,8,128]{2,1,0:T(8,128)S(1)}, f32[12,8,128]{2,1,0:T(8,128)S(1)}, f32[3,8,128]{2,1,0:T(8,128)S(1)}, f32[8,8,128]{2,1,0:T(8,128)S(1)}) custom-call(f32[8]{0:T(128)S(1)} %copy-done.2, s32[12,12]{1,0:T(8,128)S(1)} %copy-done.1, f32[4]{0:T(128)S(1)} %copy-done.3, s32[12]{0:T(128)S(1)} %copy-done.4), custom_call_target="tpu_custom_call" | custom-call | tf_op jit(solution)/shard_map/setup_kernel/pallas_call | solution.py:335
  7.6 1.2 %collective-permute-done.far = f32[336,128]{1,0:T(8,128)S(1)} collective-permute-done((f32[336,128]{1,0:T(8,128)S(1)}, f32[336,128]{1,0:T(8,128)S(1)}, u32[]{:S(2)}, u32[]{:S(2)}) %collective-permute-start) | collective-permute-done | bytes 172064 | tf_op jit(solution)/shard_map/ppermute | solution.py:350
  8.8 0.0 collective-permute-done.1.near
  8.8 0.0 copy-start
  8.8 1.6 %first_kernel.1 = (f32[12,24,128]{2,1,0:T(8,128)S(1)}, f32[192,128]{1,0:T(8,128)S(1)}, f32[192,128]{1,0:T(8,128)S(1)}, f32[12,64,128]{2,1,0:T(8,128)S(1)}) custom-call(f32[12,24,128]{2,1,0:T(8,128)S(1)} %get-tuple-element.24.own, f32[12,24,128]{2,1,0:T(8,128)S(1)} %get-tuple-element.25.force, f32[336,128]{1,0:T(8,128)S(1)} %collective-permute-done.far, ...), custom_call_target="tpu_custom_call" | custom-call | tf_op jit(solution)/shard_map/first_kernel/pallas_call | solution.py:335
  10.4 3.0 %collective-permute-start.2 = (f32[192,128]{1,0:T(8,128)S(1)}, f32[192,128]{1,0:T(8,128)S(1)}, u32[]{:S(2)}, u32[]{:S(2)}) collective-permute-start(f32[192,128]{1,0:T(8,128)S(1)} %get-tuple-element.33), channel_id=1, source_target_pairs={{1,2},{2,1},{3,4},{4,3},{5,6},{6,5},{9,10},{10,9},{11,12},{12,11},... | collective-permute-start | bytes 294920 | tf_op jit(solution)/shard_map/ppermute | solution.py:350
  13.4 1.9 %collective-permute-start.3 = (f32[192,128]{1,0:T(8,128)S(1)}, f32[192,128]{1,0:T(8,128)S(1)}, u32[]{:S(2)}, u32[]{:S(2)}) collective-permute-start(f32[192,128]{1,0:T(8,128)S(1)} %get-tuple-element.34), channel_id=1, source_target_pairs={{0,1},{1,0},{2,3},{3,2},{4,5},{5,4},{6,7},{7,6},{8,9},{9,8},{10,11... | collective-permute-start | bytes 294920 | tf_op jit(solution)/shard_map/ppermute | solution.py:351
  15.3 0.0 copy-done
  15.4 1.0 %collective-permute-done.2.far = f32[192,128]{1,0:T(8,128)S(1)} collective-permute-done((f32[192,128]{1,0:T(8,128)S(1)}, f32[192,128]{1,0:T(8,128)S(1)}, u32[]{:S(2)}, u32[]{:S(2)}) %collective-permute-start.2) | collective-permute-done | bytes 98336 | tf_op jit(solution)/shard_map/ppermute | solution.py:350
  16.3 0.3 collective-permute-done.3.near
  16.6 1.6 %second_kernel.1 = f32[576,128]{1,0:T(8,128)S(1)} custom-call(f32[12,24,128]{2,1,0:T(8,128)S(1)} %get-tuple-element.32.state, f32[192,128]{1,0:T(8,128)S(1)} %collective-permute-done.2.far, f32[192,128]{1,0:T(8,128)S(1)} %collective-permute-done.3.near, f32[12,64,128]{2,1,0:T(8,128)S(1)} %get-tuple-element.35.fwin, f32[288,128]{1,0:T(8,128)S(1)} %get-tuple-element.36.gain, ...), custom_call_target="tpu_custom_call" | custom-call | tf_op jit(solution)/shard_map/second_kernel/pallas_call | solution.py:335
  18.2 12.5 %all_to_all.27 = f32[8,1,9216]{2,1,0:T(1,128)S(1)} all-to-all(f32[8,1,9216]{2,1,0:T(1,128)S(1)} %bitcast.21), channel_id=1, replica_groups={{56,24,32,0,40,8,48,16},{120,88,96,64,104,72,112,80},{184,152,160,128,1..., dimensions={0} | all-to-all | bytes 589824 | tf_op jit(solution)/shard_map/all_to_all | solution.py:360
  30.7 0.7 local_kernel.1
  31.4 11.4 %all-to-all-start.1 = ((f32[8,1,4608]{2,1,0:T(1,128)}), f32[8,1,4608]{2,1,0:T(1,128)S(1)}, u32[]{:S(2)}, u32[]{:S(2)}) async-start(f32[8,1,4608]{2,1,0:T(1,128)} %bitcast.5), calls=%async_computation.1 | async-start | bytes 294912 | tf_op jit(solution)/shard_map/all_to_all | solution.py:360
  42.8 4.3 %collective-permute-start.4 = (f32[72,128]{1,0:T(8,128)S(1)}, f32[72,128]{1,0:T(8,128)S(1)}, u32[]{:S(2)}, u32[]{:S(2)}) collective-permute-start(f32[72,128]{1,0:T(8,128)S(1)} %get-tuple-element.39), channel_id=1, source_target_pairs={{0,64},{8,72},{16,80},{24,88},{32,96},{40,104},{48,112},{56,120},{... | collective-permute-start | bytes 110600 | tf_op jit(solution)/shard_map/ppermute | solution.py:397
  47.1 8.8 %collective-permute-done.4.tail = f32[72,128]{1,0:T(8,128)S(1)} collective-permute-done((f32[72,128]{1,0:T(8,128)S(1)}, f32[72,128]{1,0:T(8,128)S(1)}, u32[]{:S(2)}, u32[]{:S(2)}) %collective-permute-start.4) | collective-permute-done | bytes 36896 | tf_op jit(solution)/shard_map/ppermute | solution.py:397
  55.9 0.0 all-to-all-done.1
  55.9 0.1 prefix_kernel.1
  55.9 10.0 %all_to_all.28 = f32[8,1,9216]{2,1,0:T(1,128)S(1)} all-to-all(f32[8,1,9216]{2,1,0:T(1,128)S(1)} %bitcast.22), channel_id=1, replica_groups={{56,24,32,0,40,8,48,16},{120,88,96,64,104,72,112,80},{184,152,160,128,1..., dimensions={0} | all-to-all | bytes 589824 | tf_op jit(solution)/shard_map/all_to_all | solution.py:360
  66.0 1.9 %collective-permute-start.5 = (f32[144,128]{1,0:T(8,128)S(1)}, f32[144,128]{1,0:T(8,128)S(1)}, u32[]{:S(2)}, u32[]{:S(2)}) collective-permute-start(f32[144,128]{1,0:T(8,128)S(1)} %get-tuple-element.42), channel_id=1, source_target_pairs={{1,2},{2,1},{3,4},{4,3},{5,6},{6,5},{9,10},{10,9},{11,12},{12,11},... | collective-permute-start | bytes 221192 | tf_op jit(solution)/shard_map/ppermute | solution.py:350
  67.9 1.9 %collective-permute-start.6 = (f32[144,128]{1,0:T(8,128)S(1)}, f32[144,128]{1,0:T(8,128)S(1)}, u32[]{:S(2)}, u32[]{:S(2)}) collective-permute-start(f32[144,128]{1,0:T(8,128)S(1)} %get-tuple-element.43), channel_id=1, source_target_pairs={{0,1},{1,0},{2,3},{3,2},{4,5},{5,4},{6,7},{7,6},{8,9},{9,8},{10,11... | collective-permute-start | bytes 221192 | tf_op jit(solution)/shard_map/ppermute | solution.py:351
  69.9 1.8 %collective-permute-done.5.far = f32[144,128]{1,0:T(8,128)S(1)} collective-permute-done((f32[144,128]{1,0:T(8,128)S(1)}, f32[144,128]{1,0:T(8,128)S(1)}, u32[]{:S(2)}, u32[]{:S(2)}) %collective-permute-start.5) | collective-permute-done | bytes 73760 | tf_op jit(solution)/shard_map/ppermute | solution.py:350
  71.7 0.0 collective-permute-done.6.near
  71.7 2.1 %last_kernel.1 = (f32[1152,128]{1,0:T(8,128)}, f32[288,128]{1,0:T(8,128)}) custom-call(f32[12,24,128]{2,1,0:T(8,128)S(1)} %get-tuple-element.41.state, f32[144,128]{1,0:T(8,128)S(1)} %collective-permute-done.5.far, f32[144,128]{1,0:T(8,128)S(1)} %collective-permute-done.6.near, f32[12,64,128]{2,1,0:T(8,128)S(1)} %get-tuple-element.35.fwin, ...), custom_call_target="tpu_custom_call" | custom-call | tf_op jit(solution)/shard_map/last_kernel/pallas_call | solution.py:335
  (2 shorter events, 0.1 us)
Async XLA Ops:
  0.6 6.1 %copy-start.1 = (s32[12,12]{1,0:T(8,128)S(1)}, s32[12,12]{1,0:T(8,128)}, u32[]{:S(2)}) copy-start(s32[12,12]{1,0:T(8,128)} %cd.1) | copy-start | bytes 1732
  1.9 4.8 %copy-start.2 = (f32[8]{0:T(128)S(1)}, f32[8]{0:T(128)}, u32[]{:S(2)}) copy-start(f32[8]{0:T(128)} %lv.1) | copy-start | bytes 100
  1.9 4.8 %copy-start.3 = (f32[4]{0:T(128)S(1)}, f32[4]{0:T(128)}, u32[]{:S(2)}) copy-start(f32[4]{0:T(128)} %st.1) | copy-start | bytes 52
  1.9 4.8 %copy-start.4 = (s32[12]{0:T(128)S(1)}, s32[12]{0:T(128)}, u32[]{:S(2)}) copy-start(s32[12]{0:T(128)} %kl.1) | copy-start | bytes 148
  1.9 6.9 %collective-permute-start = (f32[336,128]{1,0:T(8,128)S(1)}, f32[336,128]{1,0:T(8,128)S(1)}, u32[]{:S(2)}, u32[]{:S(2)}) collective-permute-start(f32[336,128]{1,0:T(8,128)S(1)} %get-tuple-element.26), channel_id=1, source_target_pairs={{1,2},{2,1},{3,4},{4,3},{5,6},{6,5},{9,10},{10,9},{11,12},{12,11},... | collective-permute-start | bytes 516104 | tf_op jit(solution)/shard_map/ppermute | solution.py:350
  4.8 4.0 %collective-permute-start.1 = (f32[336,128]{1,0:T(8,128)S(1)}, f32[336,128]{1,0:T(8,128)S(1)}, u32[]{:S(2)}, u32[]{:S(2)}) collective-permute-start(f32[336,128]{1,0:T(8,128)S(1)} %get-tuple-element.27), channel_id=1, source_target_pairs={{0,1},{1,0},{2,3},{3,2},{4,5},{5,4},{6,7},{7,6},{8,9},{9,8},{10,11... | collective-permute-start | bytes 516104 | tf_op jit(solution)/shard_map/ppermute | solution.py:351
  8.8 6.5 %copy-start = (f32[12,6,512]{2,1,0:T(8,128)S(1)}, f32[12,6,512]{2,1,0:T(8,128)}, u32[]{:S(2)}) copy-start(f32[12,6,512]{2,1,0:T(8,128)} %raw.1) | copy-start | bytes 442372
  10.4 5.9 %collective-permute-start.2 = (f32[192,128]{1,0:T(8,128)S(1)}, f32[192,128]{1,0:T(8,128)S(1)}, u32[]{:S(2)}, u32[]{:S(2)}) collective-permute-start(f32[192,128]{1,0:T(8,128)S(1)} %get-tuple-element.33), channel_id=1, source_target_pairs={{1,2},{2,1},{3,4},{4,3},{5,6},{6,5},{9,10},{10,9},{11,12},{12,11},... | collective-permute-start | bytes 294920 | tf_op jit(solution)/shard_map/ppermute | solution.py:350
  13.4 3.2 %collective-permute-start.3 = (f32[192,128]{1,0:T(8,128)S(1)}, f32[192,128]{1,0:T(8,128)S(1)}, u32[]{:S(2)}, u32[]{:S(2)}) collective-permute-start(f32[192,128]{1,0:T(8,128)S(1)} %get-tuple-element.34), channel_id=1, source_target_pairs={{0,1},{1,0},{2,3},{3,2},{4,5},{5,4},{6,7},{7,6},{8,9},{9,8},{10,11... | collective-permute-start | bytes 294920 | tf_op jit(solution)/shard_map/ppermute | solution.py:351
  31.4 24.5 %all-to-all-start.1 = ((f32[8,1,4608]{2,1,0:T(1,128)}), f32[8,1,4608]{2,1,0:T(1,128)S(1)}, u32[]{:S(2)}, u32[]{:S(2)}) async-start(f32[8,1,4608]{2,1,0:T(1,128)} %bitcast.5), calls=%async_computation.1 | async-start | bytes 294912 | tf_op jit(solution)/shard_map/all_to_all | solution.py:360
  42.8 13.1 %collective-permute-start.4 = (f32[72,128]{1,0:T(8,128)S(1)}, f32[72,128]{1,0:T(8,128)S(1)}, u32[]{:S(2)}, u32[]{:S(2)}) collective-permute-start(f32[72,128]{1,0:T(8,128)S(1)} %get-tuple-element.39), channel_id=1, source_target_pairs={{0,64},{8,72},{16,80},{24,88},{32,96},{40,104},{48,112},{56,120},{... | collective-permute-start | bytes 110600 | tf_op jit(solution)/shard_map/ppermute | solution.py:397
  66.0 5.7 %collective-permute-start.5 = (f32[144,128]{1,0:T(8,128)S(1)}, f32[144,128]{1,0:T(8,128)S(1)}, u32[]{:S(2)}, u32[]{:S(2)}) collective-permute-start(f32[144,128]{1,0:T(8,128)S(1)} %get-tuple-element.42), channel_id=1, source_target_pairs={{1,2},{2,1},{3,4},{4,3},{5,6},{6,5},{9,10},{10,9},{11,12},{12,11},... | collective-permute-start | bytes 221192 | tf_op jit(solution)/shard_map/ppermute | solution.py:350
  67.9 3.7 %collective-permute-start.6 = (f32[144,128]{1,0:T(8,128)S(1)}, f32[144,128]{1,0:T(8,128)S(1)}, u32[]{:S(2)}, u32[]{:S(2)}) collective-permute-start(f32[144,128]{1,0:T(8,128)S(1)} %get-tuple-element.43), channel_id=1, source_target_pairs={{0,1},{1,0},{2,3},{3,2},{4,5},{5,4},{6,7},{7,6},{8,9},{9,8},{10,11... | collective-permute-start | bytes 221192 | tf_op jit(solution)/shard_map/ppermute | solution.py:351
